TPU v7x, 512 devices: a whole 4x4x16 slice. The times are simulated.
512 devices in a mesh: grid: 32 (over y, x, core), head: 16 (over z).
Axes of the slice: x: 4, y: 4, z: 16, core: 2. Of those that a mesh axis runs over, the one named last changes fastest.
Arguments:
- grid_feat: bfloat16 [32768, 1024], P('grid'), may hold values from -6 to 6
- mesh_feat: bfloat16 [8192, 1024], P('grid'), may hold values from -6 to 6
- query_weight: bfloat16 [1024, 1024], P(None, 'head'), may hold values from -0.1875 to 0.1875
- key_weight: bfloat16 [1024, 1024], P(None, 'head'), may hold values from -0.1875 to 0.1875
- value_weight: bfloat16 [1024, 1024], P(None, 'head'), may hold values from -0.1875 to 0.1875
- enc_out_weight: bfloat16 [1024, 1024], P('head'), may hold values from -0.75 to 0.75
- layer_query: bfloat16 [1024, 1024], P(None, 'head'), may hold values from -0.1875 to 0.1875
- layer_key: bfloat16 [1024, 1024], P(None, 'head'), may hold values from -0.1875 to 0.1875
- layer_value: bfloat16 [1024, 1024], P(None, 'head'), may hold values from -0.1875 to 0.1875
- layer_out_weight: bfloat16 [1024, 1024], P('head'), may hold values from -0.75 to 0.75
- enc_bias: float32 [64, 30, 16], P('grid', None, 'head'), may hold values from -4 to 360
- layer_bias: float32 [64, 3, 16], P('grid', None, 'head'), may hold values from -4 to 360
- send_list: int32 [32, 32], P('grid'), may hold values from 0 to 7
- edge_slot: int32 [64, 30], P('grid'), may hold values from 0 to 39, as said below
- edge_count: int32 [64], P('grid'), may hold values from 2 to 30, as said below
- cotangent: bfloat16 [8192, 1024], P(('grid', 'head')), may hold values from -6 to 6
Outputs:
- mesh_out: bfloat16 [8192, 1024], P(('grid', 'head'))
- key_grad: float32 [1024, 1024], P('grid', 'head')
- value_grad: float32 [1024, 1024], P('grid', 'head')
Inputs may be any that keep to these rules, and one draw needn't show every extreme that they name: `edge_slot`: row m lists the grid blocks read by mesh block m of grid shard s = m // 2: an entry below 8 is a block of shard s, an entry 8 + p is the block that shard p (never s) sends to s. The first edge_count[m] entries are live and distinct, the others are 0. Over the 2 mesh blocks of a shard, each of its 8 blocks and each of the other shards' blocks is read exactly once. `edge_count`: the counts of the 2 mesh blocks of a grid shard sum to 39, and one of them equals 30. `send_list`: entry [s, p] is the block of grid shard s, counted within that shard, that s sends to shard p; diagonal entries are not read.
All inputs are finite; a program needn't handle non-finite values.
Results may differ from a plain program's by a relative error of at most 0.029.
Values may be sent and summed in bfloat16 or wider, within the bound.
No kernel may reach another device: no remote copies, remote signals or barrier semaphores. Data moves between devices by JAX's collectives and lax.ppermute only.
A program may use at most 64 MiB of HBM per device.

v0:
```python
from functools import partial

import jax
import jax.numpy as jnp
from jax import lax
from jax.sharding import PartitionSpec as P

HEAD_DIM = 64
BLOCK = 128


epsilon = 1e-05
score_scale = 0.125


def extended_2(block, sides, width):
    for axis, dim in sides:
        count = lax.axis_size(axis)
        forward = [(i, i + 1) for i in range(count - 1)]
        forward.append((count - 1, 0))
        backward = [(target, source) for source, target in forward]
        low = lax.ppermute(
            lax.slice_in_dim(block, block.shape[dim] - width, None, axis=dim), axis, forward
        )
        high = lax.ppermute(lax.slice_in_dim(block, 0, width, axis=dim), axis, backward)
        block = jnp.concatenate([low, block, high], axis=dim)
    return block


def normalize(matrix):
    values = matrix.astype(jnp.float32)
    center = values - jnp.mean(values, axis=-1, keepdims=True)
    inverse = lax.rsqrt(jnp.mean(center * center, axis=-1, keepdims=True) + epsilon)
    return (center * inverse, inverse)


def norm_back(grad_unit, unit_rows, inverse):
    mean_grad = jnp.mean(grad_unit, axis=-1, keepdims=True)
    mean_both = jnp.mean(grad_unit * unit_rows, axis=-1, keepdims=True)
    return inverse * (grad_unit - mean_grad - unit_rows * mean_both)


def dot_right(left_rows, right_rows):
    return lax.dot_general(
        left_rows, right_rows, (((1,), (1,)), ((), ())), preferred_element_type=jnp.float32
    )


def dot_left(left_rows, right_rows):
    return lax.dot_general(
        left_rows, right_rows, (((0,), (0,)), ((), ())), preferred_element_type=jnp.float32
    )


def probabilities(query_rows, key_rows, bias_table, live_edges):
    scores = jnp.einsum("rhd,shd->hrs", query_rows, key_rows, preferred_element_type=jnp.float32)
    heads_here, row_total, key_total = scores.shape
    edge_total = bias_table.shape[1]
    scores = (
        scores.reshape(heads_here, row_total, edge_total, key_total // edge_total) * score_scale
    )
    scores = scores + bias_table[:, None, :, None]
    scores = jnp.where(live_edges[None, None, :, None], scores, -jnp.inf)
    scores = scores.reshape(heads_here, row_total, key_total)
    highest = jnp.max(scores, axis=-1, keepdims=True)
    raised = jnp.exp(scores - highest)
    return raised / jnp.sum(raised, axis=-1, keepdims=True)


def combine(soft_weights, value_rows):
    mixed_rows = jnp.einsum(
        "hrs,shd->rhd",
        soft_weights.astype(jnp.bfloat16),
        value_rows,
        preferred_element_type=jnp.float32,
    )
    return mixed_rows.astype(jnp.bfloat16)


def attend_back(query_rows, key_rows, value_rows, soft_weights, grad_rows, with_query):
    grad_soft = jnp.einsum(
        "rhd,shd->hrs", grad_rows, value_rows, preferred_element_type=jnp.float32
    )
    inner_sum = jnp.sum(soft_weights * grad_soft, axis=-1, keepdims=True)
    grad_scores = (soft_weights * (grad_soft - inner_sum) * score_scale).astype(jnp.bfloat16)
    grad_keys = jnp.einsum(
        "hrs,rhd->shd", grad_scores, query_rows, preferred_element_type=jnp.float32
    )
    grad_values = jnp.einsum(
        "hrs,rhd->shd",
        soft_weights.astype(jnp.bfloat16),
        grad_rows,
        preferred_element_type=jnp.float32,
    )
    if with_query:
        grad_query = jnp.einsum(
            "hrs,shd->rhd", grad_scores, key_rows, preferred_element_type=jnp.float32
        )
        return (grad_query, grad_keys, grad_values)
    return (None, grad_keys, grad_values)


def on_device(
    grid_feat,
    mesh_feat,
    query_weight,
    key_weight,
    value_weight,
    enc_out_weight,
    layer_query,
    layer_key,
    layer_value,
    layer_out_weight,
    enc_bias,
    layer_bias,
    send_list,
    edge_slot,
    edge_count,
    cotangent,
):
    shards = lax.axis_size("grid")
    head_parts = lax.axis_size("head")
    head_width = key_weight.shape[1]
    heads_here = head_width // HEAD_DIM
    grid_count = grid_feat.shape[0] // BLOCK
    mesh_rows = mesh_feat.shape[0]
    mesh_count = mesh_rows // BLOCK
    edge_total = edge_slot.shape[1]
    share_rows = mesh_rows // head_parts
    share_start = lax.axis_index("head") * share_rows
    grid_unit, unused_scale = normalize(grid_feat)
    grid_norm = grid_unit.astype(jnp.bfloat16)
    grid_keys = (
        jnp.dot(grid_norm, key_weight, preferred_element_type=jnp.float32)
        .astype(jnp.bfloat16)
        .reshape(grid_count, BLOCK, head_width)
    )
    grid_values = (
        jnp.dot(grid_norm, value_weight, preferred_element_type=jnp.float32)
        .astype(jnp.bfloat16)
        .reshape(grid_count, BLOCK, head_width)
    )
    outgoing = send_list[0]
    arrived_keys, arrived_values = (
        lax.all_to_all(
            jnp.take(grid_keys, outgoing, axis=0), "grid", split_axis=0, concat_axis=0, tiled=True
        ),
        lax.all_to_all(
            jnp.take(grid_values, outgoing, axis=0), "grid", split_axis=0, concat_axis=0, tiled=True
        ),
    )
    pool_keys = jnp.concatenate([grid_keys, arrived_keys], axis=0)
    pool_values = jnp.concatenate([grid_values, arrived_values], axis=0)
    live_table = jnp.arange(edge_total, dtype=jnp.int32)[None, :] < edge_count[:, None]
    edge_keys = jnp.take(pool_keys, edge_slot, axis=0).reshape(
        mesh_count, edge_total * BLOCK, heads_here, HEAD_DIM
    )
    edge_values = jnp.take(pool_values, edge_slot, axis=0).reshape(
        mesh_count, edge_total * BLOCK, heads_here, HEAD_DIM
    )
    enc_table = jnp.transpose(enc_bias, (0, 2, 1))
    mesh_unit, unused_scale = normalize(mesh_feat)
    queries = (
        jnp.dot(mesh_unit.astype(jnp.bfloat16), query_weight, preferred_element_type=jnp.float32)
        .astype(jnp.bfloat16)
        .reshape(mesh_count, BLOCK, heads_here, HEAD_DIM)
    )
    enc_soft = jax.vmap(probabilities)(queries, edge_keys, enc_table, live_table)
    enc_heads = jax.vmap(combine)(enc_soft, edge_values).reshape(mesh_rows, head_width)
    layer_weights = jnp.concatenate([layer_query, layer_key, layer_value], axis=1)
    mesh_share = lax.dynamic_slice_in_dim(mesh_feat, share_start, share_rows, 0).astype(jnp.float32)
    picked_rows = enc_heads
    encoded = mesh_share + lax.psum_scatter(
        jnp.dot(picked_rows, enc_out_weight, preferred_element_type=jnp.float32),
        "head",
        scatter_dimension=0,
        tiled=True,
    )
    enc_unit, enc_inverse = normalize(encoded)
    layer_mix = jnp.dot(
        lax.all_gather(enc_unit.astype(jnp.bfloat16), "head", axis=0, tiled=True),
        layer_weights,
        preferred_element_type=jnp.float32,
    ).astype(jnp.bfloat16)
    layer_queries = layer_mix[:, :head_width].reshape(mesh_count, BLOCK, heads_here, HEAD_DIM)
    extended = extended_2(layer_mix[:, head_width:], (("grid", 0),), BLOCK)
    extended_blocks = extended.reshape(mesh_count + 2, BLOCK, 2 * head_width)
    window = jnp.stack(
        [
            extended_blocks[0:mesh_count],
            extended_blocks[1 : mesh_count + 1],
            extended_blocks[2 : mesh_count + 2],
        ],
        axis=1,
    )
    window_keys = window[..., :head_width].reshape(mesh_count, 3 * BLOCK, heads_here, HEAD_DIM)
    window_values = window[..., head_width:].reshape(mesh_count, 3 * BLOCK, heads_here, HEAD_DIM)
    layer_table = jnp.transpose(layer_bias, (0, 2, 1))
    all_live = jnp.ones((mesh_count, 3), dtype=jnp.bool_)
    layer_soft = jax.vmap(probabilities)(layer_queries, window_keys, layer_table, all_live)
    layer_heads = jax.vmap(combine)(layer_soft, window_values).reshape(mesh_rows, head_width)
    picked_rows = layer_heads
    mixed_rows = encoded + lax.psum_scatter(
        jnp.dot(picked_rows, layer_out_weight, preferred_element_type=jnp.float32),
        "head",
        scatter_dimension=0,
        tiled=True,
    )
    mesh_out = mixed_rows.astype(jnp.bfloat16)
    grad_rows = lax.all_gather(cotangent, "head", axis=0, tiled=True)
    grad_layer = (
        dot_right(grad_rows, layer_out_weight)
        .astype(jnp.bfloat16)
        .reshape(mesh_count, BLOCK, heads_here, HEAD_DIM)
    )
    grad_layer_queries, grad_window_keys, grad_window_values = jax.vmap(
        partial(attend_back, with_query=True)
    )(layer_queries, window_keys, window_values, layer_soft, grad_layer)
    grad_window = jnp.concatenate(
        [
            grad_window_keys.reshape(mesh_count, 3, BLOCK, head_width),
            grad_window_values.reshape(mesh_count, 3, BLOCK, head_width),
        ],
        axis=-1,
    )
    no_pad = (0, 0)
    grad_extended = jnp.pad(grad_window[:, 0], ((0, 2), no_pad, no_pad))
    grad_extended = grad_extended + jnp.pad(grad_window[:, 1], ((1, 1), no_pad, no_pad))
    grad_extended = grad_extended + jnp.pad(grad_window[:, 2], ((2, 0), no_pad, no_pad))
    rim_rows = jnp.concatenate([grad_extended[0], grad_extended[mesh_count + 1]], axis=0)
    returned_rims = extended_2(rim_rows, (("grid", 0),), BLOCK)
    grad_inner = grad_extended[1 : mesh_count + 1]
    grad_inner = grad_inner.at[0].add(returned_rims[:BLOCK])
    grad_inner = grad_inner.at[mesh_count - 1].add(returned_rims[3 * BLOCK :])
    grad_projected = jnp.concatenate(
        [
            grad_layer_queries.reshape(mesh_rows, head_width),
            grad_inner.reshape(mesh_rows, 2 * head_width),
        ],
        axis=1,
    ).astype(jnp.bfloat16)
    grad_share = lax.psum_scatter(
        dot_right(grad_projected, layer_weights), "head", scatter_dimension=0, tiled=True
    )
    grad_enc = cotangent.astype(jnp.float32) + norm_back(grad_share, enc_unit, enc_inverse)
    grad_heads = dot_right(
        lax.all_gather(grad_enc.astype(jnp.bfloat16), "head", axis=0, tiled=True), enc_out_weight
    ).astype(jnp.bfloat16)
    grad_enc_rows = grad_heads.reshape(mesh_count, BLOCK, heads_here, HEAD_DIM)
    unused_query, grad_edge_keys, grad_edge_values = jax.vmap(
        partial(attend_back, with_query=False)
    )(queries, edge_keys, edge_values, enc_soft, grad_enc_rows)
    edge_flat = mesh_count * edge_total
    pool_count = grid_count + shards
    slot_onehot = (
        edge_slot.reshape(edge_flat)[None, :] == jnp.arange(pool_count, dtype=jnp.int32)[:, None]
    ).astype(jnp.float32)
    grad_pool_keys = jnp.dot(
        slot_onehot,
        grad_edge_keys.reshape(edge_flat, BLOCK * head_width),
        precision=lax.Precision.HIGHEST,
    )
    grad_pool_values = jnp.dot(
        slot_onehot,
        grad_edge_values.reshape(edge_flat, BLOCK * head_width),
        precision=lax.Precision.HIGHEST,
    )
    back_keys, back_values = (
        lax.all_to_all(
            grad_pool_keys[grid_count:].reshape(shards, BLOCK, head_width),
            "grid",
            split_axis=0,
            concat_axis=0,
            tiled=True,
        ),
        lax.all_to_all(
            grad_pool_values[grid_count:].reshape(shards, BLOCK, head_width),
            "grid",
            split_axis=0,
            concat_axis=0,
            tiled=True,
        ),
    )
    owner_onehot = (outgoing[None, :] == jnp.arange(grid_count, dtype=jnp.int32)[:, None]).astype(
        jnp.float32
    )
    grad_key_rows = grad_pool_keys[:grid_count] + jnp.dot(
        owner_onehot, back_keys.reshape(shards, BLOCK * head_width), precision=lax.Precision.HIGHEST
    )
    grad_value_rows = grad_pool_values[:grid_count] + jnp.dot(
        owner_onehot,
        back_values.reshape(shards, BLOCK * head_width),
        precision=lax.Precision.HIGHEST,
    )
    key_part = dot_left(
        grid_norm, grad_key_rows.reshape(grid_count * BLOCK, head_width).astype(jnp.bfloat16)
    )
    value_part = dot_left(
        grid_norm, grad_value_rows.reshape(grid_count * BLOCK, head_width).astype(jnp.bfloat16)
    )
    key_grad, value_grad = (
        lax.psum_scatter(
            key_part.astype(jnp.bfloat16), "grid", scatter_dimension=0, tiled=True
        ).astype(jnp.float32),
        lax.psum_scatter(
            value_part.astype(jnp.bfloat16), "grid", scatter_dimension=0, tiled=True
        ).astype(jnp.float32),
    )
    return (mesh_out, key_grad, value_grad)


def solution(mesh):
    in_specs = (
        P("grid", None),
        P("grid", None),
        P(None, "head"),
        P(None, "head"),
        P(None, "head"),
        P("head", None),
        P(None, "head"),
        P(None, "head"),
        P(None, "head"),
        P("head", None),
        P("grid", None, "head"),
        P("grid", None, "head"),
        P("grid", None),
        P("grid", None),
        P("grid"),
        P(("grid", "head"), None),
    )
    out_specs = (P(("grid", "head"), None), P("grid", "head"), P("grid", "head"))
    return jax.shard_map(
        on_device, mesh=mesh, in_specs=in_specs, out_specs=out_specs, check_vma=False
    )
```

profile of v0, /device:TPU:1, one launch (start us, length us, event | category | flops | bytes accessed | tf_op | source)
XLA Modules:
  0.0 682.8 jit_solution(13293367191859179096)
XLA Ops:
  17.6 10.4 %all-to-all-start.1 = ((bf16[32,128,64]{1,2,0:T(8,128)(2,1)}), bf16[32,128,64]{1,2,0:T(8,128)(2,1)S(1)}, u32[]{:S(2)}, u32[]{:S(2)}) async-start(bf16[32,128,64]{1,2,0:T(8,128)(2,1)} %get-tuple-element.48), calls=%async_computation.1 | async-start | bytes 1048576 | tf_op jit(solution)/shard_map/all_to_all | solution.py:145
  31.6 8.1 %all-to-all-done.1 = bf16[32,128,64]{1,2,0:T(8,128)(2,1)S(1)} async-done(((bf16[32,128,64]{1,2,0:T(8,128)(2,1)}), bf16[32,128,64]{1,2,0:T(8,128)(2,1)S(1)}, u32[]{:S(2)}, u32[]{:S(2)}) %all-to-all-start.1) | async-done | bytes 524320 | tf_op jit(solution)/shard_map/all_to_all | solution.py:145
  39.7 4.6 all-to-all-start
  48.6 7.4 %all-to-all-done = bf16[32,128,64]{1,2,0:T(8,128)(2,1)} async-done(((bf16[32,128,64]{1,2,0:T(8,128)(2,1)}), bf16[32,128,64]{1,2,0:T(8,128)(2,1)}, u32[]{:S(2)}, u32[]{:S(2)}) %all-to-all-start) | async-done | bytes 524320 | tf_op jit(solution)/shard_map/all_to_all | solution.py:148
  61.5 4.4 fusion.130
  73.4 32.3 %all_gather.10 = bf16[256,1024]{1,0:T(8,128)(2,1)} all-gather(bf16[16,1024]{1,0:T(8,128)(2,1)S(1)} %copy-done.10), channel_id=1, replica_groups=mesh['grid'=32,'head'=16] {'head'}, dimensions={0}, use_global_device_ids=true | all-gather | bytes 557056 | tf_op jit(solution)/shard_map/all_gather | solution.py:210
  105.7 24.4 %reduce-scatter.6.cloned.1.call-done = f32[16,1024]{1,0:T(8,128)} async-done(((f32[256,1024]{1,0:T(8,128)}), f32[16,1024]{1,0:T(8,128)}) %reduce-scatter.6.cloned.1.call-update) | async-done | bytes 65552 | tf_op jit(solution)/shard_map/reduce_scatter | solution.py:173
  131.4 23.6 %all_gather.9 = bf16[256,1024]{1,0:T(8,128)(2,1)S(1)} all-gather(bf16[16,1024]{1,0:T(8,128)(2,1)S(1)} %fusion.69), channel_id=1, replica_groups=mesh['grid'=32,'head'=16] {'head'}, dimensions={0}, use_global_device_ids=true | all-gather | bytes 557056 | tf_op jit(solution)/shard_map/all_gather | solution.py:181
  157.0 20.3 %collective-permute-start = (bf16[128,128]{0,1:T(8,128)(2,1)}, bf16[128,128]{0,1:T(8,128)(2,1)}, u32[]{:S(2)}, u32[]{:S(2)}) collective-permute-start(bf16[128,128]{0,1:T(8,128)(2,1)} %get-tuple-element.40), channel_id=1, source_target_pairs={{0,16},{16,32},{32,48},{48,64},{64,80},{80,96},{96,112},{112,128},... | collective-permute-start | bytes 98312 | tf_op jit(solution)/shard_map/ppermute | solution.py:22
  209.4 4.0 collective-permute-start.3
  227.4 56.6 %reduce-scatter.10.cloned.1.call-done = f32[16,1024]{1,0:T(8,128)} async-done(((f32[256,1024]{1,0:T(8,128)}), f32[16,1024]{1,0:T(8,128)}) %reduce-scatter.10.cloned.1.call-update) | async-done | bytes 65552 | tf_op jit(solution)/shard_map/reduce_scatter | solution.py:242
  285.1 70.0 %reduce-scatter.8.cloned.1.call-done = f32[16,1024]{1,0:T(8,128)} async-done(((f32[256,1024]{1,0:T(8,128)}), f32[16,1024]{1,0:T(8,128)}) %reduce-scatter.8.cloned.1.call-update) | async-done | bytes 65552 | tf_op jit(solution)/shard_map/reduce_scatter | solution.py:203
  356.6 24.0 %all_gather.11 = bf16[256,1024]{1,0:T(8,128)(2,1)S(1)} all-gather(bf16[16,1024]{1,0:T(8,128)(2,1)S(1)} %get-tuple-element.42), channel_id=1, replica_groups=mesh['grid'=32,'head'=16] {'head'}, dimensions={0}, use_global_device_ids=true | all-gather | bytes 557056 | tf_op jit(solution)/shard_map/all_gather | solution.py:247
  383.5 8.2 %convolution_bitcast_fusion.1 = f32[2,3840,1,64]{1,3,0,2:T(8,128)} fusion(f32[2,128,3840]{2,1,0:T(8,128)} %fusion.43, bf16[8,2,8,128]{3,2,1,0:T(8,128)(2,1)S(1)} %copy-done.19, f32[2,128,3840]{2,1,0:T(8,128)} %get-tuple-element.51, f32[2,128]{1,0:T(2,128)S(1)} %copy-done.23), kind=kOutput, calls=%fused_computation.26 | convolution fusion | flops 132714496 | bytes 9864192 | tf_op jit(solution)/shard_map/vmap(hrs,rhd->shd)/dot_general | solution.py:86
  391.8 3.7 copy.82
  395.4 4.5 reshape.383
  409.1 24.0 %all-to-all-start.2 = ((f32[32,128,64]{1,2,0:T(8,128)}), f32[32,128,64]{1,2,0:T(8,128)}, u32[]{:S(2)}, u32[]{:S(2)}) async-start(f32[32,128,64]{1,2,0:T(8,128)} %copy.83), calls=%async_computation.5 | async-start | bytes 2097152 | tf_op jit(solution)/shard_map/all_to_all | solution.py:269
  433.1 3.9 convolution_bitcast_fusion
  437.0 3.6 copy.86
  440.7 4.5 reshape.386
  455.1 7.6 %all-to-all-start.3 = ((f32[32,128,64]{1,2,0:T(8,128)}), f32[32,128,64]{1,2,0:T(8,128)}, u32[]{:S(2)}, u32[]{:S(2)}) async-start(f32[32,128,64]{1,2,0:T(8,128)} %copy.87), calls=%async_computation.7 | async-start | bytes 2097152 | tf_op jit(solution)/shard_map/all_to_all | solution.py:276
  474.1 5.7 all-to-all-done.3
  491.0 79.8 %reduce-scatter.12.cloned.1.call-done = bf16[32,64]{1,0:T(8,128)(2,1)} async-done(((bf16[1024,64]{1,0:T(8,128)(2,1)}), bf16[32,64]{1,0:T(8,128)(2,1)}) %reduce-scatter.12.cloned.1.call-update) | async-done | bytes 4112 | tf_op jit(solution)/shard_map/reduce_scatter | solution.py:302
  572.1 102.9 %reduce-scatter.14.cloned.1.call-done = bf16[32,64]{1,0:T(8,128)(2,1)} async-done(((bf16[1024,64]{1,0:T(8,128)(2,1)}), bf16[32,64]{1,0:T(8,128)(2,1)}) %reduce-scatter.14.cloned.1.call-update) | async-done | bytes 4112 | tf_op jit(solution)/shard_map/reduce_scatter | solution.py:305
  (175 shorter events, 129.7 us)
Async XLA Ops:
  7.2 172.1 %copy-start = (bf16[64,1024]{1,0:T(8,128)(2,1)S(1)}, bf16[64,1024]{1,0:T(8,128)(2,1)}, u32[]{:S(2)}) copy-start(bf16[64,1024]{1,0:T(8,128)(2,1)} %param.33) | copy-start | bytes 393220
  15.1 12.9 %copy-start.17 = (s32[2,30]{1,0:T(2,128)S(1)}, s32[2,30]{1,0:T(2,128)}, u32[]{:S(2)}) copy-start(s32[2,30]{1,0:T(2,128)} %param.37) | copy-start | bytes 724
  15.1 12.9 %copy-start.15 = (f32[2,30,1]{1,2,0:T(1,128)S(1)}, f32[2,30,1]{1,2,0:T(1,128)}, u32[]{:S(2)}) copy-start(f32[2,30,1]{1,2,0:T(1,128)} %param.34) | copy-start | bytes 724
  17.6 22.1 %all-to-all-start.1 = ((bf16[32,128,64]{1,2,0:T(8,128)(2,1)}), bf16[32,128,64]{1,2,0:T(8,128)(2,1)S(1)}, u32[]{:S(2)}, u32[]{:S(2)}) async-start(bf16[32,128,64]{1,2,0:T(8,128)(2,1)} %get-tuple-element.48), calls=%async_computation.1 | async-start | bytes 1048576 | tf_op jit(solution)/shard_map/all_to_all | solution.py:145
  39.7 16.4 %all-to-all-start = ((bf16[32,128,64]{1,2,0:T(8,128)(2,1)}), bf16[32,128,64]{1,2,0:T(8,128)(2,1)}, u32[]{:S(2)}, u32[]{:S(2)}) async-start(bf16[32,128,64]{1,2,0:T(8,128)(2,1)} %get-tuple-element.49), calls=%async_computation | async-start | bytes 1048576 | tf_op jit(solution)/shard_map/all_to_all | solution.py:148
  44.4 85.8 %reduce-scatter.6.cloned.1.call-start = ((), (), s32[]{:S(2)}) async-start(), calls=%async_computation.9 | async-start | bytes 1114112 | tf_op jit(solution)/shard_map/reduce_scatter | solution.py:173
  45.8 15.7 %copy-start.18 = (bf16[8,2,8,128]{3,2,1,0:T(8,128)(2,1)}, bf16[8,2,8,128]{3,2,1,0:T(8,128)(2,1)S(1)}, u32[]{:S(2)}) copy-start(bf16[8,2,8,128]{3,2,1,0:T(8,128)(2,1)S(1)} %fusion.33) | copy-start | bytes 98308
  70.4 213.7 %reduce-scatter.10.cloned.1.call-start = ((), (), s32[]{:S(2)}) async-start(), calls=%async_computation.11 | async-start | bytes 1114112 | tf_op jit(solution)/shard_map/reduce_scatter | solution.py:242
  157.0 25.0 %collective-permute-start = (bf16[128,128]{0,1:T(8,128)(2,1)}, bf16[128,128]{0,1:T(8,128)(2,1)}, u32[]{:S(2)}, u32[]{:S(2)}) collective-permute-start(bf16[128,128]{0,1:T(8,128)(2,1)} %get-tuple-element.40), channel_id=1, source_target_pairs={{0,16},{16,32},{32,48},{48,64},{64,80},{80,96},{96,112},{112,128},... | collective-permute-start | bytes 98312 | tf_op jit(solution)/shard_map/ppermute | solution.py:22
  177.3 5.3 collective-permute-start.1
  199.5 13.9 %copy-start.21 = (f32[2,128]{1,0:T(2,128)S(1)}, f32[2,128]{1,0:T(2,128)}, u32[]{:S(2)}) copy-start(f32[2,128]{1,0:T(2,128)} %copy-done.20) | copy-start | bytes 3076
  206.4 11.7 %collective-permute-start.2 = (f32[128,128]{0,1:T(8,128)}, f32[128,128]{0,1:T(8,128)}, u32[]{:S(2)}, u32[]{:S(2)}) collective-permute-start(f32[128,128]{0,1:T(8,128)} %get-tuple-element.37), channel_id=1, source_target_pairs={{0,16},{16,32},{32,48},{48,64},{64,80},{80,96},{96,112},{112,128},... | collective-permute-start | bytes 196616 | tf_op jit(solution)/shard_map/ppermute | solution.py:22
  209.4 10.1 %collective-permute-start.3 = (f32[128,128]{0,1:T(8,128)}, f32[128,128]{0,1:T(8,128)}, u32[]{:S(2)}, u32[]{:S(2)}) collective-permute-start(f32[128,128]{0,1:T(8,128)} %get-tuple-element.36), channel_id=1, source_target_pairs={{16,0},{32,16},{48,32},{64,48},{80,64},{96,80},{112,96},{128,112},... | collective-permute-start | bytes 196616 | tf_op jit(solution)/shard_map/ppermute | solution.py:25
  219.5 161.1 %copy-start.6 = (bf16[64,1024]{1,0:T(8,128)(2,1)S(1)}, bf16[64,1024]{1,0:T(8,128)(2,1)}, u32[]{:S(2)}) copy-start(bf16[64,1024]{1,0:T(8,128)(2,1)} %param.29) | copy-start | bytes 393220
  222.1 133.0 %copy-start.11 = (bf16[16,1024]{1,0:T(8,128)(2,1)S(1)}, bf16[16,1024]{1,0:T(8,128)(2,1)}, u32[]{:S(2)}) copy-start(bf16[16,1024]{1,0:T(8,128)(2,1)} %param.39) | copy-start | bytes 98308
  224.5 130.6 %reduce-scatter.8.cloned.1.call-start = ((), (), s32[]{:S(2)}) async-start(), calls=%async_computation.10 | async-start | bytes 1114112 | tf_op jit(solution)/shard_map/reduce_scatter | solution.py:203
  227.3 156.3 %copy-start.19 = (bf16[8,2,8,128]{3,2,1,0:T(8,128)(2,1)S(1)}, bf16[8,2,8,128]{3,2,1,0:T(8,128)(2,1)}, u32[]{:S(2)}) copy-start(bf16[8,2,8,128]{3,2,1,0:T(8,128)(2,1)} %copy-done.18) | copy-start | bytes 98308
  227.3 156.3 %copy-start.23 = (f32[2,128]{1,0:T(2,128)S(1)}, f32[2,128]{1,0:T(2,128)}, u32[]{:S(2)}) copy-start(f32[2,128]{1,0:T(2,128)} %copy-done.22) | copy-start | bytes 3076
  409.1 46.0 %all-to-all-start.2 = ((f32[32,128,64]{1,2,0:T(8,128)}), f32[32,128,64]{1,2,0:T(8,128)}, u32[]{:S(2)}, u32[]{:S(2)}) async-start(f32[32,128,64]{1,2,0:T(8,128)} %copy.83), calls=%async_computation.5 | async-start | bytes 2097152 | tf_op jit(solution)/shard_map/all_to_all | solution.py:269
  455.1 13.9 %copy-start.14 = (s32[1,32]{1,0:T(1,128)S(1)}, s32[1,32]{1,0:T(1,128)}, u32[]{:S(2)}) copy-start(s32[1,32]{1,0:T(1,128)} %param.36) | copy-start | bytes 388
  455.1 24.8 %all-to-all-start.3 = ((f32[32,128,64]{1,2,0:T(8,128)}), f32[32,128,64]{1,2,0:T(8,128)}, u32[]{:S(2)}, u32[]{:S(2)}) async-start(f32[32,128,64]{1,2,0:T(8,128)} %copy.87), calls=%async_computation.7 | async-start | bytes 2097152 | tf_op jit(solution)/shard_map/all_to_all | solution.py:276
  462.6 108.1 %reduce-scatter.12.cloned.1.call-start = ((), (), s32[]{:S(2)}) async-start(), calls=%async_computation.12 | async-start | bytes 270336 | tf_op jit(solution)/shard_map/reduce_scatter | solution.py:302
  474.1 200.9 %reduce-scatter.14.cloned.1.call-start = ((), (), s32[]{:S(2)}) async-start(), calls=%async_computation.13 | async-start | bytes 270336 | tf_op jit(solution)/shard_map/reduce_scatter | solution.py:305
  483.0 193.3 %copy-start.1 = (bf16[64,1024]{1,0:T(8,128)(2,1)S(1)}, bf16[64,1024]{1,0:T(8,128)(2,1)}, u32[]{:S(2)}) copy-start(bf16[64,1024]{1,0:T(8,128)(2,1)} %param.33) | copy-start | bytes 393220
  (13 other events, 59.3 us)
Sparse Core Ops, SparseCore 0:
  70.5 59.5 reduce-scatter.5
  224.7 59.3 reduce-scatter.9
  286.8 68.2 reduce-scatter.7
  474.2 96.5 reduce-scatter.11
  575.6 99.3 reduce-scatter.13
where the time goes:
time: 686 us; the launch traced here: 683 us
  waiting for transfers between devices  356 us (52%)
  blocking collectives  79.9 us (12%)
  starting transfers between devices  76.4 us (11%)
  local copies, waits for them, and re-layouts  67.7 us (10%)
  matrix products  59.9 us (9%)
  other arithmetic  28.8 us (4%)
  between operations  14.3 us (2%)
    reduce_scatter x1, waiting for transfers between devices, on_device(): lax.psum_scatter(value_part.astype(jnp.bfloat16), 'grid', scatter_dimensi...  103 us
    reduce_scatter x1, waiting for transfers between devices, on_device(): lax.psum_scatter(key_part.astype(jnp.bfloat16), 'grid', scatter_dimension...  79.8 us
    reduce_scatter x1, waiting for transfers between devices, on_device(): lax.psum_scatter(jnp.dot(picked_rows, layer_out_weight, preferred_element...  70 us
    reduce_scatter x1, waiting for transfers between devices, on_device(): lax.psum_scatter(dot_right(grad_projected, layer_weights), 'head', scatte...  56.6 us
    all_gather x1, blocking collectives, on_device(): grad_rows = lax.all_gather(cotangent, 'head', axis=0, tiled=True)  32.3 us
    reduce_scatter x1, waiting for transfers between devices, on_device(): lax.psum_scatter(jnp.dot(picked_rows, enc_out_weight, preferred_element_t...  24.4 us
    all_to_all x1, starting transfers between devices, on_device(): lax.all_to_all(grad_pool_keys[grid_count:].reshape(shards, BLOCK, head_wi...  24 us
    all_gather x1, blocking collectives, on_device(): lax.all_gather(grad_enc.astype(jnp.bfloat16), 'head', axis=0, tiled=True)  24 us
  transfers between devices with their start and end apart: 13, of which 9 were waited for; matrix products, arithmetic and copies ran while one was open for 10% of the time, Pallas kernels for 0%

commit v1 on v0

v1 whole, which is shorter than its diff:
```python
import jax
import jax.numpy as jnp
from jax import lax
from jax.experimental import pallas as pl
from jax.experimental.pallas import tpu as pltpu
from jax.sharding import PartitionSpec as P

D = 64
B = 128
C = 1024
FULL = 30
REST = 9
epsilon = 1e-05
score_scale = 0.125

f32 = jnp.float32
bf16 = jnp.bfloat16

NN = (((1,), (0,)), ((), ()))
NT = (((1,), (1,)), ((), ()))
TN = (((0,), (0,)), ((), ()))

VMEM = pl.BlockSpec(memory_space=pltpu.VMEM)
SMEM = pl.BlockSpec(memory_space=pltpu.SMEM)


def dot(left, right, dims=NN):
    return lax.dot_general(left, right, dims, preferred_element_type=f32)


def struct(shape, dtype):
    return jax.ShapeDtypeStruct(shape, dtype)


def call(body, outs, specs, scratch=(), mib=40, flops=1 << 26, data=1 << 22, name=None, **extra):
    return pl.pallas_call(
        body,
        out_shape=outs,
        in_specs=specs,
        scratch_shapes=list(scratch),
        compiler_params=pltpu.CompilerParams(vmem_limit_bytes=mib << 20),
        cost_estimate=pl.CostEstimate(flops=flops, bytes_accessed=data, transcendentals=0),
        name=name,
        **extra,
    )


def normalize(values):
    center = values - jnp.mean(values, axis=-1, keepdims=True)
    inverse = lax.rsqrt(jnp.mean(center * center, axis=-1, keepdims=True) + epsilon)
    return center * inverse, inverse


def grid_kernel(send_ref, feat_ref, wk_ref, wv_ref, norm_ref, kv_ref, out_ref):
    step = pl.program_id(0)
    unit, _ = normalize(feat_ref[...].astype(f32))
    rows = unit.astype(bf16)
    norm_ref[...] = rows
    keys = dot(rows, wk_ref[...]).astype(bf16)
    values = dot(rows, wv_ref[...]).astype(bf16)
    both = jnp.concatenate([keys, values], axis=1)
    per = both.shape[0] // B
    for i in range(per):
        kv_ref[step * per + i] = both[i * B : (i + 1) * B]

    @pl.when(step == pl.num_programs(0) - 1)
    def _():
        for i in range(out_ref.shape[0]):
            out_ref[i] = kv_ref[send_ref[i]]


def grid_part(send, feat, wk, wv, shards):
    rows = feat.shape[0]
    steps = 4
    return pl.pallas_call(
        grid_kernel,
        grid=(steps,),
        out_shape=(
            struct((rows, C), bf16),
            struct((rows // B, B, 2 * D), bf16),
            struct((shards, B, 2 * D), bf16),
        ),
        in_specs=[
            SMEM,
            pl.BlockSpec((rows // steps, C), lambda i: (i, 0)),
            pl.BlockSpec((C, D), lambda i: (0, 0)),
            pl.BlockSpec((C, D), lambda i: (0, 0)),
        ],
        out_specs=(
            pl.BlockSpec((rows // steps, C), lambda i: (i, 0)),
            pl.BlockSpec((rows // B, B, 2 * D), lambda i: (0, 0, 0)),
            pl.BlockSpec((shards, B, 2 * D), lambda i: (0, 0, 0)),
        ),
        compiler_params=pltpu.CompilerParams(vmem_limit_bytes=40 << 20),
        cost_estimate=pl.CostEstimate(
            flops=1 << 28, bytes_accessed=6 << 20, transcendentals=0
        ),
        name="grid_part",
    )(send, feat, wk, wv)


def query_kernel(mesh_ref, wq_ref, out_ref):
    for b in range(out_ref.shape[0]):
        unit, _ = normalize(mesh_ref[b * B : (b + 1) * B].astype(f32))
        rows = dot(unit.astype(bf16), wq_ref[...]).astype(bf16).astype(f32) * score_scale
        out_ref[b] = rows.T.astype(bf16)


def fill_pool(pool_ref, own_ref, arrived_ref):
    own = own_ref.shape[0]
    for i in range(own):
        pool_ref[i] = own_ref[i]
    for i in range(arrived_ref.shape[0]):
        pool_ref[own + i] = arrived_ref[i]


def folded(op, values):
    parts = [values[i * 8 : (i + 1) * 8] for i in range(values.shape[0] // 8)]
    while len(parts) > 1:
        parts = [
            op(parts[i], parts[i + 1]) if i + 1 < len(parts) else parts[i]
            for i in range(0, len(parts), 2)
        ]
    return parts[0]


def encoder_kernel(
    slot_ref, count_ref, bias_ref, own_ref, arrived_ref, query_ref,
    wide_ref, out_ref, lse_ref, pool_ref, score_ref,
):
    fill_pool(pool_ref, own_ref, arrived_ref)
    full = jnp.where(count_ref[0] == FULL, 0, 1)
    for m, total in ((full, FULL), (1 - full, REST)):
        stack = jnp.concatenate([query_ref[m], jnp.zeros((D, B), bf16)], axis=0)

        def scores(e, top, m=m, stack=stack):
            value = dot(pool_ref[slot_ref[m, e]], stack) + bias_ref[m, e]
            score_ref[e] = value
            return jnp.maximum(top, folded(jnp.maximum, value))

        top = lax.fori_loop(0, total, scores, jnp.full((8, B), -jnp.inf, f32), unroll=3)
        top = jnp.max(top, axis=0, keepdims=True)

        def mix(e, carry, m=m, top=top):
            low, acc = carry
            raised = jnp.exp(score_ref[e] - top)
            acc = acc + dot(pool_ref[slot_ref[m, e]], raised.astype(bf16), TN)
            return low + folded(jnp.add, raised), acc

        low, acc = lax.fori_loop(
            0, total, mix, (jnp.zeros((8, B), f32), jnp.zeros((2 * D, B), f32)), unroll=3
        )
        low = jnp.sum(low, axis=0, keepdims=True)
        rows = acc[D:] / low
        wide_ref[m] = rows
        out_ref[m] = rows.astype(bf16)
        lse_ref[m] = jnp.broadcast_to(top + jnp.log(low), (8, B))


def middle_kernel(
    heads_ref, gathered_ref, mesh_ref, wq_ref, wk_ref, wv_ref, wl_ref,
    pack_ref, enc_ref, unit_ref, inv_ref,
):
    parts = heads_ref.shape[0]
    w_out = gathered_ref[:, 0:D, :].reshape(parts * D, C)
    half = parts // 2
    queries, grads = [], []
    for b in range(2):
        rows = slice(b * B, (b + 1) * B)
        heads = heads_ref[:, b].reshape(parts * D, B)
        enc = mesh_ref[rows].astype(f32) + dot(heads, w_out, TN)
        enc_ref[rows] = enc
        unit, inverse = normalize(enc)
        unit = unit.astype(bf16)
        unit_ref[rows] = unit
        inv_ref[rows] = jnp.broadcast_to(inverse, (B, 128))
        queries.append((dot(unit, wq_ref[...]).astype(bf16).astype(f32) * score_scale).astype(bf16))
        keys = dot(unit, wk_ref[...]).astype(bf16)
        values = dot(unit, wv_ref[...]).astype(bf16)
        pack_ref[rows] = jnp.concatenate([keys, values], axis=1)
        cot = gathered_ref[half * b : half * (b + 1), D:, :].reshape(B, C)
        grads.append(dot(cot, wl_ref[...], NT).astype(bf16))
    pack_ref[2 * B : 3 * B] = jnp.concatenate(queries, axis=1)
    pack_ref[3 * B : 4 * B] = jnp.concatenate(grads, axis=1)


def side_kernel(gathered_ref, unit_ref, inv_ref, wo_ref, cot_ref, unit_out_ref, inv_out_ref, sum_ref):
    half = gathered_ref.shape[0] // 2
    weight = wo_ref[...]
    for b in range(2):
        rows = slice(b * B, (b + 1) * B)
        cot = gathered_ref[half * b : half * (b + 1), D:, :].reshape(B, C)
        cot_ref[b] = dot(weight, cot, NT)
        unit_out_ref[b] = dot(weight, unit_ref[rows], NT)
        inv_out_ref[b] = inv_ref[rows].T[0:8]
    sum_ref[...] = jnp.broadcast_to(
        jnp.sum(weight.astype(f32), axis=1, keepdims=True), sum_ref.shape
    )


def layer_kernel(
    bias_ref, left_bias_ref, right_bias_ref, own_ref, left_ref, right_ref, unit_ref,
    wq_ref, wk_ref, wv_ref, gathered_ref, send_ref, heads_ref,
):
    zero = jnp.zeros((B, D), bf16)

    def block(ref, b):
        return ref[b * B : (b + 1) * B]

    def stacked(ref, b):
        lanes = slice(b * D, (b + 1) * D)
        query = ref[2 * B : 3 * B][:, lanes]
        grad = ref[3 * B : 4 * B][:, lanes]
        return jnp.concatenate(
            [jnp.concatenate([query, zero], axis=1), jnp.concatenate([zero, grad], axis=1)], axis=0
        )

    kv = [block(ref, b) for ref in (left_ref, own_ref, right_ref) for b in range(2)]
    queries = [(left_ref, 1, left_bias_ref), (own_ref, 0, bias_ref), (own_ref, 1, bias_ref)]
    queries.append((right_ref, 0, right_bias_ref))
    grad_kv = [jnp.zeros((B, 2 * D), f32), jnp.zeros((B, 2 * D), f32)]
    grad_q = []
    for j, (ref, b, table) in enumerate(queries):
        pair = stacked(ref, b)
        window = kv[j : j + 3]
        both = [dot(rows, pair, NT) for rows in window]
        scores = [both[n][:, :B] + table[b, n] for n in range(3)]
        top = folded(jnp.maximum, jnp.concatenate(scores, axis=0))
        top = jnp.max(top, axis=0, keepdims=True)
        raised = [jnp.exp(s - top) for s in scores]
        low = sum(folded(jnp.add, r) for r in raised)
        scale = 1.0 / jnp.sum(low, axis=0, keepdims=True)
        soft = [r * scale for r in raised]
        inner = sum(folded(jnp.add, soft[n] * both[n][:, B:]) for n in range(3))
        inner = jnp.sum(inner, axis=0, keepdims=True)
        mixed = [
            jnp.concatenate(
                [(soft[n] * (both[n][:, B:] - inner)).astype(bf16), soft[n].astype(bf16)], axis=1
            )
            for n in range(3)
        ]
        for n in range(3):
            own = j + n - 2
            if 0 <= own < 2:
                grad_kv[own] = grad_kv[own] + dot(mixed[n], pair)
        if 1 <= j <= 2:
            back = sum(dot(mixed[n], window[n], TN) for n in range(3))
            grad_q.append((back[:B, :D] * score_scale).astype(bf16))
            heads_ref[b * B : (b + 1) * B] = back[B:, D:].astype(bf16)
    parts = gathered_ref.shape[0]
    totals, stats = [], []
    lane = lax.broadcasted_iota(jnp.int32, (B, 128), 1)
    for b in range(2):
        grad = grad_kv[b].astype(bf16)
        total = (
            dot(grad_q[b], wq_ref[...], NT)
            + dot(grad[:, :D], wk_ref[...], NT)
            + dot(grad[:, D:], wv_ref[...], NT)
        )
        first = jnp.mean(total, axis=1, keepdims=True)
        second = jnp.mean(total * unit_ref[b * B : (b + 1) * B].astype(f32), axis=1, keepdims=True)
        table = jnp.where(lane == 0, first, jnp.where(lane == 1, second, 0.0)).T[0:8]
        high = table.astype(bf16).astype(f32)
        stats.append(jnp.concatenate([high, table - high], axis=0).astype(bf16))
        totals.append(total.astype(bf16))
    total = jnp.concatenate(totals, axis=0)
    for z in range(parts):
        piece = dot(gathered_ref[z, 0:D, :], total, NT).astype(bf16)
        for b in range(2):
            send_ref[z, b, 0:D] = piece[:, b * B : (b + 1) * B]
            send_ref[z, b, D : D + 16] = stats[b]


def back_kernel(
    slot_ref, count_ref, bias_ref, me_ref, arrived_grad_ref, cot_ref, unit_ref, inv_ref, sum_ref,
    wide_ref, lse_ref, query_ref, own_ref, arrived_ref,
    own_out_ref, send_ref, pool_ref, grad_ref, pair_ref, inner_ref,
):
    fill_pool(pool_ref, own_ref, arrived_ref)
    zero = jnp.zeros((D, B), bf16)
    for b in range(2):
        total = arrived_grad_ref[0, b].astype(f32)
        for z in range(1, arrived_grad_ref.shape[0]):
            total = total + arrived_grad_ref[z, b].astype(f32)
        stats = total[D : D + 8] + total[D + 8 : D + 16]
        inside = total[:D] - stats[0:1] * sum_ref[...] - stats[1:2] * unit_ref[b]
        grad = (cot_ref[b] + inv_ref[b][0:1] * inside).astype(bf16)
        inner = jnp.sum(grad.astype(f32) * wide_ref[b], axis=0, keepdims=True)
        inner_ref[b] = jnp.broadcast_to(inner, (8, B))
        pair_ref[b] = jnp.concatenate(
            [
                jnp.concatenate([query_ref[b], zero], axis=1),
                jnp.concatenate([zero, grad], axis=1),
            ],
            axis=0,
        )
    own = own_ref.shape[0]
    grad_ref[own + me_ref[0]] = jnp.zeros((B, 2 * D), f32)
    full = jnp.where(count_ref[0] == FULL, 0, 1)
    for m, total in ((full, FULL), (1 - full, REST)):
        pair = pair_ref[m]
        lse = lse_ref[m][0:1]
        inner = inner_ref[m][0:1]

        def step(e, carry, m=m, pair=pair, lse=lse, inner=inner):
            slot = slot_ref[m, e]
            both = dot(pool_ref[slot], pair)
            soft = jnp.exp(both[:, :B] + (bias_ref[m, e] - lse))
            mixed = jnp.concatenate(
                [(soft * (both[:, B:] - inner)).astype(bf16), soft.astype(bf16)], axis=1
            )
            grad_ref[slot] = dot(mixed, pair, NT)
            return carry

        lax.fori_loop(0, total, step, 0, unroll=3)
    for i in range(own):
        own_out_ref[i] = grad_ref[i]
    for i in range(send_ref.shape[0]):
        send_ref[i] = grad_ref[own + i].astype(bf16)


def final_kernel(send_ref, norm_ref, own_ref, back_ref, out_ref, acc_ref):
    for i in range(own_ref.shape[0]):
        acc_ref[i] = own_ref[i]

    def add(i, carry):
        slot = send_ref[i]
        acc_ref[slot] = acc_ref[slot] + back_ref[i].astype(f32)
        return carry

    lax.fori_loop(0, back_ref.shape[0], add, 0, unroll=2)
    rows = acc_ref[...].reshape(norm_ref.shape[0], 2 * D).astype(bf16)
    shards, height = out_ref.shape[0], out_ref.shape[1]
    tile = 256
    for c in range(C // tile):
        part = dot(rows, norm_ref[:, c * tile : (c + 1) * tile], TN).T
        per = tile // height
        out_ref[c * per : (c + 1) * per] = part.astype(bf16).reshape(per, height, 2 * D)


def output_kernel(at_ref, heads_ref, weight_ref, enc_ref, out_ref):
    height = out_ref.shape[0]
    total = enc_ref[pl.ds(pl.multiple_of(at_ref[0] * height, height), height), :]
    for h in range(heads_ref.shape[0]):
        total = total + dot(heads_ref[h], weight_ref[h * D : (h + 1) * D])
    out_ref[...] = total.astype(bf16)


def sum_kernel(parts_ref, key_ref, value_ref):
    total = parts_ref[0].astype(f32)
    for i in range(1, parts_ref.shape[0]):
        total = total + parts_ref[i].astype(f32)
    key_ref[...] = total[:, :D]
    value_ref[...] = total[:, D:]


def exchange(array, axis):
    return lax.all_to_all(array, axis, split_axis=0, concat_axis=0, tiled=True)


def on_device(
    grid_feat,
    mesh_feat,
    query_weight,
    key_weight,
    value_weight,
    enc_out_weight,
    layer_query,
    layer_key,
    layer_value,
    layer_out_weight,
    enc_bias,
    layer_bias,
    send_list,
    edge_slot,
    edge_count,
    cotangent,
):
    shards = lax.axis_size("grid")
    parts = lax.axis_size("head")
    own = grid_feat.shape[0] // B
    share = cotangent.shape[0]
    send = send_list[0]
    enc_table = enc_bias[:, :, 0]
    layer_table = layer_bias[:, :, 0]
    shard_at = lax.axis_index("grid").astype(jnp.int32)[None]
    head_at = lax.axis_index("head").astype(jnp.int32)[None]
    forward = [(i, (i + 1) % shards) for i in range(shards)]
    backward = [(t, s) for s, t in forward]

    gathered = lax.all_gather(
        jnp.concatenate([enc_out_weight, cotangent], axis=0), "head", axis=0, tiled=False
    )
    layer_out_all = lax.all_gather(layer_out_weight, "head", axis=0, tiled=True)

    grid_norm, own_kv, outgoing = grid_part(send, grid_feat, key_weight, value_weight, shards)
    arrived_kv = exchange(outgoing, "grid")
    left_bias = lax.ppermute(layer_table, "grid", forward)
    right_bias = lax.ppermute(layer_table, "grid", backward)
    queries = call(
        query_kernel, struct((2, D, B), bf16), [VMEM] * 2, name="query_part", data=1 << 20
    )(mesh_feat, query_weight)
    wide_heads, enc_heads, lse = call(
        encoder_kernel,
        (struct((2, D, B), f32), struct((2, D, B), bf16), struct((2, 8, B), f32)),
        [SMEM] * 3 + [VMEM] * 3,
        [pltpu.VMEM((own + shards, B, 2 * D), bf16), pltpu.VMEM((FULL, B, B), f32)],
        name="encoder_part",
    )(edge_slot, edge_count, enc_table, own_kv, arrived_kv, queries)
    all_heads = lax.all_gather(enc_heads, "head", axis=0, tiled=False)
    pack, encoded, unit, inverse = call(
        middle_kernel,
        (
            struct((4 * B, 2 * D), bf16),
            struct((2 * B, C), f32),
            struct((2 * B, C), bf16),
            struct((2 * B, 128), f32),
        ),
        [VMEM] * 7,
        name="middle_part",
    )(
        all_heads, gathered, mesh_feat, layer_query, layer_key, layer_value, layer_out_weight
    )
    left = lax.ppermute(pack, "grid", forward)
    right = lax.ppermute(pack, "grid", backward)
    cot_part, unit_part, inverse_row, weight_sum = call(
        side_kernel,
        (
            struct((2, D, B), f32),
            struct((2, D, B), f32),
            struct((2, 8, B), f32),
            struct((D, B), f32),
        ),
        [VMEM] * 4,
        name="side_part",
    )(gathered, unit, inverse, enc_out_weight)
    mixed, layer_heads = call(
        layer_kernel,
        (struct((parts, 2, D + 16, B), bf16), struct((2 * B, D), bf16)),
        [SMEM] * 3 + [VMEM] * 8,
        name="layer_part",
    )(
        layer_table, left_bias, right_bias, pack, left, right, unit,
        layer_query, layer_key, layer_value, gathered,
    )
    arrived_grad = exchange(mixed, "head")
    own_grad, send_grad = call(
        back_kernel,
        (struct((own, B, 2 * D), f32), struct((shards, B, 2 * D), bf16)),
        [SMEM] * 4 + [VMEM] * 10,
        [
            pltpu.VMEM((own + shards, B, 2 * D), bf16),
            pltpu.VMEM((own + shards, B, 2 * D), f32),
            pltpu.VMEM((2, 2 * D, 2 * B), bf16),
            pltpu.VMEM((2, 8, B), f32),
        ],
        name="back_part",
    )(
        edge_slot, edge_count, enc_table, shard_at, arrived_grad, cot_part, unit_part,
        inverse_row, weight_sum, wide_heads, lse, queries, own_kv, arrived_kv,
    )
    back_grad = exchange(send_grad, "grid")
    row_heads = exchange(layer_heads.reshape(parts, share, D), "head")
    product = call(
        final_kernel,
        struct((shards, C // shards, 2 * D), bf16),
        [SMEM] + [VMEM] * 3,
        [pltpu.VMEM((own, B, 2 * D), f32)],
        name="final_part",
    )(send, grid_norm, own_grad, back_grad)
    pieces = exchange(product, "grid")
    mesh_out = call(
        output_kernel,
        struct((share, C), bf16),
        [SMEM] + [VMEM] * 3,
        name="output_part",
    )(head_at, row_heads, layer_out_all, encoded)
    key_grad, value_grad = call(
        sum_kernel,
        (struct((C // shards, D), f32), struct((C // shards, D), f32)),
        [VMEM],
        name="sum_part",
    )(pieces)
    return mesh_out, key_grad, value_grad


def solution(mesh):
    in_specs = (
        P("grid", None),
        P("grid", None),
        P(None, "head"),
        P(None, "head"),
        P(None, "head"),
        P("head", None),
        P(None, "head"),
        P(None, "head"),
        P(None, "head"),
        P("head", None),
        P("grid", None, "head"),
        P("grid", None, "head"),
        P("grid", None),
        P("grid", None),
        P("grid"),
        P(("grid", "head"), None),
    )
    out_specs = (P(("grid", "head"), None), P("grid", "head"), P("grid", "head"))
    return jax.shard_map(
        on_device, mesh=mesh, in_specs=in_specs, out_specs=out_specs, check_vma=False
    )
```

time: 686 us -> 254 us (0.37)
  waiting for transfers between devices: 356 us -> 75 us
  matrix products: 59.9 us -> 0 us
  blocking collectives: 79.9 us -> 35.3 us
  local copies, waits for them, and re-layouts: 67.7 us -> 35.5 us
  Pallas kernels: 0 us -> 28.7 us
  other arithmetic: 28.8 us -> 1.6 us
  starting transfers between devices: 76.4 us -> 62.2 us
    reduce_scatter x5 -> x0, waiting for transfers between devices: 334 us -> none  [the longest x1 103 us: on_device(): lax.psum_scatter(value_part.astype(jnp.bfloat16), 'grid', scatter_dimensi...]
    dot_general x24 -> x0, matrix products: 53.5 us -> none  [the longest x2 11.4 us: attend_back(): jnp.einsum('hrs,rhd->shd', grad_scores, query_rows, preferred_element_typ...]
    all_to_all x4 -> x5, waiting for transfers between devices: 21.3 us -> 74.1 us  [exchange(): return lax.all_to_all(array, axis, split_axis=0, concat_axis=0, tiled=True)]
    all_gather x3 -> x1, blocking collectives: 79.9 us -> 35.3 us  [on_device(): all_heads = lax.all_gather(enc_heads, 'head', axis=0, tiled=False)]
    unnamed x57 -> x106, local copies, waits for them, and re-layouts: 3.57 us -> 35.5 us
    reshape x13 -> x0, local copies, waits for them, and re-layouts: 30.1 us -> none  [the longest x2 6.27 us: on_device(): grad_pool_values[grid_count:].reshape(shards, BLOCK, head_width)]
    pallas_call x0 -> x10, Pallas kernels: none -> 28.7 us  [the longest x1 5.6 us: on_device(): call(encoder_kernel, (struct((2, D, B), f32), struct((2, D, B), bf16), st...]
    ppermute x4, starting transfers between devices: 29.3 us -> 19.3 us  [the longest x1 7.65 us: on_device(): left = lax.ppermute(pack, 'grid', forward)]
  transfers between devices with their start and end apart: 13 -> 11, of which waited for: 9 -> 6; matrix products, arithmetic and copies ran while one was open for 10% -> 2% of each run, Pallas kernels for 0% -> 10%
where the time goes in v1:
time: 254 us; the launch traced here: 253 us
  waiting for transfers between devices  75 us (30%)
  starting transfers between devices  62.2 us (24%)
  local copies, waits for them, and re-layouts  35.5 us (14%)
  blocking collectives  35.3 us (14%)
  Pallas kernels  28.7 us (11%)
  between operations  14.5 us (6%)
    all_to_all x5, waiting for transfers between devices, exchange(): return lax.all_to_all(array, axis, split_axis=0, concat_axis=0, tiled=True)  74.1 us
    all_to_all x5, starting transfers between devices, exchange(): return lax.all_to_all(array, axis, split_axis=0, concat_axis=0, tiled=True)  42.8 us
    unnamed x106, local copies, waits for them, and re-layouts  35.5 us
    all_gather x1, blocking collectives, on_device(): all_heads = lax.all_gather(enc_heads, 'head', axis=0, tiled=False)  35.3 us
    ppermute x1, starting transfers between devices, on_device(): left = lax.ppermute(pack, 'grid', forward)  7.65 us
    ppermute x1, starting transfers between devices, on_device(): right_bias = lax.ppermute(layer_table, 'grid', backward)  6.04 us
    pallas_call x1, Pallas kernels, on_device(): call(encoder_kernel, (struct((2, D, B), f32), struct((2, D, B), bf16), st...  5.6 us
    pallas_call x1, Pallas kernels, on_device(): call(back_kernel, (struct((own, B, 2 * D), f32), struct((shards, B, 2 * D...  5.56 us
  transfers between devices with their start and end apart: 11, of which 6 were waited for; matrix products, arithmetic and copies ran while one was open for 2% of the time, Pallas kernels for 10%

profile of v1, /device:TPU:1, one launch (start us, length us, event | category | flops | bytes accessed | tf_op | source)
XLA Modules:
  0.0 252.6 jit_solution(92470336484600330)
XLA Ops:
  7.2 1.6 pad_maximum_fusion
  11.0 1.6 copy-done.7
  13.2 4.9 %grid_part.1 = (bf16[1024,1024]{1,0:T(8,128)(2,1)S(1)}, bf16[8,128,128]{2,1,0:T(8,128)(2,1)S(1)}, bf16[32,128,128]{2,1,0:T(8,128)(2,1)}) custom-call(s32[32]{0:T(128)S(1)} %bitcast.15, bf16[1024,1024]{1,0:T(8,128)(2,1)S(1)} %copy-done.7, bf16[1024,64]{1,0:T(8,128)(2,1)S(1)} %copy.28.wk_ref, bf16[1024,64]{1,0:T(8,128)(2,1)S(1)} %copy.29.wv_ref), custom_call_target="tpu_custom_call" | custom-call | flops 268435456 | bytes 6291456 | tf_op jit(solution)/shard_map/grid_part/pallas_call | solution.py:75
  19.5 10.6 %all-to-all-start = ((bf16[32,128,128]{2,1,0:T(8,128)(2,1)}), bf16[32,128,128]{2,1,0:T(8,128)(2,1)S(1)}, u32[]{:S(2)}, u32[]{:S(2)}) async-start(bf16[32,128,128]{2,1,0:T(8,128)(2,1)} %get-tuple-element.24), calls=%async_computation | async-start | bytes 2097152 | tf_op jit(solution)/shard_map/all_to_all | solution.py:358
  32.4 14.9 %all-to-all-done.arrived_ref = bf16[32,128,128]{2,1,0:T(8,128)(2,1)S(1)} async-done(((bf16[32,128,128]{2,1,0:T(8,128)(2,1)}), bf16[32,128,128]{2,1,0:T(8,128)(2,1)S(1)}, u32[]{:S(2)}, u32[]{:S(2)}) %all-to-all-start) | async-done | bytes 1048608 | tf_op jit(solution)/shard_map/all_to_all | solution.py:358
  47.4 5.6 %encoder_part.1 = (f32[2,64,128]{2,1,0:T(8,128)S(1)}, bf16[2,64,128]{2,1,0:T(8,128)(2,1)S(1)}, f32[2,8,128]{2,1,0:T(8,128)S(1)}) custom-call(s32[2,30]{1,0:T(2,128)S(1)} %copy-done.37, s32[2]{0:T(128)S(1)} %copy-done.41, f32[2,30]{1,0:T(2,128)S(1)} %bitcast.13, bf16[8,128,128]{2,1,0:T(8,128)(2,1)S(1)} %get-tuple-element.23.own_ref, ...), custom_call_target="tpu_custom_call" | custom-call | flops 67108864 | bytes 4194304 | tf_op jit(solution)/shard_map/encoder_part/pallas_call | solution.py:403
  53.0 35.3 %all-gather = bf16[32,64,128]{2,1,0:T(8,128)(2,1)} all-gather(bf16[2,64,128]{2,1,0:T(8,128)(2,1)S(1)} %get-tuple-element.25), channel_id=2, replica_groups=mesh['grid'=32,'head'=16] {'head'}, dimensions={0}, use_global_device_ids=true | all-gather | bytes 557056 | tf_op jit(solution)/shard_map/all_gather | solution.py:410
  88.4 1.7 copy-done
  92.2 2.8 %middle_part.1 = (bf16[512,128]{1,0:T(8,128)(2,1)}, f32[256,1024]{1,0:T(8,128)S(1)}, bf16[256,1024]{1,0:T(8,128)(2,1)S(1)}, f32[256,128]{1,0:T(8,128)S(1)}) custom-call(bf16[16,2,64,128]{3,2,1,0:T(8,128)(2,1)S(1)} %bitcast.11, bf16[16,80,1024]{2,1,0:T(8,128)(2,1)S(1)} %bitcast.8, bf16[256,1024]{1,0:T(8,128)(2,1)S(1)} %copy-done.5, ...), custom_call_target="tpu_custom_call" | custom-call | flops 67108864 | bytes 4194304 | tf_op jit(solution)/shard_map/middle_part/pallas_call | solution.py:411
  97.4 7.6 %collective-permute-start.2 = (bf16[512,128]{1,0:T(8,128)(2,1)}, bf16[512,128]{1,0:T(8,128)(2,1)S(1)}, u32[]{:S(2)}, u32[]{:S(2)}) collective-permute-start(bf16[512,128]{1,0:T(8,128)(2,1)} %get-tuple-element.26.own_ref), channel_id=1, source_target_pairs={{0,16},{16,32},{32,48},{48,64},{64,80},{80,96},{96,112},{112,128},... | collective-permute-start | bytes 393224 | tf_op jit(solution)/shard_map/ppermute | solution.py:424
  105.1 2.7 %collective-permute-start.3 = (bf16[512,128]{1,0:T(8,128)(2,1)}, bf16[512,128]{1,0:T(8,128)(2,1)}, u32[]{:S(2)}, u32[]{:S(2)}) collective-permute-start(bf16[512,128]{1,0:T(8,128)(2,1)} %get-tuple-element.26.own_ref), channel_id=1, source_target_pairs={{16,0},{32,16},{48,32},{64,48},{80,64},{96,80},{112,96},{128,112},... | collective-permute-start | bytes 393224 | tf_op jit(solution)/shard_map/ppermute | solution.py:425
  107.9 2.8 %collective-permute-start = (f32[2,3]{1,0:T(2,128)S(1)}, f32[2,3]{1,0:T(2,128)S(1)}, u32[]{:S(2)}, u32[]{:S(2)}) collective-permute-start(f32[2,3]{1,0:T(2,128)S(1)} %bitcast.17), channel_id=1, source_target_pairs={{0,16},{16,32},{32,48},{48,64},{64,80},{80,96},{96,112},{112,128},... | collective-permute-start | bytes 80 | tf_op jit(solution)/shard_map/ppermute | solution.py:398
  110.7 6.0 %collective-permute-start.1 = (f32[2,3]{1,0:T(2,128)S(1)}, f32[2,3]{1,0:T(2,128)S(1)}, u32[]{:S(2)}, u32[]{:S(2)}) collective-permute-start(f32[2,3]{1,0:T(2,128)S(1)} %bitcast.18), channel_id=1, source_target_pairs={{16,0},{32,16},{48,32},{64,48},{80,64},{96,80},{112,96},{128,112},... | collective-permute-start | bytes 80 | tf_op jit(solution)/shard_map/ppermute | solution.py:399
  118.6 4.9 %layer_part.1 = (bf16[16,2,80,128]{3,2,1,0:T(8,128)(2,1)S(1)}, bf16[256,64]{1,0:T(8,128)(2,1)S(1)}) custom-call(f32[2,3]{1,0:T(2,128)S(1)} %bitcast.19, f32[2,3]{1,0:T(2,128)S(1)} %collective-permute-done.left_bias_ref, f32[2,3]{1,0:T(2,128)S(1)} %collective-permute-done.1.right_bias_ref, bf16[512,128]{1,0:T(8,128)(2,1)} %get-tuple-element.26.own_ref, ...), custom_call_target="tpu_custom_call" | custom-call | flops 67108864 | bytes 4194304 | tf_op jit(solution)/shard_map/layer_part/pallas_call | solution.py:437
  125.1 6.6 %all-to-all-start.2 = ((bf16[16,2,80,128]{3,2,1,0:T(8,128)(2,1)}), bf16[16,2,80,128]{3,2,1,0:T(8,128)(2,1)S(1)}, u32[]{:S(2)}, u32[]{:S(2)}) async-start(bf16[16,2,80,128]{3,2,1,0:T(8,128)(2,1)} %copy-done.19), calls=%async_computation.2 | async-start | bytes 1310720 | tf_op jit(solution)/shard_map/all_to_all | solution.py:358
  136.8 30.1 %all-to-all-done.2.arrived_grad_ref = bf16[16,2,80,128]{3,2,1,0:T(8,128)(2,1)S(1)} async-done(((bf16[16,2,80,128]{3,2,1,0:T(8,128)(2,1)}), bf16[16,2,80,128]{3,2,1,0:T(8,128)(2,1)S(1)}, u32[]{:S(2)}, u32[]{:S(2)}) %all-to-all-start.2) | async-done | bytes 655392 | tf_op jit(solution)/shard_map/all_to_all | solution.py:358
  174.2 5.6 %back_part.1 = (f32[8,128,128]{2,1,0:T(8,128)S(1)}, bf16[32,128,128]{2,1,0:T(8,128)(2,1)S(1)}) custom-call(s32[2,30]{1,0:T(2,128)S(1)} %copy-done.38, s32[2]{0:T(128)S(1)} %copy-done.42, f32[2,30]{1,0:T(2,128)S(1)} %bitcast.14, s32[1]{0:T(128)} %bitcast.7.me_ref, bf16[16,2,80,128]{3,2,1,0:T(8,128)(2,1)S(1)} %all-to-all-done.2.arrived_grad_ref, ...), custom_call_target="tpu_custom_call" | custom-call | flops 67108864 | bytes 4194304 | tf_op jit(solution)/shard_map/back_part/pallas_call | solution.py:447
  181.6 12.1 %all-to-all-start.3 = ((bf16[32,128,128]{2,1,0:T(8,128)(2,1)}), bf16[32,128,128]{2,1,0:T(8,128)(2,1)S(1)}, u32[]{:S(2)}, u32[]{:S(2)}) async-start(bf16[32,128,128]{2,1,0:T(8,128)(2,1)} %copy-done.18), calls=%async_computation.3 | async-start | bytes 2097152 | tf_op jit(solution)/shard_map/all_to_all | solution.py:358
  195.2 15.7 %all-to-all-done.3.back_ref = bf16[32,128,128]{2,1,0:T(8,128)(2,1)S(1)} async-done(((bf16[32,128,128]{2,1,0:T(8,128)(2,1)}), bf16[32,128,128]{2,1,0:T(8,128)(2,1)S(1)}, u32[]{:S(2)}, u32[]{:S(2)}) %all-to-all-start.3) | async-done | bytes 1048608 | tf_op jit(solution)/shard_map/all_to_all | solution.py:358
  210.9 8.3 %all-to-all-start.1 = ((bf16[16,2,512]{2,1,0:T(2,128)(2,1)}), bf16[16,2,512]{2,1,0:T(2,128)(2,1)S(1)}, u32[]{:S(2)}, u32[]{:S(2)}) async-start(bf16[16,2,512]{2,1,0:T(2,128)(2,1)} %reshape.12), calls=%async_computation.1 | async-start | bytes 65536 | tf_op jit(solution)/shard_map/all_to_all | solution.py:358
  220.3 2.1 final_part.1
  222.4 8.3 %all-to-all-done.1 = bf16[16,2,512]{2,1,0:T(2,128)(2,1)S(1)} async-done(((bf16[16,2,512]{2,1,0:T(2,128)(2,1)}), bf16[16,2,512]{2,1,0:T(2,128)(2,1)S(1)}, u32[]{:S(2)}, u32[]{:S(2)}) %all-to-all-start.1) | async-done | bytes 32800 | tf_op jit(solution)/shard_map/all_to_all | solution.py:358
  230.8 5.3 %all-to-all-start.4 = ((bf16[32,32,128]{2,1,0:T(8,128)(2,1)}), bf16[32,32,128]{2,1,0:T(8,128)(2,1)S(1)}, u32[]{:S(2)}, u32[]{:S(2)}) async-start(bf16[32,32,128]{2,1,0:T(8,128)(2,1)} %final_part.1), calls=%async_computation.4 | async-start | bytes 524288 | tf_op jit(solution)/shard_map/all_to_all | solution.py:358
  240.0 5.0 %all-to-all-done.4.parts_ref = bf16[32,32,128]{2,1,0:T(8,128)(2,1)S(1)} async-done(((bf16[32,32,128]{2,1,0:T(8,128)(2,1)}), bf16[32,32,128]{2,1,0:T(8,128)(2,1)S(1)}, u32[]{:S(2)}, u32[]{:S(2)}) %all-to-all-start.4) | async-done | bytes 262176 | tf_op jit(solution)/shard_map/all_to_all | solution.py:358
  (118 shorter events, 35.9 us)
Async XLA Ops:
  7.2 81.2 %all-gather.7.cloned.1.call-start = ((), (), s32[]{:S(2)}) async-start(), calls=%async_computation.6 | async-start | bytes 2785280 | tf_op jit(solution)/shard_map/all_gather | solution.py:391
  13.2 17.1 %copy-start.47 = (bf16[1024,64]{0,1:T(8,128)(2,1)S(1)}, bf16[1024,64]{0,1:T(8,128)(2,1)}, u32[]{:S(2)}) copy-start(bf16[1024,64]{0,1:T(8,128)(2,1)} %param.22) | copy-start | bytes 393220
  19.4 27.9 %copy-start.14 = (bf16[8,128,128]{2,1,0:T(8,128)(2,1)}, bf16[8,128,128]{2,1,0:T(8,128)(2,1)S(1)}, u32[]{:S(2)}) copy-start(bf16[8,128,128]{2,1,0:T(8,128)(2,1)S(1)} %get-tuple-element.23.own_ref) | copy-start | bytes 786436
  19.4 27.9 %copy-start.37 = (s32[2,30]{1,0:T(2,128)S(1)}, s32[2,30]{1,0:T(2,128)}, u32[]{:S(2)}) copy-start(s32[2,30]{1,0:T(2,128)} %slot_ref.3) | copy-start | bytes 724
  19.4 27.9 %copy-start.39 = (f32[2,30,1]{1,2,0:T(1,128)S(1)}, f32[2,30,1]{1,2,0:T(1,128)}, u32[]{:S(2)}) copy-start(f32[2,30,1]{1,2,0:T(1,128)} %param.26) | copy-start | bytes 724
  19.5 27.9 %copy-start.41 = (s32[2]{0:T(128)S(1)}, s32[2]{0:T(128)}, u32[]{:S(2)}) copy-start(s32[2]{0:T(128)} %count_ref.3) | copy-start | bytes 28
  19.5 27.9 %all-to-all-start = ((bf16[32,128,128]{2,1,0:T(8,128)(2,1)}), bf16[32,128,128]{2,1,0:T(8,128)(2,1)S(1)}, u32[]{:S(2)}, u32[]{:S(2)}) async-start(bf16[32,128,128]{2,1,0:T(8,128)(2,1)} %get-tuple-element.24), calls=%async_computation | async-start | bytes 2097152 | tf_op jit(solution)/shard_map/all_to_all | solution.py:358
  30.1 58.3 %copy-start.22 = (bf16[64,1024]{1,0:T(8,128)(2,1)S(1)}, bf16[64,1024]{1,0:T(8,128)(2,1)}, u32[]{:S(2)}) copy-start(bf16[64,1024]{1,0:T(8,128)(2,1)} %wl_ref.1) | copy-start | bytes 393220
  30.1 206.1 %all-gather.5.cloned.1.call-start = ((), (), s32[]{:S(2)}) async-start(), calls=%async_computation.5 | async-start | bytes 2228224 | tf_op jit(solution)/shard_map/all_gather | solution.py:394
  32.4 55.9 %copy-start.24 = (bf16[2,64,128]{2,1,0:T(8,128)(2,1)}, bf16[2,64,128]{2,1,0:T(8,128)(2,1)S(1)}, u32[]{:S(2)}) copy-start(bf16[2,64,128]{2,1,0:T(8,128)(2,1)S(1)} %query_part.1.query_ref) | copy-start | bytes 98308
  47.4 41.0 %copy-start.2 = (bf16[32,128,128]{2,1,0:T(8,128)(2,1)}, bf16[32,128,128]{2,1,0:T(8,128)(2,1)S(1)}, u32[]{:S(2)}) copy-start(bf16[32,128,128]{2,1,0:T(8,128)(2,1)S(1)} %all-to-all-done.arrived_ref) | copy-start | bytes 3145732
  53.0 35.3 %copy-start.28 = (f32[2,64,128]{2,1,0:T(8,128)}, f32[2,64,128]{2,1,0:T(8,128)S(1)}, u32[]{:S(2)}) copy-start(f32[2,64,128]{2,1,0:T(8,128)S(1)} %get-tuple-element.37.wide_ref) | copy-start | bytes 196612
  92.2 25.4 %copy-start.1 = (bf16[1280,1024]{1,0:T(8,128)(2,1)S(1)}, bf16[1280,1024]{1,0:T(8,128)(2,1)}, u32[]{:S(2)}) copy-start(bf16[1280,1024]{1,0:T(8,128)(2,1)} %all-gather.7.cloned.1.call-done) | copy-start | bytes 7864324
  97.4 20.1 %collective-permute-start.2 = (bf16[512,128]{1,0:T(8,128)(2,1)}, bf16[512,128]{1,0:T(8,128)(2,1)S(1)}, u32[]{:S(2)}, u32[]{:S(2)}) collective-permute-start(bf16[512,128]{1,0:T(8,128)(2,1)} %get-tuple-element.26.own_ref), channel_id=1, source_target_pairs={{0,16},{16,32},{32,48},{48,64},{64,80},{80,96},{96,112},{112,128},... | collective-permute-start | bytes 393224 | tf_op jit(solution)/shard_map/ppermute | solution.py:424
  105.1 12.5 %collective-permute-start.3 = (bf16[512,128]{1,0:T(8,128)(2,1)}, bf16[512,128]{1,0:T(8,128)(2,1)}, u32[]{:S(2)}, u32[]{:S(2)}) collective-permute-start(bf16[512,128]{1,0:T(8,128)(2,1)} %get-tuple-element.26.own_ref), channel_id=1, source_target_pairs={{16,0},{32,16},{48,32},{64,48},{80,64},{96,80},{112,96},{128,112},... | collective-permute-start | bytes 393224 | tf_op jit(solution)/shard_map/ppermute | solution.py:425
  107.9 8.9 %collective-permute-start = (f32[2,3]{1,0:T(2,128)S(1)}, f32[2,3]{1,0:T(2,128)S(1)}, u32[]{:S(2)}, u32[]{:S(2)}) collective-permute-start(f32[2,3]{1,0:T(2,128)S(1)} %bitcast.17), channel_id=1, source_target_pairs={{0,16},{16,32},{32,48},{48,64},{64,80},{80,96},{96,112},{112,128},... | collective-permute-start | bytes 80 | tf_op jit(solution)/shard_map/ppermute | solution.py:398
  110.7 6.8 %collective-permute-start.1 = (f32[2,3]{1,0:T(2,128)S(1)}, f32[2,3]{1,0:T(2,128)S(1)}, u32[]{:S(2)}, u32[]{:S(2)}) collective-permute-start(f32[2,3]{1,0:T(2,128)S(1)} %bitcast.18), channel_id=1, source_target_pairs={{16,0},{32,16},{48,32},{64,48},{80,64},{96,80},{112,96},{128,112},... | collective-permute-start | bytes 80 | tf_op jit(solution)/shard_map/ppermute | solution.py:399
  125.1 41.9 %copy-start.15 = (bf16[8,128,128]{2,1,0:T(8,128)(2,1)S(1)}, bf16[8,128,128]{2,1,0:T(8,128)(2,1)}, u32[]{:S(2)}) copy-start(bf16[8,128,128]{2,1,0:T(8,128)(2,1)} %copy-done.14) | copy-start | bytes 786436
  125.1 41.9 %all-to-all-start.2 = ((bf16[16,2,80,128]{3,2,1,0:T(8,128)(2,1)}), bf16[16,2,80,128]{3,2,1,0:T(8,128)(2,1)S(1)}, u32[]{:S(2)}, u32[]{:S(2)}) async-start(bf16[16,2,80,128]{3,2,1,0:T(8,128)(2,1)} %copy-done.19), calls=%async_computation.2 | async-start | bytes 1310720 | tf_op jit(solution)/shard_map/all_to_all | solution.py:358
  181.6 37.7 %copy-start.9 = (bf16[1024,1024]{1,0:T(8,128)(2,1)S(1)}, bf16[1024,1024]{1,0:T(8,128)(2,1)}, u32[]{:S(2)}) copy-start(bf16[1024,1024]{1,0:T(8,128)(2,1)} %copy-done.8) | copy-start | bytes 6291460
  181.6 37.7 %copy-start.44 = (s32[1,32]{1,0:T(1,128)S(1)}, s32[1,32]{1,0:T(1,128)}, u32[]{:S(2)}) copy-start(s32[1,32]{1,0:T(1,128)} %param.28) | copy-start | bytes 388
  181.6 29.3 %all-to-all-start.3 = ((bf16[32,128,128]{2,1,0:T(8,128)(2,1)}), bf16[32,128,128]{2,1,0:T(8,128)(2,1)S(1)}, u32[]{:S(2)}, u32[]{:S(2)}) async-start(bf16[32,128,128]{2,1,0:T(8,128)(2,1)} %copy-done.18), calls=%async_computation.3 | async-start | bytes 2097152 | tf_op jit(solution)/shard_map/all_to_all | solution.py:358
  210.9 19.8 %all-to-all-start.1 = ((bf16[16,2,512]{2,1,0:T(2,128)(2,1)}), bf16[16,2,512]{2,1,0:T(2,128)(2,1)S(1)}, u32[]{:S(2)}, u32[]{:S(2)}) async-start(bf16[16,2,512]{2,1,0:T(2,128)(2,1)} %reshape.12), calls=%async_computation.1 | async-start | bytes 65536 | tf_op jit(solution)/shard_map/all_to_all | solution.py:358
  230.8 14.3 %all-to-all-start.4 = ((bf16[32,32,128]{2,1,0:T(8,128)(2,1)}), bf16[32,32,128]{2,1,0:T(8,128)(2,1)S(1)}, u32[]{:S(2)}, u32[]{:S(2)}) async-start(bf16[32,32,128]{2,1,0:T(8,128)(2,1)} %final_part.1), calls=%async_computation.4 | async-start | bytes 524288 | tf_op jit(solution)/shard_map/all_to_all | solution.py:358
  (36 other events, 86.1 us)
Sparse Core Ops, SparseCore 0:
  10.1 73.3 all-gather.6
  108.0 80.2 all-gather.4

commit v2 on v1

--- a/solution.py
+++ b/solution.py
@@ -32,7 +32,7 @@
     return jax.ShapeDtypeStruct(shape, dtype)
 
 
-def call(body, outs, specs, scratch=(), mib=40, flops=1 << 26, data=1 << 22, name=None, **extra):
+def call(body, outs, specs, scratch=(), mib=60, flops=1 << 26, data=1 << 22, name=None, **extra):
     return pl.pallas_call(
         body,
         out_shape=outs,
@@ -56,9 +56,8 @@
     unit, _ = normalize(feat_ref[...].astype(f32))
     rows = unit.astype(bf16)
     norm_ref[...] = rows
-    keys = dot(rows, wk_ref[...]).astype(bf16)
-    values = dot(rows, wv_ref[...]).astype(bf16)
-    both = jnp.concatenate([keys, values], axis=1)
+    weight = jnp.concatenate([wk_ref[...], wv_ref[...]], axis=0)
+    both = dot(rows, weight, NT).astype(bf16)
     per = both.shape[0] // B
     for i in range(per):
         kv_ref[step * per + i] = both[i * B : (i + 1) * B]
@@ -83,15 +82,15 @@
         in_specs=[
             SMEM,
             pl.BlockSpec((rows // steps, C), lambda i: (i, 0)),
-            pl.BlockSpec((C, D), lambda i: (0, 0)),
-            pl.BlockSpec((C, D), lambda i: (0, 0)),
+            pl.BlockSpec((D, C), lambda i: (0, 0)),
+            pl.BlockSpec((D, C), lambda i: (0, 0)),
         ],
         out_specs=(
             pl.BlockSpec((rows // steps, C), lambda i: (i, 0)),
             pl.BlockSpec((rows // B, B, 2 * D), lambda i: (0, 0, 0)),
             pl.BlockSpec((shards, B, 2 * D), lambda i: (0, 0, 0)),
         ),
-        compiler_params=pltpu.CompilerParams(vmem_limit_bytes=40 << 20),
+        compiler_params=pltpu.CompilerParams(vmem_limit_bytes=60 << 20),
         cost_estimate=pl.CostEstimate(
             flops=1 << 28, bytes_accessed=6 << 20, transcendentals=0
         ),
@@ -102,8 +101,8 @@
 def query_kernel(mesh_ref, wq_ref, out_ref):
     for b in range(out_ref.shape[0]):
         unit, _ = normalize(mesh_ref[b * B : (b + 1) * B].astype(f32))
-        rows = dot(unit.astype(bf16), wq_ref[...]).astype(bf16).astype(f32) * score_scale
-        out_ref[b] = rows.T.astype(bf16)
+        rows = dot(wq_ref[...], unit.astype(bf16), NT).astype(bf16).astype(f32) * score_scale
+        out_ref[b] = rows.astype(bf16)
 
 
 def fill_pool(pool_ref, own_ref, arrived_ref):
@@ -158,11 +157,12 @@
 
 
 def middle_kernel(
-    heads_ref, gathered_ref, mesh_ref, wq_ref, wk_ref, wv_ref, wl_ref,
+    bias_ref, heads_ref, gathered_ref, mesh_ref, wq_ref, wk_ref, wv_ref, wl_ref,
     pack_ref, enc_ref, unit_ref, inv_ref,
 ):
     parts = heads_ref.shape[0]
     w_out = gathered_ref[:, 0:D, :].reshape(parts * D, C)
+    w_layer = jnp.concatenate([wk_ref[...], wv_ref[...], wq_ref[...]], axis=0)
     half = parts // 2
     queries, grads = [], []
     for b in range(2):
@@ -174,14 +174,23 @@
         unit = unit.astype(bf16)
         unit_ref[rows] = unit
         inv_ref[rows] = jnp.broadcast_to(inverse, (B, 128))
-        queries.append((dot(unit, wq_ref[...]).astype(bf16).astype(f32) * score_scale).astype(bf16))
-        keys = dot(unit, wk_ref[...]).astype(bf16)
-        values = dot(unit, wv_ref[...]).astype(bf16)
-        pack_ref[rows] = jnp.concatenate([keys, values], axis=1)
-        cot = gathered_ref[half * b : half * (b + 1), D:, :].reshape(B, C)
+        both = dot(unit, w_layer, NT).astype(bf16)
+        pack_ref[rows] = both[:, : 2 * D]
+        queries.append((both[:, 2 * D :].astype(f32) * score_scale).astype(bf16))
+        cot = gathered_ref[half * b : half * (b + 1), 2 * D :, :].reshape(B, C)
         grads.append(dot(cot, wl_ref[...], NT).astype(bf16))
     pack_ref[2 * B : 3 * B] = jnp.concatenate(queries, axis=1)
     pack_ref[3 * B : 4 * B] = jnp.concatenate(grads, axis=1)
+    row = lax.broadcasted_iota(jnp.int32, (8, 128), 0)
+    table = jnp.zeros((8, 128), f32)
+    for b in range(2):
+        for n in range(3):
+            table = jnp.where(row == 3 * b + n, bias_ref[b, n], table)
+    high = table.astype(bf16).astype(f32)
+    rest = table - high
+    middle = rest.astype(bf16).astype(f32)
+    tail = [high, middle, rest - middle, jnp.zeros((8, 128), f32)]
+    pack_ref[4 * B : 4 * B + 32] = jnp.concatenate(tail, axis=0).astype(bf16)
 
 
 def side_kernel(gathered_ref, unit_ref, inv_ref, wo_ref, cot_ref, unit_out_ref, inv_out_ref, sum_ref):
@@ -189,7 +198,7 @@
     weight = wo_ref[...]
     for b in range(2):
         rows = slice(b * B, (b + 1) * B)
-        cot = gathered_ref[half * b : half * (b + 1), D:, :].reshape(B, C)
+        cot = gathered_ref[half * b : half * (b + 1), 2 * D :, :].reshape(B, C)
         cot_ref[b] = dot(weight, cot, NT)
         unit_out_ref[b] = dot(weight, unit_ref[rows], NT)
         inv_out_ref[b] = inv_ref[rows].T[0:8]
@@ -199,8 +208,7 @@
 
 
 def layer_kernel(
-    bias_ref, left_bias_ref, right_bias_ref, own_ref, left_ref, right_ref, unit_ref,
-    wq_ref, wk_ref, wv_ref, gathered_ref, send_ref, heads_ref,
+    own_ref, left_ref, right_ref, unit_ref, wq_ref, wk_ref, wv_ref, gathered_ref, send_ref
 ):
     zero = jnp.zeros((B, D), bf16)
 
@@ -215,16 +223,22 @@
             [jnp.concatenate([query, zero], axis=1), jnp.concatenate([zero, grad], axis=1)], axis=0
         )
 
+    def table(ref):
+        tail = ref[4 * B : 4 * B + 32].astype(f32)
+        return tail[0:8] + tail[8:16] + tail[16:24]
+
     kv = [block(ref, b) for ref in (left_ref, own_ref, right_ref) for b in range(2)]
-    queries = [(left_ref, 1, left_bias_ref), (own_ref, 0, bias_ref), (own_ref, 1, bias_ref)]
-    queries.append((right_ref, 0, right_bias_ref))
+    own_bias = table(own_ref)
+    queries = [(left_ref, 1, table(left_ref)), (own_ref, 0, own_bias), (own_ref, 1, own_bias)]
+    queries.append((right_ref, 0, table(right_ref)))
+    heads = []
     grad_kv = [jnp.zeros((B, 2 * D), f32), jnp.zeros((B, 2 * D), f32)]
     grad_q = []
-    for j, (ref, b, table) in enumerate(queries):
+    for j, (ref, b, bias) in enumerate(queries):
         pair = stacked(ref, b)
         window = kv[j : j + 3]
         both = [dot(rows, pair, NT) for rows in window]
-        scores = [both[n][:, :B] + table[b, n] for n in range(3)]
+        scores = [both[n][:, :B] + bias[3 * b + n : 3 * b + n + 1] for n in range(3)]
         top = folded(jnp.maximum, jnp.concatenate(scores, axis=0))
         top = jnp.max(top, axis=0, keepdims=True)
         raised = [jnp.exp(s - top) for s in scores]
@@ -246,29 +260,34 @@
         if 1 <= j <= 2:
             back = sum(dot(mixed[n], window[n], TN) for n in range(3))
             grad_q.append((back[:B, :D] * score_scale).astype(bf16))
-            heads_ref[b * B : (b + 1) * B] = back[B:, D:].astype(bf16)
+            heads.append(back[B:, D:].astype(bf16))
     parts = gathered_ref.shape[0]
-    totals, stats = [], []
+    w_layer = jnp.concatenate([wk_ref[...], wv_ref[...], wq_ref[...]], axis=0)
+    totals, stats = [], jnp.zeros((8, 128), f32)
     lane = lax.broadcasted_iota(jnp.int32, (B, 128), 1)
     for b in range(2):
-        grad = grad_kv[b].astype(bf16)
-        total = (
-            dot(grad_q[b], wq_ref[...], NT)
-            + dot(grad[:, :D], wk_ref[...], NT)
-            + dot(grad[:, D:], wv_ref[...], NT)
-        )
+        grad = jnp.concatenate([grad_kv[b].astype(bf16), grad_q[b]], axis=1)
+        total = dot(grad, w_layer)
         first = jnp.mean(total, axis=1, keepdims=True)
         second = jnp.mean(total * unit_ref[b * B : (b + 1) * B].astype(f32), axis=1, keepdims=True)
-        table = jnp.where(lane == 0, first, jnp.where(lane == 1, second, 0.0)).T[0:8]
-        high = table.astype(bf16).astype(f32)
-        stats.append(jnp.concatenate([high, table - high], axis=0).astype(bf16))
+        first_high = first.astype(bf16).astype(f32)
+        second_high = second.astype(bf16).astype(f32)
+        columns = (first_high, second_high, first - first_high, second - second_high)
+        table_b = jnp.zeros((B, 128), f32)
+        for k, column in enumerate(columns):
+            table_b = jnp.where(lane == 4 * b + k, column, table_b)
+        stats = stats + table_b.T[0:8]
         totals.append(total.astype(bf16))
+    stats = jnp.concatenate([stats[:, :D], stats[:, D:]], axis=0).astype(bf16)
     total = jnp.concatenate(totals, axis=0)
+    heads = jnp.concatenate(heads, axis=0)
+    share = heads.shape[0] // parts
     for z in range(parts):
         piece = dot(gathered_ref[z, 0:D, :], total, NT).astype(bf16)
         for b in range(2):
-            send_ref[z, b, 0:D] = piece[:, b * B : (b + 1) * B]
-            send_ref[z, b, D : D + 16] = stats[b]
+            send_ref[z, b * D : (b + 1) * D] = piece[:, b * B : (b + 1) * B]
+        rows = heads[z * share : (z + 1) * share]
+        send_ref[z, 2 * D :] = jnp.concatenate([rows, stats], axis=1)
 
 
 def back_kernel(
@@ -278,12 +297,15 @@
 ):
     fill_pool(pool_ref, own_ref, arrived_ref)
     zero = jnp.zeros((D, B), bf16)
+    total = arrived_grad_ref[0].astype(f32)
+    for z in range(1, arrived_grad_ref.shape[0]):
+        total = total + arrived_grad_ref[z].astype(f32)
+    stats = total[2 * D :, D:]
+    stats = jnp.concatenate([stats[0:8], stats[8:16]], axis=1)
     for b in range(2):
-        total = arrived_grad_ref[0, b].astype(f32)
-        for z in range(1, arrived_grad_ref.shape[0]):
-            total = total + arrived_grad_ref[z, b].astype(f32)
-        stats = total[D : D + 8] + total[D + 8 : D + 16]
-        inside = total[:D] - stats[0:1] * sum_ref[...] - stats[1:2] * unit_ref[b]
+        first = stats[4 * b : 4 * b + 1] + stats[4 * b + 2 : 4 * b + 3]
+        second = stats[4 * b + 1 : 4 * b + 2] + stats[4 * b + 3 : 4 * b + 4]
+        inside = total[b * D : (b + 1) * D] - first * sum_ref[...] - second * unit_ref[b]
         grad = (cot_ref[b] + inv_ref[b][0:1] * inside).astype(bf16)
         inner = jnp.sum(grad.astype(f32) * wide_ref[b], axis=0, keepdims=True)
         inner_ref[b] = jnp.broadcast_to(inner, (8, B))
@@ -342,7 +364,7 @@
     height = out_ref.shape[0]
     total = enc_ref[pl.ds(pl.multiple_of(at_ref[0] * height, height), height), :]
     for h in range(heads_ref.shape[0]):
-        total = total + dot(heads_ref[h], weight_ref[h * D : (h + 1) * D])
+        total = total + dot(heads_ref[h, 2 * D :][:, :D], weight_ref[h, D : 2 * D])
     out_ref[...] = total.astype(bf16)
 
 
@@ -389,14 +411,18 @@
     backward = [(t, s) for s, t in forward]
 
     gathered = lax.all_gather(
-        jnp.concatenate([enc_out_weight, cotangent], axis=0), "head", axis=0, tiled=False
-    )
-    layer_out_all = lax.all_gather(layer_out_weight, "head", axis=0, tiled=True)
+        jnp.concatenate([enc_out_weight, layer_out_weight, cotangent], axis=0),
+        "head",
+        axis=0,
+        tiled=False,
+    )
+    query_weight, key_weight, value_weight, layer_query, layer_key, layer_value = (
+        weight.T
+        for weight in (query_weight, key_weight, value_weight, layer_query, layer_key, layer_value)
+    )
 
     grid_norm, own_kv, outgoing = grid_part(send, grid_feat, key_weight, value_weight, shards)
     arrived_kv = exchange(outgoing, "grid")
-    left_bias = lax.ppermute(layer_table, "grid", forward)
-    right_bias = lax.ppermute(layer_table, "grid", backward)
     queries = call(
         query_kernel, struct((2, D, B), bf16), [VMEM] * 2, name="query_part", data=1 << 20
     )(mesh_feat, query_weight)
@@ -411,15 +437,15 @@
     pack, encoded, unit, inverse = call(
         middle_kernel,
         (
-            struct((4 * B, 2 * D), bf16),
+            struct((4 * B + 32, 2 * D), bf16),
             struct((2 * B, C), f32),
             struct((2 * B, C), bf16),
             struct((2 * B, 128), f32),
         ),
-        [VMEM] * 7,
+        [SMEM] + [VMEM] * 7,
         name="middle_part",
     )(
-        all_heads, gathered, mesh_feat, layer_query, layer_key, layer_value, layer_out_weight
+        layer_table, all_heads, gathered, mesh_feat, layer_query, layer_key, layer_value, layer_out_weight
     )
     left = lax.ppermute(pack, "grid", forward)
     right = lax.ppermute(pack, "grid", backward)
@@ -434,15 +460,9 @@
         [VMEM] * 4,
         name="side_part",
     )(gathered, unit, inverse, enc_out_weight)
-    mixed, layer_heads = call(
-        layer_kernel,
-        (struct((parts, 2, D + 16, B), bf16), struct((2 * B, D), bf16)),
-        [SMEM] * 3 + [VMEM] * 8,
-        name="layer_part",
-    )(
-        layer_table, left_bias, right_bias, pack, left, right, unit,
-        layer_query, layer_key, layer_value, gathered,
-    )
+    mixed = call(
+        layer_kernel, struct((parts, 2 * D + share, B), bf16), [VMEM] * 8, name="layer_part"
+    )(pack, left, right, unit, layer_query, layer_key, layer_value, gathered)
     arrived_grad = exchange(mixed, "head")
     own_grad, send_grad = call(
         back_kernel,
@@ -460,7 +480,6 @@
         inverse_row, weight_sum, wide_heads, lse, queries, own_kv, arrived_kv,
     )
     back_grad = exchange(send_grad, "grid")
-    row_heads = exchange(layer_heads.reshape(parts, share, D), "head")
     product = call(
         final_kernel,
         struct((shards, C // shards, 2 * D), bf16),
@@ -474,7 +493,7 @@
         struct((share, C), bf16),
         [SMEM] + [VMEM] * 3,
         name="output_part",
-    )(head_at, row_heads, layer_out_all, encoded)
+    )(head_at, arrived_grad, gathered, encoded)
     key_grad, value_grad = call(
         sum_kernel,
         (struct((C // shards, D), f32), struct((C // shards, D), f32)),

time: 254 us -> 217 us (0.85)
  blocking collectives: 35.3 us -> 71 us
  local copies, waits for them, and re-layouts: 35.5 us -> 3.23 us
  waiting for transfers between devices: 75 us -> 45.1 us
  starting transfers between devices: 62.2 us -> 32.8 us
  Pallas kernels: 28.7 us -> 48.1 us
    all_to_all x5 -> x3, waiting for transfers between devices: 74.1 us -> 39.1 us  [exchange(): return lax.all_to_all(array, axis, split_axis=0, concat_axis=0, tiled=True)]
    all_to_all x0 -> x1, blocking collectives: none -> 33 us  [exchange(): return lax.all_to_all(array, axis, split_axis=0, concat_axis=0, tiled=True)]
    unnamed x106 -> x10, local copies, waits for them, and re-layouts: 35.5 us -> 3.23 us
    all_to_all x5 -> x3, starting transfers between devices: 42.8 us -> 21.3 us  [exchange(): return lax.all_to_all(array, axis, split_axis=0, concat_axis=0, tiled=True)]
    ppermute x2 -> x0, starting transfers between devices: 8.88 us -> none  [the longest x1 6.04 us: on_device(): right_bias = lax.ppermute(layer_table, 'grid', backward)]
    ppermute x1, starting transfers between devices: 2.72 us -> 8.58 us  [on_device(): right = lax.ppermute(pack, 'grid', backward)]
    pallas_call x2, Pallas kernels: 7.7 us -> 12.8 us  [the longest x1 7.63 us: on_device(): call(layer_kernel, struct((parts, 2 * D + share, B), bf16), [VMEM] * 8, n...]
    ppermute x1, starting transfers between devices: 7.65 us -> 2.96 us  [on_device(): left = lax.ppermute(pack, 'grid', forward)]
  transfers between devices with their start and end apart: 11 -> 6, of which waited for: 6 -> 6; matrix products, arithmetic and copies ran while one was open for 2% -> 0% of each run, Pallas kernels for 10% -> 10%
where the time goes in v2:
time: 217 us; the launch traced here: 216 us
  blocking collectives  71 us (33%)
  Pallas kernels  48.1 us (22%)
  waiting for transfers between devices  45.1 us (21%)
  starting transfers between devices  32.8 us (15%)
  between operations  14.1 us (6%)
  local copies, waits for them, and re-layouts  3.23 us (1%)
    all_to_all x3, waiting for transfers between devices, exchange(): return lax.all_to_all(array, axis, split_axis=0, concat_axis=0, tiled=True)  39.1 us
    all_gather x1, blocking collectives, on_device(): all_heads = lax.all_gather(enc_heads, 'head', axis=0, tiled=False)  38 us
    all_to_all x1, blocking collectives, exchange(): return lax.all_to_all(array, axis, split_axis=0, concat_axis=0, tiled=True)  33 us
    all_to_all x3, starting transfers between devices, exchange(): return lax.all_to_all(array, axis, split_axis=0, concat_axis=0, tiled=True)  21.3 us
    ppermute x1, starting transfers between devices, on_device(): right = lax.ppermute(pack, 'grid', backward)  8.58 us
    pallas_call x1, Pallas kernels, on_device(): call(back_kernel, (struct((own, B, 2 * D), f32), struct((shards, B, 2 * D...  7.72 us
    pallas_call x1, Pallas kernels, on_device(): call(layer_kernel, struct((parts, 2 * D + share, B), bf16), [VMEM] * 8, n...  7.63 us
    pallas_call x1, Pallas kernels, on_device(): call(encoder_kernel, (struct((2, D, B), f32), struct((2, D, B), bf16), st...  6.96 us
  transfers between devices with their start and end apart: 6, of which 6 were waited for; matrix products, arithmetic and copies ran while one was open for 0% of the time, Pallas kernels for 10%

profile of v2, /device:TPU:1, one launch (start us, length us, event | category | flops | bytes accessed | tf_op | source)
XLA Modules:
  0.0 216.0 jit_solution(9548191546566085471)
XLA Ops:
  7.2 1.7 pad_maximum_fusion
  9.0 5.5 %grid_part.1 = (bf16[1024,1024]{1,0:T(8,128)(2,1)}, bf16[8,128,128]{2,1,0:T(8,128)(2,1)}, bf16[32,128,128]{2,1,0:T(8,128)(2,1)}) custom-call(s32[32]{0:T(128)} %bitcast.29, bf16[1024,1024]{1,0:T(8,128)(2,1)} %feat_ref.1, bf16[64,1024]{1,0:T(8,128)(2,1)} %bitcast.24, bf16[64,1024]{1,0:T(8,128)(2,1)} %bitcast.25), custom_call_target="tpu_custom_call" | custom-call | flops 268435456 | bytes 6291456 | tf_op jit(solution)/shard_map/grid_part/pallas_call | solution.py:74
  14.4 10.5 %all-to-all-start = ((bf16[32,128,128]{2,1,0:T(8,128)(2,1)}), bf16[32,128,128]{2,1,0:T(8,128)(2,1)S(1)}, u32[]{:S(2)}, u32[]{:S(2)}) async-start(bf16[32,128,128]{2,1,0:T(8,128)(2,1)} %get-tuple-element.22), calls=%async_computation | async-start | bytes 2097152 | tf_op jit(solution)/shard_map/all_to_all | solution.py:380
  24.9 2.3 %query_part.1.query_ref = bf16[2,64,128]{2,1,0:T(8,128)(2,1)} custom-call(bf16[256,1024]{1,0:T(8,128)(2,1)} %mesh_ref.3, bf16[64,1024]{1,0:T(8,128)(2,1)} %bitcast.26), custom_call_target="tpu_custom_call" | custom-call | flops 67108864 | bytes 1048576 | tf_op jit(solution)/shard_map/query_part/pallas_call | solution.py:426
  27.2 15.0 %all-to-all-done.arrived_ref = bf16[32,128,128]{2,1,0:T(8,128)(2,1)S(1)} async-done(((bf16[32,128,128]{2,1,0:T(8,128)(2,1)}), bf16[32,128,128]{2,1,0:T(8,128)(2,1)S(1)}, u32[]{:S(2)}, u32[]{:S(2)}) %all-to-all-start) | async-done | bytes 1048608 | tf_op jit(solution)/shard_map/all_to_all | solution.py:380
  42.2 1.0 copy-done
  43.2 7.0 %encoder_part.1 = (f32[2,64,128]{2,1,0:T(8,128)}, bf16[2,64,128]{2,1,0:T(8,128)(2,1)}, f32[2,8,128]{2,1,0:T(8,128)}) custom-call(s32[2,30]{1,0:T(2,128)} %slot_ref.3, s32[2]{0:T(128)} %count_ref.3, f32[2,30]{1,0:T(2,128)} %bitcast.27, bf16[8,128,128]{2,1,0:T(8,128)(2,1)} %get-tuple-element.21.own_ref, bf16[32,128,128]{2,1,0:T(8,128)(2,1)} %copy-done, ...), custom_call_target="tpu_custom_call" | custom-call | flops 67108864 | bytes 4194304 | tf_op jit(solution)/shard_map/encoder_part/pallas_call | solution.py:429
  50.2 38.0 %all-gather = bf16[32,64,128]{2,1,0:T(8,128)(2,1)} all-gather(bf16[2,64,128]{2,1,0:T(8,128)(2,1)} %get-tuple-element.23), channel_id=2, replica_groups=mesh['grid'=32,'head'=16] {'head'}, dimensions={0}, use_global_device_ids=true | all-gather | bytes 557056 | tf_op jit(solution)/shard_map/all_gather | solution.py:436
  88.2 3.7 %all-gather.4.cloned.1.call-done = bf16[2304,1024]{1,0:T(8,128)(2,1)} async-done(((bf16[144,1024]{1,0:T(8,128)(2,1)}), bf16[2304,1024]{1,0:T(8,128)(2,1)}) %all-gather.4.cloned.1.call-update) | async-done | bytes 4718608 | tf_op jit(solution)/shard_map/all_gather | solution.py:413
  91.9 5.2 %middle_part.1 = (bf16[544,128]{1,0:T(8,128)(2,1)}, f32[256,1024]{1,0:T(8,128)}, bf16[256,1024]{1,0:T(8,128)(2,1)}, f32[256,128]{1,0:T(8,128)}) custom-call(f32[2,3]{1,0:T(2,128)} %bitcast.31, bf16[16,2,64,128]{3,2,1,0:T(8,128)(2,1)} %bitcast.17, bf16[16,144,1024]{2,1,0:T(8,128)(2,1)} %bitcast.13, bf16[256,1024]{1,0:T(8,128)(2,1)} %mesh_ref.3, ...), custom_call_target="tpu_custom_call" | custom-call | flops 67108864 | bytes 4194304 | tf_op jit(solution)/shard_map/middle_part/pallas_call | solution.py:437
  97.1 8.6 %collective-permute-start.1 = (bf16[544,128]{1,0:T(8,128)(2,1)}, bf16[544,128]{1,0:T(8,128)(2,1)S(1)}, u32[]{:S(2)}, u32[]{:S(2)}) collective-permute-start(bf16[544,128]{1,0:T(8,128)(2,1)} %get-tuple-element.24.own_ref), channel_id=1, source_target_pairs={{16,0},{32,16},{48,32},{64,48},{80,64},{96,80},{112,96},{128,112},... | collective-permute-start | bytes 417800 | tf_op jit(solution)/shard_map/ppermute | solution.py:451
  105.7 3.0 %collective-permute-start = (bf16[544,128]{1,0:T(8,128)(2,1)}, bf16[544,128]{1,0:T(8,128)(2,1)S(1)}, u32[]{:S(2)}, u32[]{:S(2)}) collective-permute-start(bf16[544,128]{1,0:T(8,128)(2,1)} %get-tuple-element.24.own_ref), channel_id=1, source_target_pairs={{0,16},{16,32},{32,48},{48,64},{64,80},{80,96},{96,112},{112,128},... | collective-permute-start | bytes 417800 | tf_op jit(solution)/shard_map/ppermute | solution.py:450
  109.7 1.3 collective-permute-done.left_ref
  111.6 7.6 %layer_part.1 = bf16[16,144,128]{2,1,0:T(8,128)(2,1)} custom-call(bf16[544,128]{1,0:T(8,128)(2,1)} %get-tuple-element.24.own_ref, bf16[544,128]{1,0:T(8,128)(2,1)} %copy-done.4, bf16[544,128]{1,0:T(8,128)(2,1)} %copy-done.3, bf16[256,1024]{1,0:T(8,128)(2,1)} %get-tuple-element.25.unit_ref, bf16[64,1024]{1,0:T(8,128)(2,1)} %bitcast.19, ...), custom_call_target="tpu_custom_call" | custom-call | flops 67108864 | bytes 4194304 | tf_op jit(solution)/shard_map/layer_part/pallas_call | solution.py:463
  119.3 6.9 %all-to-all-start.1 = ((bf16[16,144,128]{2,1,0:T(8,128)(2,1)}), bf16[16,144,128]{2,1,0:T(8,128)(2,1)S(1)}, u32[]{:S(2)}, u32[]{:S(2)}) async-start(bf16[16,144,128]{2,1,0:T(8,128)(2,1)} %layer_part.1), calls=%async_computation.1 | async-start | bytes 1179648 | tf_op jit(solution)/shard_map/all_to_all | solution.py:380
  126.2 3.6 %side_part.1 = (f32[2,64,128]{2,1,0:T(8,128)}, f32[2,64,128]{2,1,0:T(8,128)}, f32[2,8,128]{2,1,0:T(8,128)}, f32[64,128]{1,0:T(8,128)}) custom-call(bf16[16,144,1024]{2,1,0:T(8,128)(2,1)} %bitcast.15, bf16[256,1024]{1,0:T(8,128)(2,1)} %get-tuple-element.25.unit_ref, f32[256,128]{1,0:T(8,128)} %get-tuple-element.28.inv_ref, bf16[64,1024]{1,0:T(8,128)(2,1)} %wo_ref.1), custom_call_target="tpu_custom_call" | custom-call | flops 67108864 | bytes 4194304 | tf_op jit(solution)/shard_map/side_part/pallas_call | solution.py:452
  129.8 18.9 %all-to-all-done.1.heads_ref.arrived_grad_ref = bf16[16,144,128]{2,1,0:T(8,128)(2,1)S(1)} async-done(((bf16[16,144,128]{2,1,0:T(8,128)(2,1)}), bf16[16,144,128]{2,1,0:T(8,128)(2,1)S(1)}, u32[]{:S(2)}, u32[]{:S(2)}) %all-to-all-start.1) | async-done | bytes 589856 | tf_op jit(solution)/shard_map/all_to_all | solution.py:380
  149.5 7.7 %back_part.1 = (f32[8,128,128]{2,1,0:T(8,128)}, bf16[32,128,128]{2,1,0:T(8,128)(2,1)}) custom-call(s32[2,30]{1,0:T(2,128)} %slot_ref.3, s32[2]{0:T(128)} %count_ref.3, f32[2,30]{1,0:T(2,128)} %bitcast.28, s32[1]{0:T(128)} %bitcast.12.me_ref, bf16[16,144,128]{2,1,0:T(8,128)(2,1)} %copy-done.1, f32[2,64,128]{2,1,0:T(8,128)} %get-tuple-element.29.cot_ref, ...), custom_call_target="tpu_custom_call" | custom-call | flops 67108864 | bytes 4194304 | tf_op jit(solution)/shard_map/back_part/pallas_call | solution.py:467
  157.2 33.0 %all_to_all.20.back_ref = bf16[32,128,128]{2,1,0:T(8,128)(2,1)} all-to-all(bf16[32,128,128]{2,1,0:T(8,128)(2,1)} %get-tuple-element.36), channel_id=1, replica_groups=mesh['grid'=32,'head'=16] {'grid'}, dimensions={0} | all-to-all | bytes 2097152 | tf_op jit(solution)/shard_map/all_to_all | solution.py:380
  190.3 3.6 %final_part.1 = bf16[32,32,128]{2,1,0:T(8,128)(2,1)} custom-call(s32[32]{0:T(128)} %bitcast.30, bf16[1024,1024]{1,0:T(8,128)(2,1)} %get-tuple-element.27.norm_ref, f32[8,128,128]{2,1,0:T(8,128)} %get-tuple-element.35.own_ref, bf16[32,128,128]{2,1,0:T(8,128)(2,1)} %all_to_all.20.back_ref), custom_call_target="tpu_custom_call" | custom-call | flops 67108864 | bytes 4194304 | tf_op jit(solution)/shard_map/final_part/pallas_call | solution.py:483
  193.9 3.9 %all-to-all-start.3 = ((bf16[32,32,128]{2,1,0:T(8,128)(2,1)}), bf16[32,32,128]{2,1,0:T(8,128)(2,1)S(1)}, u32[]{:S(2)}, u32[]{:S(2)}) async-start(bf16[32,32,128]{2,1,0:T(8,128)(2,1)} %final_part.1), calls=%async_computation.3 | async-start | bytes 524288 | tf_op jit(solution)/shard_map/all_to_all | solution.py:380
  197.8 3.8 %output_part.1 = bf16[16,1024]{1,0:T(8,128)(2,1)} custom-call(s32[1]{0:T(128)} %bitcast.at_ref, bf16[16,144,128]{2,1,0:T(8,128)(2,1)} %copy-done.1, bf16[16,144,1024]{2,1,0:T(8,128)(2,1)} %bitcast.16, f32[256,1024]{1,0:T(8,128)} %get-tuple-element.26.enc_ref), custom_call_target="tpu_custom_call" | custom-call | flops 67108864 | bytes 4194304 | tf_op jit(solution)/shard_map/output_part/pallas_call | solution.py:491
  201.6 5.2 %all-to-all-done.3.parts_ref = bf16[32,32,128]{2,1,0:T(8,128)(2,1)S(1)} async-done(((bf16[32,32,128]{2,1,0:T(8,128)(2,1)}), bf16[32,32,128]{2,1,0:T(8,128)(2,1)S(1)}, u32[]{:S(2)}, u32[]{:S(2)}) %all-to-all-start.3) | async-done | bytes 262176 | tf_op jit(solution)/shard_map/all_to_all | solution.py:380
  207.5 1.7 sum_part.1
  (12 shorter events, 3.3 us)
Async XLA Ops:
  7.2 84.7 %all-gather.4.cloned.1.call-start = ((), (), s32[]{:S(2)}) async-start(), calls=%async_computation.4 | async-start | bytes 5013504 | tf_op jit(solution)/shard_map/all_gather | solution.py:413
  14.4 27.8 %all-to-all-start = ((bf16[32,128,128]{2,1,0:T(8,128)(2,1)}), bf16[32,128,128]{2,1,0:T(8,128)(2,1)S(1)}, u32[]{:S(2)}, u32[]{:S(2)}) async-start(bf16[32,128,128]{2,1,0:T(8,128)(2,1)} %get-tuple-element.22), calls=%async_computation | async-start | bytes 2097152 | tf_op jit(solution)/shard_map/all_to_all | solution.py:380
  42.2 1.0 copy-start
  97.1 12.6 %collective-permute-start.1 = (bf16[544,128]{1,0:T(8,128)(2,1)}, bf16[544,128]{1,0:T(8,128)(2,1)S(1)}, u32[]{:S(2)}, u32[]{:S(2)}) collective-permute-start(bf16[544,128]{1,0:T(8,128)(2,1)} %get-tuple-element.24.own_ref), channel_id=1, source_target_pairs={{16,0},{32,16},{48,32},{64,48},{80,64},{96,80},{112,96},{128,112},... | collective-permute-start | bytes 417800 | tf_op jit(solution)/shard_map/ppermute | solution.py:451
  105.7 5.3 %collective-permute-start = (bf16[544,128]{1,0:T(8,128)(2,1)}, bf16[544,128]{1,0:T(8,128)(2,1)S(1)}, u32[]{:S(2)}, u32[]{:S(2)}) collective-permute-start(bf16[544,128]{1,0:T(8,128)(2,1)} %get-tuple-element.24.own_ref), channel_id=1, source_target_pairs={{0,16},{16,32},{32,48},{48,64},{64,80},{80,96},{96,112},{112,128},... | collective-permute-start | bytes 417800 | tf_op jit(solution)/shard_map/ppermute | solution.py:450
  109.7 1.3 copy-start.3
  111.0 0.7 copy-start.4
  119.3 29.4 %all-to-all-start.1 = ((bf16[16,144,128]{2,1,0:T(8,128)(2,1)}), bf16[16,144,128]{2,1,0:T(8,128)(2,1)S(1)}, u32[]{:S(2)}, u32[]{:S(2)}) async-start(bf16[16,144,128]{2,1,0:T(8,128)(2,1)} %layer_part.1), calls=%async_computation.1 | async-start | bytes 1179648 | tf_op jit(solution)/shard_map/all_to_all | solution.py:380
  148.7 0.8 copy-start.1
  193.9 12.9 %all-to-all-start.3 = ((bf16[32,32,128]{2,1,0:T(8,128)(2,1)}), bf16[32,32,128]{2,1,0:T(8,128)(2,1)S(1)}, u32[]{:S(2)}, u32[]{:S(2)}) async-start(bf16[32,32,128]{2,1,0:T(8,128)(2,1)} %final_part.1), calls=%async_computation.3 | async-start | bytes 524288 | tf_op jit(solution)/shard_map/all_to_all | solution.py:380
  206.8 0.7 copy-start.2
Sparse Core Ops, SparseCore 0:
  10.1 81.7 all-gather.3

commit v3 on v2

--- a/solution.py
+++ b/solution.py
@@ -32,7 +32,7 @@
     return jax.ShapeDtypeStruct(shape, dtype)
 
 
-def call(body, outs, specs, scratch=(), mib=60, flops=1 << 26, data=1 << 22, name=None, **extra):
+def call(body, outs, specs, scratch=(), mib=16, flops=1 << 26, data=1 << 22, name=None, **extra):
     return pl.pallas_call(
         body,
         out_shape=outs,
@@ -157,13 +157,15 @@
 
 
 def middle_kernel(
-    bias_ref, heads_ref, gathered_ref, mesh_ref, wq_ref, wk_ref, wv_ref, wl_ref,
-    pack_ref, enc_ref, unit_ref, inv_ref,
+    at_ref, bias_ref, heads_ref, gathered_ref, mesh_ref, wq_ref, wk_ref, wv_ref, wl_ref,
+    pack_ref, tail_ref, unit_ref, enc_ref,
 ):
     parts = heads_ref.shape[0]
     w_out = gathered_ref[:, 0:D, :].reshape(parts * D, C)
     w_layer = jnp.concatenate([wk_ref[...], wv_ref[...], wq_ref[...]], axis=0)
     half = parts // 2
+    height = 2 * B // parts
+    tail_ref[height:] = jnp.zeros((8, C), f32)
     queries, grads = [], []
     for b in range(2):
         rows = slice(b * B, (b + 1) * B)
@@ -173,12 +175,13 @@
         unit, inverse = normalize(enc)
         unit = unit.astype(bf16)
         unit_ref[rows] = unit
-        inv_ref[rows] = jnp.broadcast_to(inverse, (B, 128))
+        tail_ref[height:, b * B : (b + 1) * B] = jnp.broadcast_to(inverse, (B, 128)).T[0:8]
         both = dot(unit, w_layer, NT).astype(bf16)
         pack_ref[rows] = both[:, : 2 * D]
         queries.append((both[:, 2 * D :].astype(f32) * score_scale).astype(bf16))
         cot = gathered_ref[half * b : half * (b + 1), 2 * D :, :].reshape(B, C)
         grads.append(dot(cot, wl_ref[...], NT).astype(bf16))
+    tail_ref[:height] = enc_ref[pl.ds(pl.multiple_of(at_ref[0] * height, height), height), :]
     pack_ref[2 * B : 3 * B] = jnp.concatenate(queries, axis=1)
     pack_ref[3 * B : 4 * B] = jnp.concatenate(grads, axis=1)
     row = lax.broadcasted_iota(jnp.int32, (8, 128), 0)
@@ -193,7 +196,7 @@
     pack_ref[4 * B : 4 * B + 32] = jnp.concatenate(tail, axis=0).astype(bf16)
 
 
-def side_kernel(gathered_ref, unit_ref, inv_ref, wo_ref, cot_ref, unit_out_ref, inv_out_ref, sum_ref):
+def side_kernel(gathered_ref, unit_ref, tail_ref, wo_ref, cot_ref, unit_out_ref, inv_out_ref, sum_ref):
     half = gathered_ref.shape[0] // 2
     weight = wo_ref[...]
     for b in range(2):
@@ -201,7 +204,7 @@
         cot = gathered_ref[half * b : half * (b + 1), 2 * D :, :].reshape(B, C)
         cot_ref[b] = dot(weight, cot, NT)
         unit_out_ref[b] = dot(weight, unit_ref[rows], NT)
-        inv_out_ref[b] = inv_ref[rows].T[0:8]
+        inv_out_ref[b] = tail_ref[tail_ref.shape[0] - 8 :, b * B : (b + 1) * B]
     sum_ref[...] = jnp.broadcast_to(
         jnp.sum(weight.astype(f32), axis=1, keepdims=True), sum_ref.shape
     )
@@ -360,9 +363,8 @@
         out_ref[c * per : (c + 1) * per] = part.astype(bf16).reshape(per, height, 2 * D)
 
 
-def output_kernel(at_ref, heads_ref, weight_ref, enc_ref, out_ref):
-    height = out_ref.shape[0]
-    total = enc_ref[pl.ds(pl.multiple_of(at_ref[0] * height, height), height), :]
+def output_kernel(heads_ref, weight_ref, tail_ref, out_ref):
+    total = tail_ref[: out_ref.shape[0]]
     for h in range(heads_ref.shape[0]):
         total = total + dot(heads_ref[h, 2 * D :][:, :D], weight_ref[h, D : 2 * D])
     out_ref[...] = total.astype(bf16)
@@ -434,18 +436,18 @@
         name="encoder_part",
     )(edge_slot, edge_count, enc_table, own_kv, arrived_kv, queries)
     all_heads = lax.all_gather(enc_heads, "head", axis=0, tiled=False)
-    pack, encoded, unit, inverse = call(
+    pack, tail, unit = call(
         middle_kernel,
         (
             struct((4 * B + 32, 2 * D), bf16),
-            struct((2 * B, C), f32),
+            struct((share + 8, C), f32),
             struct((2 * B, C), bf16),
-            struct((2 * B, 128), f32),
         ),
-        [SMEM] + [VMEM] * 7,
+        [SMEM] * 2 + [VMEM] * 7,
+        [pltpu.VMEM((2 * B, C), f32)],
         name="middle_part",
     )(
-        layer_table, all_heads, gathered, mesh_feat, layer_query, layer_key, layer_value, layer_out_weight
+        head_at, layer_table, all_heads, gathered, mesh_feat, layer_query, layer_key, layer_value, layer_out_weight
     )
     left = lax.ppermute(pack, "grid", forward)
     right = lax.ppermute(pack, "grid", backward)
@@ -459,7 +461,7 @@
         ),
         [VMEM] * 4,
         name="side_part",
-    )(gathered, unit, inverse, enc_out_weight)
+    )(gathered, unit, tail, enc_out_weight)
     mixed = call(
         layer_kernel, struct((parts, 2 * D + share, B), bf16), [VMEM] * 8, name="layer_part"
     )(pack, left, right, unit, layer_query, layer_key, layer_value, gathered)
@@ -491,9 +493,9 @@
     mesh_out = call(
         output_kernel,
         struct((share, C), bf16),
-        [SMEM] + [VMEM] * 3,
+        [VMEM] * 3,
         name="output_part",
-    )(head_at, arrived_grad, gathered, encoded)
+    )(arrived_grad, gathered, tail)
     key_grad, value_grad = call(
         sum_kernel,
         (struct((C // shards, D), f32), struct((C // shards, D), f32)),

time: 217 us -> 206 us (0.949)
  Pallas kernels: 48.1 us -> 28.8 us
  waiting for transfers between devices: 45.1 us -> 52.8 us
  local copies, waits for them, and re-layouts: 3.23 us -> 8.33 us
  blocking collectives: 71 us -> 67.1 us
    pallas_call x2, Pallas kernels: 9.04 us -> 3.34 us  [the longest x1 2.33 us: on_device(): call(middle_kernel, (struct((4 * B + 32, 2 * D), bf16), struct((share + 8...]
    unnamed x10 -> x44, local copies, waits for them, and re-layouts: 3.23 us -> 8.33 us
    all_gather x1, waiting for transfers between devices: 3.69 us -> 8.77 us  [on_device(): lax.all_gather(jnp.concatenate([enc_out_weight, layer_out_weight, cotange...]
    all_gather x1, blocking collectives: 38 us -> 34.8 us  [on_device(): all_heads = lax.all_gather(enc_heads, 'head', axis=0, tiled=False)]
    pallas_call x1, Pallas kernels: 3.63 us -> 0.47 us  [on_device(): call(side_kernel, (struct((2, D, B), f32), struct((2, D, B), f32), struct...]
    all_to_all x3, waiting for transfers between devices: 39.1 us -> 42 us  [exchange(): return lax.all_to_all(array, axis, split_axis=0, concat_axis=0, tiled=True)]
    pallas_call x1, Pallas kernels: 7.63 us -> 4.87 us  [on_device(): call(layer_kernel, struct((parts, 2 * D + share, B), bf16), [VMEM] * 8, n...]
  transfers between devices with their start and end apart: 6 -> 6, of which waited for: 6 -> 6; matrix products, arithmetic and copies ran while one was open for 0% -> 0% of each run, Pallas kernels for 10% -> 6%
where the time goes in v3:
time: 206 us; the launch traced here: 205 us
  blocking collectives  67.1 us (33%)
  waiting for transfers between devices  52.8 us (26%)
  starting transfers between devices  32.2 us (16%)
  Pallas kernels  28.8 us (14%)
  between operations  14.3 us (7%)
  local copies, waits for them, and re-layouts  8.33 us (4%)
    all_to_all x3, waiting for transfers between devices, exchange(): return lax.all_to_all(array, axis, split_axis=0, concat_axis=0, tiled=True)  42 us
    all_gather x1, blocking collectives, on_device(): all_heads = lax.all_gather(enc_heads, 'head', axis=0, tiled=False)  34.8 us
    all_to_all x1, blocking collectives, exchange(): return lax.all_to_all(array, axis, split_axis=0, concat_axis=0, tiled=True)  32.3 us
    all_to_all x3, starting transfers between devices, exchange(): return lax.all_to_all(array, axis, split_axis=0, concat_axis=0, tiled=True)  20.7 us
    all_gather x1, waiting for transfers between devices, on_device(): lax.all_gather(jnp.concatenate([enc_out_weight, layer_out_weight, cotange...  8.77 us
    ppermute x1, starting transfers between devices, on_device(): right = lax.ppermute(pack, 'grid', backward)  8.47 us
    unnamed x44, local copies, waits for them, and re-layouts  8.33 us
    pallas_call x1, Pallas kernels, on_device(): call(encoder_kernel, (struct((2, D, B), f32), struct((2, D, B), bf16), st...  5.59 us
  transfers between devices with their start and end apart: 6, of which 6 were waited for; matrix products, arithmetic and copies ran while one was open for 0% of the time, Pallas kernels for 6%

profile of v3, /device:TPU:1, one launch (start us, length us, event | category | flops | bytes accessed | tf_op | source)
XLA Modules:
  0.0 205.3 jit_solution(8829376600417381753)
XLA Ops:
  7.2 1.8 pad_maximum_fusion
  9.0 5.6 %grid_part.1 = (bf16[1024,1024]{1,0:T(8,128)(2,1)}, bf16[8,128,128]{2,1,0:T(8,128)(2,1)}, bf16[32,128,128]{2,1,0:T(8,128)(2,1)}) custom-call(s32[32]{0:T(128)} %bitcast.27, bf16[1024,1024]{1,0:T(8,128)(2,1)} %feat_ref.1, bf16[64,1024]{1,0:T(8,128)(2,1)} %bitcast.30, bf16[64,1024]{1,0:T(8,128)(2,1)} %bitcast.31), custom_call_target="tpu_custom_call" | custom-call | flops 268435456 | bytes 6291456 | tf_op jit(solution)/shard_map/grid_part/pallas_call | solution.py:74
  14.7 10.6 %all-to-all-start = ((bf16[32,128,128]{2,1,0:T(8,128)(2,1)}), bf16[32,128,128]{2,1,0:T(8,128)(2,1)S(1)}, u32[]{:S(2)}, u32[]{:S(2)}) async-start(bf16[32,128,128]{2,1,0:T(8,128)(2,1)} %get-tuple-element.21), calls=%async_computation | async-start | bytes 2097152 | tf_op jit(solution)/shard_map/all_to_all | solution.py:382
  25.9 16.7 %all-to-all-done.arrived_ref = bf16[32,128,128]{2,1,0:T(8,128)(2,1)S(1)} async-done(((bf16[32,128,128]{2,1,0:T(8,128)(2,1)}), bf16[32,128,128]{2,1,0:T(8,128)(2,1)S(1)}, u32[]{:S(2)}, u32[]{:S(2)}) %all-to-all-start) | async-done | bytes 1048608 | tf_op jit(solution)/shard_map/all_to_all | solution.py:382
  42.6 5.6 %encoder_part.1 = (f32[2,64,128]{2,1,0:T(8,128)S(1)}, bf16[2,64,128]{2,1,0:T(8,128)(2,1)S(1)}, f32[2,8,128]{2,1,0:T(8,128)S(1)}) custom-call(s32[2,30]{1,0:T(2,128)S(1)} %copy-done.17, s32[2]{0:T(128)S(1)} %copy-done.19, f32[2,30]{1,0:T(2,128)S(1)} %bitcast.25, bf16[8,128,128]{2,1,0:T(8,128)(2,1)S(1)} %copy-done.6, ...), custom_call_target="tpu_custom_call" | custom-call | flops 67108864 | bytes 4194304 | tf_op jit(solution)/shard_map/encoder_part/pallas_call | solution.py:431
  48.8 34.8 %all-gather = bf16[32,64,128]{2,1,0:T(8,128)(2,1)S(1)} all-gather(bf16[2,64,128]{2,1,0:T(8,128)(2,1)S(1)} %get-tuple-element.22), channel_id=2, replica_groups=mesh['grid'=32,'head'=16] {'head'}, dimensions={0}, use_global_device_ids=true | all-gather | bytes 557056 | tf_op jit(solution)/shard_map/all_gather | solution.py:438
  83.6 8.8 %all-gather.4.cloned.1.call-done = bf16[2304,1024]{1,0:T(8,128)(2,1)} async-done(((bf16[144,1024]{1,0:T(8,128)(2,1)}), bf16[2304,1024]{1,0:T(8,128)(2,1)}) %all-gather.4.cloned.1.call-update) | async-done | bytes 4718608 | tf_op jit(solution)/shard_map/all_gather | solution.py:415
  92.4 2.3 %copy-done = bf16[2304,1024]{1,0:T(8,128)(2,1)S(1)} copy-done((bf16[2304,1024]{1,0:T(8,128)(2,1)S(1)}, bf16[2304,1024]{1,0:T(8,128)(2,1)}, u32[]{:S(2)}) %copy-start) | copy-done | bytes 4718616
  94.7 2.3 %middle_part.1 = (bf16[544,128]{1,0:T(8,128)(2,1)S(1)}, f32[24,1024]{1,0:T(8,128)S(1)}, bf16[256,1024]{1,0:T(8,128)(2,1)S(1)}) custom-call(s32[1]{0:T(128)} %bitcast.at_ref, f32[2,3]{1,0:T(2,128)S(1)} %bitcast.29, bf16[16,2,64,128]{3,2,1,0:T(8,128)(2,1)S(1)} %bitcast.17, bf16[16,144,1024]{2,1,0:T(8,128)(2,1)S(1)} %bitcast.13, ...), custom_call_target="tpu_custom_call" | custom-call | flops 67108864 | bytes 4194304 | tf_op jit(solution)/shard_map/middle_part/pallas_call | solution.py:439
  97.7 8.5 %collective-permute-start.1 = (bf16[544,128]{1,0:T(8,128)(2,1)S(1)}, bf16[544,128]{1,0:T(8,128)(2,1)S(1)}, u32[]{:S(2)}, u32[]{:S(2)}) collective-permute-start(bf16[544,128]{1,0:T(8,128)(2,1)S(1)} %get-tuple-element.23.own_ref), channel_id=1, source_target_pairs={{16,0},{32,16},{48,32},{64,48},{80,64},{96,80},{112,96},{128,112},... | collective-permute-start | bytes 417800 | tf_op jit(solution)/shard_map/ppermute | solution.py:453
  106.2 3.0 %collective-permute-start = (bf16[544,128]{1,0:T(8,128)(2,1)S(1)}, bf16[544,128]{1,0:T(8,128)(2,1)S(1)}, u32[]{:S(2)}, u32[]{:S(2)}) collective-permute-start(bf16[544,128]{1,0:T(8,128)(2,1)S(1)} %get-tuple-element.23.own_ref), channel_id=1, source_target_pairs={{0,16},{16,32},{32,48},{48,64},{64,80},{80,96},{96,112},{112,128},... | collective-permute-start | bytes 417800 | tf_op jit(solution)/shard_map/ppermute | solution.py:452
  109.2 0.8 collective-permute-done.1.right_ref
  110.0 1.2 collective-permute-done.left_ref
  111.2 4.9 %layer_part.1 = bf16[16,144,128]{2,1,0:T(8,128)(2,1)} custom-call(bf16[544,128]{1,0:T(8,128)(2,1)S(1)} %get-tuple-element.23.own_ref, bf16[544,128]{1,0:T(8,128)(2,1)S(1)} %collective-permute-done.left_ref, bf16[544,128]{1,0:T(8,128)(2,1)S(1)} %collective-permute-done.1.right_ref, bf16[256,1024]{1,0:T(8,128)(2,1)S(1)} %get-tuple-element.24.unit_ref, ...), custom_call_target="tpu_custom_call" | custom-call | flops 67108864 | bytes 4194304 | tf_op jit(solution)/shard_map/layer_part/pallas_call | solution.py:465
  116.1 6.2 %all-to-all-start.1 = ((bf16[16,144,128]{2,1,0:T(8,128)(2,1)}), bf16[16,144,128]{2,1,0:T(8,128)(2,1)S(1)}, u32[]{:S(2)}, u32[]{:S(2)}) async-start(bf16[16,144,128]{2,1,0:T(8,128)(2,1)} %layer_part.1), calls=%async_computation.1 | async-start | bytes 1179648 | tf_op jit(solution)/shard_map/all_to_all | solution.py:382
  122.3 2.3 %copy-done.2 = bf16[2304,1024]{1,0:T(8,128)(2,1)S(1)} copy-done((bf16[2304,1024]{1,0:T(8,128)(2,1)S(1)}, bf16[2304,1024]{1,0:T(8,128)(2,1)}, u32[]{:S(2)}) %copy-start.2) | copy-done | bytes 4718616
  125.1 19.7 %all-to-all-done.1.heads_ref.arrived_grad_ref = bf16[16,144,128]{2,1,0:T(8,128)(2,1)S(1)} async-done(((bf16[16,144,128]{2,1,0:T(8,128)(2,1)}), bf16[16,144,128]{2,1,0:T(8,128)(2,1)S(1)}, u32[]{:S(2)}, u32[]{:S(2)}) %all-to-all-start.1) | async-done | bytes 589856 | tf_op jit(solution)/shard_map/all_to_all | solution.py:382
  144.8 5.6 %back_part.1 = (f32[8,128,128]{2,1,0:T(8,128)S(1)}, bf16[32,128,128]{2,1,0:T(8,128)(2,1)S(1)}) custom-call(s32[2,30]{1,0:T(2,128)S(1)} %copy-done.17, s32[2]{0:T(128)S(1)} %copy-done.19, f32[2,30]{1,0:T(2,128)S(1)} %bitcast.26, s32[1]{0:T(128)} %bitcast.12.me_ref, bf16[16,144,128]{2,1,0:T(8,128)(2,1)S(1)} %all-to-all-done.1.heads_ref.arrived_grad_ref, ...), custom_call_target="tpu_custom_call" | custom-call | flops 67108864 | bytes 4194304 | tf_op jit(solution)/shard_map/back_part/pallas_call | solution.py:469
  150.4 32.3 %all_to_all.20.back_ref = bf16[32,128,128]{2,1,0:T(8,128)(2,1)S(1)} all-to-all(bf16[32,128,128]{2,1,0:T(8,128)(2,1)S(1)} %get-tuple-element.34), channel_id=1, replica_groups=mesh['grid'=32,'head'=16] {'grid'}, dimensions={0} | all-to-all | bytes 2097152 | tf_op jit(solution)/shard_map/all_to_all | solution.py:382
  182.7 2.1 %final_part.1 = bf16[32,32,128]{2,1,0:T(8,128)(2,1)} custom-call(s32[32]{0:T(128)S(1)} %bitcast.28, bf16[1024,1024]{1,0:T(8,128)(2,1)S(1)} %copy-done.4, f32[8,128,128]{2,1,0:T(8,128)S(1)} %get-tuple-element.33.own_ref, bf16[32,128,128]{2,1,0:T(8,128)(2,1)S(1)} %all_to_all.20.back_ref), custom_call_target="tpu_custom_call" | custom-call | flops 67108864 | bytes 4194304 | tf_op jit(solution)/shard_map/final_part/pallas_call | solution.py:485
  184.8 3.9 %all-to-all-start.3 = ((bf16[32,32,128]{2,1,0:T(8,128)(2,1)}), bf16[32,32,128]{2,1,0:T(8,128)(2,1)S(1)}, u32[]{:S(2)}, u32[]{:S(2)}) async-start(bf16[32,32,128]{2,1,0:T(8,128)(2,1)} %final_part.1), calls=%async_computation.3 | async-start | bytes 524288 | tf_op jit(solution)/shard_map/all_to_all | solution.py:382
  188.7 2.3 %copy-done.3 = bf16[2304,1024]{1,0:T(8,128)(2,1)S(1)} copy-done((bf16[2304,1024]{1,0:T(8,128)(2,1)S(1)}, bf16[2304,1024]{1,0:T(8,128)(2,1)}, u32[]{:S(2)}) %copy-start.3) | copy-done | bytes 4718616
  191.1 1.0 output_part.1
  192.1 5.7 %all-to-all-done.3.parts_ref = bf16[32,32,128]{2,1,0:T(8,128)(2,1)S(1)} async-done(((bf16[32,32,128]{2,1,0:T(8,128)(2,1)}), bf16[32,32,128]{2,1,0:T(8,128)(2,1)S(1)}, u32[]{:S(2)}, u32[]{:S(2)}) %all-to-all-start.3) | async-done | bytes 262176 | tf_op jit(solution)/shard_map/all_to_all | solution.py:382
  (46 shorter events, 3.2 us)
Async XLA Ops:
  7.2 85.2 %all-gather.4.cloned.1.call-start = ((), (), s32[]{:S(2)}) async-start(), calls=%async_computation.4 | async-start | bytes 5013504 | tf_op jit(solution)/shard_map/all_gather | solution.py:415
  9.0 16.3 %copy-start.5 = (bf16[256,1024]{1,0:T(8,128)(2,1)S(1)}, bf16[256,1024]{1,0:T(8,128)(2,1)}, u32[]{:S(2)}) copy-start(bf16[256,1024]{1,0:T(8,128)(2,1)} %mesh_ref.3) | copy-start | bytes 1572868
  9.0 16.3 %copy-start.14 = (bf16[1024,64]{0,1:T(8,128)(2,1)S(1)}, bf16[1024,64]{0,1:T(8,128)(2,1)}, u32[]{:S(2)}) copy-start(bf16[1024,64]{0,1:T(8,128)(2,1)} %param.18) | copy-start | bytes 393220
  9.0 33.6 %copy-start.17 = (s32[2,30]{1,0:T(2,128)S(1)}, s32[2,30]{1,0:T(2,128)}, u32[]{:S(2)}) copy-start(s32[2,30]{1,0:T(2,128)} %slot_ref.3) | copy-start | bytes 724
  9.0 33.6 %copy-start.18 = (f32[2,30,1]{1,2,0:T(1,128)S(1)}, f32[2,30,1]{1,2,0:T(1,128)}, u32[]{:S(2)}) copy-start(f32[2,30,1]{1,2,0:T(1,128)} %param.26) | copy-start | bytes 724
  9.0 33.5 %copy-start.19 = (s32[2]{0:T(128)S(1)}, s32[2]{0:T(128)}, u32[]{:S(2)}) copy-start(s32[2]{0:T(128)} %count_ref.3) | copy-start | bytes 28
  14.6 28.0 %copy-start.6 = (bf16[8,128,128]{2,1,0:T(8,128)(2,1)S(1)}, bf16[8,128,128]{2,1,0:T(8,128)(2,1)}, u32[]{:S(2)}) copy-start(bf16[8,128,128]{2,1,0:T(8,128)(2,1)} %get-tuple-element.20.own_ref) | copy-start | bytes 786436
  14.6 77.7 %copy-start.7 = (bf16[1024,64]{0,1:T(8,128)(2,1)S(1)}, bf16[1024,64]{0,1:T(8,128)(2,1)}, u32[]{:S(2)}) copy-start(bf16[1024,64]{0,1:T(8,128)(2,1)} %param.22) | copy-start | bytes 393220
  14.6 77.7 %copy-start.8 = (bf16[1024,64]{0,1:T(8,128)(2,1)S(1)}, bf16[1024,64]{0,1:T(8,128)(2,1)}, u32[]{:S(2)}) copy-start(bf16[1024,64]{0,1:T(8,128)(2,1)} %param.23) | copy-start | bytes 393220
  14.6 77.7 %copy-start.9 = (bf16[1024,64]{0,1:T(8,128)(2,1)S(1)}, bf16[1024,64]{0,1:T(8,128)(2,1)}, u32[]{:S(2)}) copy-start(bf16[1024,64]{0,1:T(8,128)(2,1)} %param.24) | copy-start | bytes 393220
  14.7 77.7 %copy-start.10 = (bf16[64,1024]{1,0:T(8,128)(2,1)S(1)}, bf16[64,1024]{1,0:T(8,128)(2,1)}, u32[]{:S(2)}) copy-start(bf16[64,1024]{1,0:T(8,128)(2,1)} %wl_ref.1) | copy-start | bytes 393220
  14.7 77.7 %copy-start.21 = (f32[2,3,1]{1,2,0:T(1,128)S(1)}, f32[2,3,1]{1,2,0:T(1,128)}, u32[]{:S(2)}) copy-start(f32[2,3,1]{1,2,0:T(1,128)} %param.27) | copy-start | bytes 76
  14.7 27.9 %all-to-all-start = ((bf16[32,128,128]{2,1,0:T(8,128)(2,1)}), bf16[32,128,128]{2,1,0:T(8,128)(2,1)S(1)}, u32[]{:S(2)}, u32[]{:S(2)}) async-start(bf16[32,128,128]{2,1,0:T(8,128)(2,1)} %get-tuple-element.21), calls=%async_computation | async-start | bytes 2097152 | tf_op jit(solution)/shard_map/all_to_all | solution.py:382
  92.4 2.3 %copy-start = (bf16[2304,1024]{1,0:T(8,128)(2,1)S(1)}, bf16[2304,1024]{1,0:T(8,128)(2,1)}, u32[]{:S(2)}) copy-start(bf16[2304,1024]{1,0:T(8,128)(2,1)} %all-gather.4.cloned.1.call-done) | copy-start | bytes 14155780
  94.7 16.5 %copy-start.1 = (bf16[2304,1024]{1,0:T(8,128)(2,1)S(1)}, bf16[2304,1024]{1,0:T(8,128)(2,1)}, u32[]{:S(2)}) copy-start(bf16[2304,1024]{1,0:T(8,128)(2,1)} %all-gather.4.cloned.1.call-done) | copy-start | bytes 14155780
  97.7 12.3 %collective-permute-start.1 = (bf16[544,128]{1,0:T(8,128)(2,1)S(1)}, bf16[544,128]{1,0:T(8,128)(2,1)S(1)}, u32[]{:S(2)}, u32[]{:S(2)}) collective-permute-start(bf16[544,128]{1,0:T(8,128)(2,1)S(1)} %get-tuple-element.23.own_ref), channel_id=1, source_target_pairs={{16,0},{32,16},{48,32},{64,48},{80,64},{96,80},{112,96},{128,112},... | collective-permute-start | bytes 417800 | tf_op jit(solution)/shard_map/ppermute | solution.py:453
  106.2 5.0 %collective-permute-start = (bf16[544,128]{1,0:T(8,128)(2,1)S(1)}, bf16[544,128]{1,0:T(8,128)(2,1)S(1)}, u32[]{:S(2)}, u32[]{:S(2)}) collective-permute-start(bf16[544,128]{1,0:T(8,128)(2,1)S(1)} %get-tuple-element.23.own_ref), channel_id=1, source_target_pairs={{0,16},{16,32},{32,48},{48,64},{64,80},{80,96},{96,112},{112,128},... | collective-permute-start | bytes 417800 | tf_op jit(solution)/shard_map/ppermute | solution.py:452
  111.2 11.1 %copy-start.11 = (bf16[64,1024]{1,0:T(8,128)(2,1)S(1)}, bf16[64,1024]{1,0:T(8,128)(2,1)}, u32[]{:S(2)}) copy-start(bf16[64,1024]{1,0:T(8,128)(2,1)} %wo_ref.1) | copy-start | bytes 393220
  111.2 11.1 %copy-start.13 = (f32[24,1024]{1,0:T(8,128)S(1)}, f32[24,1024]{1,0:T(8,128)}, u32[]{:S(2)}) copy-start(f32[24,1024]{1,0:T(8,128)} %copy-done.12) | copy-start | bytes 294916
  116.1 28.7 %all-to-all-start.1 = ((bf16[16,144,128]{2,1,0:T(8,128)(2,1)}), bf16[16,144,128]{2,1,0:T(8,128)(2,1)S(1)}, u32[]{:S(2)}, u32[]{:S(2)}) async-start(bf16[16,144,128]{2,1,0:T(8,128)(2,1)} %layer_part.1), calls=%async_computation.1 | async-start | bytes 1179648 | tf_op jit(solution)/shard_map/all_to_all | solution.py:382
  124.6 20.2 %copy-start.16 = (f32[2,64,128]{2,1,0:T(8,128)S(1)}, f32[2,64,128]{2,1,0:T(8,128)}, u32[]{:S(2)}) copy-start(f32[2,64,128]{2,1,0:T(8,128)} %copy-done.15) | copy-start | bytes 196612
  144.8 37.9 %copy-start.4 = (bf16[1024,1024]{1,0:T(8,128)(2,1)S(1)}, bf16[1024,1024]{1,0:T(8,128)(2,1)}, u32[]{:S(2)}) copy-start(bf16[1024,1024]{1,0:T(8,128)(2,1)} %get-tuple-element.26.norm_ref) | copy-start | bytes 6291460
  144.8 37.9 %copy-start.20 = (s32[1,32]{1,0:T(1,128)S(1)}, s32[1,32]{1,0:T(1,128)}, u32[]{:S(2)}) copy-start(s32[1,32]{1,0:T(1,128)} %param.28) | copy-start | bytes 388
  184.8 12.9 %all-to-all-start.3 = ((bf16[32,32,128]{2,1,0:T(8,128)(2,1)}), bf16[32,32,128]{2,1,0:T(8,128)(2,1)S(1)}, u32[]{:S(2)}, u32[]{:S(2)}) async-start(bf16[32,32,128]{2,1,0:T(8,128)(2,1)} %final_part.1), calls=%async_computation.3 | async-start | bytes 524288 | tf_op jit(solution)/shard_map/all_to_all | solution.py:382
  (4 other events, 5.9 us)
Sparse Core Ops, SparseCore 0:
  10.1 82.2 all-gather.3

commit v4 on v3

--- a/solution.py
+++ b/solution.py
@@ -22,6 +22,7 @@
 
 VMEM = pl.BlockSpec(memory_space=pltpu.VMEM)
 SMEM = pl.BlockSpec(memory_space=pltpu.SMEM)
+HBM = pl.BlockSpec(memory_space=pltpu.HBM)
 
 
 def dot(left, right, dims=NN):
@@ -98,6 +99,22 @@
     )(send, feat, wk, wv)
 
 
+def rows_kernel(wo_ref, wl_ref, cot_ref, out_ref, sem_ref):
+    half = D // 2
+    start = pl.multiple_of(lax.rem(lax.axis_index("grid"), 2) * half, half)
+    copies = [
+        pltpu.make_async_copy(wo_ref, out_ref.at[0:D], sem_ref.at[0]),
+        pltpu.make_async_copy(
+            wl_ref.at[pl.ds(start, half)], out_ref.at[D : D + half], sem_ref.at[1]
+        ),
+        pltpu.make_async_copy(cot_ref, out_ref.at[D + half :], sem_ref.at[2]),
+    ]
+    for copy in copies:
+        copy.start()
+    for copy in copies:
+        copy.wait()
+
+
 def query_kernel(mesh_ref, wq_ref, out_ref):
     for b in range(out_ref.shape[0]):
         unit, _ = normalize(mesh_ref[b * B : (b + 1) * B].astype(f32))
@@ -123,12 +140,28 @@
     return parts[0]
 
 
+def fill_tables(slot_ref, bias_ref, full, reader_ref, edge_ref):
+    for i in range(reader_ref.shape[0]):
+        reader_ref[i] = 0
+        edge_ref[i] = 0.0
+    for m, total in ((full, FULL), (1 - full, REST)):
+
+        def put(e, carry, m=m):
+            slot = slot_ref[m, e]
+            reader_ref[slot] = m
+            edge_ref[slot] = bias_ref[m, e]
+            return carry
+
+        lax.fori_loop(0, total, put, 0, unroll=3)
+
+
 def encoder_kernel(
-    slot_ref, count_ref, bias_ref, own_ref, arrived_ref, query_ref,
-    wide_ref, out_ref, lse_ref, pool_ref, score_ref,
+    slot_ref, count_ref, bias_ref, me_ref, own_ref, arrived_ref, query_ref,
+    out_ref, lse_ref, early_ref, pool_ref, score_ref, reader_ref, edge_ref,
 ):
     fill_pool(pool_ref, own_ref, arrived_ref)
     full = jnp.where(count_ref[0] == FULL, 0, 1)
+    fill_tables(slot_ref, bias_ref, full, reader_ref, edge_ref)
     for m, total in ((full, FULL), (1 - full, REST)):
         stack = jnp.concatenate([query_ref[m], jnp.zeros((D, B), bf16)], axis=0)
 
@@ -150,18 +183,51 @@
             0, total, mix, (jnp.zeros((8, B), f32), jnp.zeros((2 * D, B), f32)), unroll=3
         )
         low = jnp.sum(low, axis=0, keepdims=True)
-        rows = acc[D:] / low
-        wide_ref[m] = rows
-        out_ref[m] = rows.astype(bf16)
+        out_ref[m] = (acc[D:] / low).astype(bf16)
         lse_ref[m] = jnp.broadcast_to(top + jnp.log(low), (8, B))
+    own = own_ref.shape[0]
+    row = lax.broadcasted_iota(jnp.int32, (16, B), 0)
+    for p in range(early_ref.shape[0]):
+        m = reader_ref[own + p]
+        other = me_ref[0] != p
+        early_ref[p, 0:D] = jnp.where(other, query_ref[m], jnp.zeros((D, B), bf16))
+        early_ref[p, D : 2 * D] = jnp.where(other, out_ref[m], jnp.zeros((D, B), bf16))
+        shift = jnp.concatenate([lse_ref[m], lse_ref[m]], axis=0) - edge_ref[own + p]
+        shift = jnp.where(other, shift, 0.0)
+        high = shift.astype(bf16).astype(f32)
+        middle = (shift - high).astype(bf16).astype(f32)
+        rest = shift - high - middle
+        tail = jnp.where(row == 0, high, jnp.where(row == 1, middle, jnp.where(row == 2, rest, 0.0)))
+        early_ref[p, 2 * D :] = tail.astype(bf16)
 
 
 def middle_kernel(
     at_ref, bias_ref, heads_ref, gathered_ref, mesh_ref, wq_ref, wk_ref, wv_ref, wl_ref,
-    pack_ref, tail_ref, unit_ref, enc_ref,
+    pack_ref, tail_ref, unit_ref, enc_ref, w_out_ref, cot_ref, sem_ref,
 ):
     parts = heads_ref.shape[0]
-    w_out = gathered_ref[:, 0:D, :].reshape(parts * D, C)
+    first = parts // 2
+    copies = [
+        pltpu.make_async_copy(
+            gathered_ref.at[0:first, 0:D, :], w_out_ref.at[0:first], sem_ref.at[0]
+        ),
+        pltpu.make_async_copy(
+            gathered_ref.at[first:parts, 0:D, :], w_out_ref.at[first:parts], sem_ref.at[1]
+        ),
+        pltpu.make_async_copy(
+            gathered_ref.at[:, D + D // 2 :, :], cot_ref, sem_ref.at[2]
+        ),
+    ]
+    for copy in copies:
+        copy.start()
+    copies[0].wait()
+    for b in range(2):
+        rows = slice(b * B, (b + 1) * B)
+        heads = heads_ref[0:first, b].reshape(first * D, B)
+        w_out = w_out_ref[0:first].reshape(first * D, C)
+        enc_ref[rows] = mesh_ref[rows].astype(f32) + dot(heads, w_out, TN)
+    copies[1].wait()
+    copies[2].wait()
     w_layer = jnp.concatenate([wk_ref[...], wv_ref[...], wq_ref[...]], axis=0)
     half = parts // 2
     height = 2 * B // parts
@@ -169,8 +235,9 @@
     queries, grads = [], []
     for b in range(2):
         rows = slice(b * B, (b + 1) * B)
-        heads = heads_ref[:, b].reshape(parts * D, B)
-        enc = mesh_ref[rows].astype(f32) + dot(heads, w_out, TN)
+        heads = heads_ref[first:, b].reshape((parts - first) * D, B)
+        w_out = w_out_ref[first:].reshape((parts - first) * D, C)
+        enc = enc_ref[rows] + dot(heads, w_out, TN)
         enc_ref[rows] = enc
         unit, inverse = normalize(enc)
         unit = unit.astype(bf16)
@@ -179,7 +246,7 @@
         both = dot(unit, w_layer, NT).astype(bf16)
         pack_ref[rows] = both[:, : 2 * D]
         queries.append((both[:, 2 * D :].astype(f32) * score_scale).astype(bf16))
-        cot = gathered_ref[half * b : half * (b + 1), 2 * D :, :].reshape(B, C)
+        cot = cot_ref[half * b : half * (b + 1)].reshape(B, C)
         grads.append(dot(cot, wl_ref[...], NT).astype(bf16))
     tail_ref[:height] = enc_ref[pl.ds(pl.multiple_of(at_ref[0] * height, height), height), :]
     pack_ref[2 * B : 3 * B] = jnp.concatenate(queries, axis=1)
@@ -196,23 +263,27 @@
     pack_ref[4 * B : 4 * B + 32] = jnp.concatenate(tail, axis=0).astype(bf16)
 
 
-def side_kernel(gathered_ref, unit_ref, tail_ref, wo_ref, cot_ref, unit_out_ref, inv_out_ref, sum_ref):
+def side_kernel(gathered_ref, unit_ref, tail_ref, wo_ref, cot_ref, unit_out_ref, inv_out_ref, sum_ref, half_ref):
     half = gathered_ref.shape[0] // 2
     weight = wo_ref[...]
     for b in range(2):
         rows = slice(b * B, (b + 1) * B)
-        cot = gathered_ref[half * b : half * (b + 1), 2 * D :, :].reshape(B, C)
+        cot = gathered_ref[half * b : half * (b + 1), D + D // 2 :, :].reshape(B, C)
         cot_ref[b] = dot(weight, cot, NT)
         unit_out_ref[b] = dot(weight, unit_ref[rows], NT)
         inv_out_ref[b] = tail_ref[tail_ref.shape[0] - 8 :, b * B : (b + 1) * B]
     sum_ref[...] = jnp.broadcast_to(
         jnp.sum(weight.astype(f32), axis=1, keepdims=True), sum_ref.shape
     )
+    half_ref[...] = gathered_ref[:, D : D + D // 2, :]
 
 
 def layer_kernel(
-    own_ref, left_ref, right_ref, unit_ref, wq_ref, wk_ref, wv_ref, gathered_ref, send_ref
+    own_ref, left_ref, right_ref, unit_ref, wq_ref, wk_ref, wv_ref, gathered_ref, send_ref,
+    w_out_ref, sem_ref,
 ):
+    copy = pltpu.make_async_copy(gathered_ref.at[:, 0:D, :], w_out_ref, sem_ref)
+    copy.start()
     zero = jnp.zeros((B, D), bf16)
 
     def block(ref, b):
@@ -285,88 +356,98 @@
     total = jnp.concatenate(totals, axis=0)
     heads = jnp.concatenate(heads, axis=0)
     share = heads.shape[0] // parts
+    copy.wait()
     for z in range(parts):
-        piece = dot(gathered_ref[z, 0:D, :], total, NT).astype(bf16)
+        piece = dot(w_out_ref[z], total, NT).astype(bf16)
         for b in range(2):
             send_ref[z, b * D : (b + 1) * D] = piece[:, b * B : (b + 1) * B]
         rows = heads[z * share : (z + 1) * share]
         send_ref[z, 2 * D :] = jnp.concatenate([rows, stats], axis=1)
 
 
-def back_kernel(
-    slot_ref, count_ref, bias_ref, me_ref, arrived_grad_ref, cot_ref, unit_ref, inv_ref, sum_ref,
-    wide_ref, lse_ref, query_ref, own_ref, arrived_ref,
-    own_out_ref, send_ref, pool_ref, grad_ref, pair_ref, inner_ref,
+def grad_kernel(
+    slot_ref, count_ref, bias_ref, me_ref, arrived_ref, cot_ref, unit_ref, inv_ref, sum_ref,
+    grad_ref, send_ref, reader_ref, edge_ref,
 ):
-    fill_pool(pool_ref, own_ref, arrived_ref)
-    zero = jnp.zeros((D, B), bf16)
-    total = arrived_grad_ref[0].astype(f32)
-    for z in range(1, arrived_grad_ref.shape[0]):
-        total = total + arrived_grad_ref[z].astype(f32)
+    full = jnp.where(count_ref[0] == FULL, 0, 1)
+    fill_tables(slot_ref, bias_ref, full, reader_ref, edge_ref)
+    total = arrived_ref[0].astype(f32)
+    for z in range(1, arrived_ref.shape[0]):
+        total = total + arrived_ref[z].astype(f32)
     stats = total[2 * D :, D:]
     stats = jnp.concatenate([stats[0:8], stats[8:16]], axis=1)
     for b in range(2):
         first = stats[4 * b : 4 * b + 1] + stats[4 * b + 2 : 4 * b + 3]
         second = stats[4 * b + 1 : 4 * b + 2] + stats[4 * b + 3 : 4 * b + 4]
         inside = total[b * D : (b + 1) * D] - first * sum_ref[...] - second * unit_ref[b]
-        grad = (cot_ref[b] + inv_ref[b][0:1] * inside).astype(bf16)
-        inner = jnp.sum(grad.astype(f32) * wide_ref[b], axis=0, keepdims=True)
-        inner_ref[b] = jnp.broadcast_to(inner, (8, B))
-        pair_ref[b] = jnp.concatenate(
-            [
-                jnp.concatenate([query_ref[b], zero], axis=1),
-                jnp.concatenate([zero, grad], axis=1),
-            ],
-            axis=0,
+        grad_ref[b] = (cot_ref[b] + inv_ref[b][0:1] * inside).astype(bf16)
+    shards = send_ref.shape[0]
+    own = reader_ref.shape[0] - shards
+    for p in range(shards):
+        block = grad_ref[reader_ref[own + p]]
+        send_ref[p] = jnp.where(me_ref[0] != p, block, jnp.zeros((D, B), bf16))
+
+
+def final_kernel(
+    send_ref, slot_ref, count_ref, bias_ref, norm_ref, kv_ref, early_ref, grads_ref,
+    query_ref, heads_ref, lse_ref, grad_ref, out_ref, acc_ref, reader_ref, edge_ref,
+    held_ref, sem_ref,
+):
+    copy = pltpu.make_async_copy(norm_ref, held_ref, sem_ref)
+    copy.start()
+    full = jnp.where(count_ref[0] == FULL, 0, 1)
+    fill_tables(slot_ref, bias_ref, full, reader_ref, edge_ref)
+    zero = jnp.zeros((D, B), bf16)
+
+    def back(keys, query, heads, shift, grad):
+        inner = jnp.sum(grad.astype(f32) * heads.astype(f32), axis=0, keepdims=True)
+        pair = jnp.concatenate(
+            [jnp.concatenate([query, zero], axis=1), jnp.concatenate([zero, grad], axis=1)], axis=0
         )
-    own = own_ref.shape[0]
-    grad_ref[own + me_ref[0]] = jnp.zeros((B, 2 * D), f32)
-    full = jnp.where(count_ref[0] == FULL, 0, 1)
-    for m, total in ((full, FULL), (1 - full, REST)):
-        pair = pair_ref[m]
-        lse = lse_ref[m][0:1]
-        inner = inner_ref[m][0:1]
-
-        def step(e, carry, m=m, pair=pair, lse=lse, inner=inner):
-            slot = slot_ref[m, e]
-            both = dot(pool_ref[slot], pair)
-            soft = jnp.exp(both[:, :B] + (bias_ref[m, e] - lse))
-            mixed = jnp.concatenate(
-                [(soft * (both[:, B:] - inner)).astype(bf16), soft.astype(bf16)], axis=1
-            )
-            grad_ref[slot] = dot(mixed, pair, NT)
-            return carry
-
-        lax.fori_loop(0, total, step, 0, unroll=3)
-    for i in range(own):
-        own_out_ref[i] = grad_ref[i]
-    for i in range(send_ref.shape[0]):
-        send_ref[i] = grad_ref[own + i].astype(bf16)
-
-
-def final_kernel(send_ref, norm_ref, own_ref, back_ref, out_ref, acc_ref):
-    for i in range(own_ref.shape[0]):
-        acc_ref[i] = own_ref[i]
-
-    def add(i, carry):
-        slot = send_ref[i]
-        acc_ref[slot] = acc_ref[slot] + back_ref[i].astype(f32)
+        both = dot(keys, pair)
+        soft = jnp.exp(both[:, :B] - shift)
+        mixed = jnp.concatenate(
+            [(soft * (both[:, B:] - inner)).astype(bf16), soft.astype(bf16)], axis=1
+        )
+        return dot(mixed, pair, NT)
+
+    def own_step(v, carry):
+        m = reader_ref[v]
+        shift = lse_ref[m][0:1] - edge_ref[v]
+        acc_ref[v] = back(kv_ref[v], query_ref[m], heads_ref[m], shift, grad_ref[m])
         return carry
 
-    lax.fori_loop(0, back_ref.shape[0], add, 0, unroll=2)
+    lax.fori_loop(0, kv_ref.shape[0], own_step, 0, unroll=4)
+
+    def sent_step(r, carry):
+        slot = send_ref[r]
+        block = early_ref[r]
+        tail = block[2 * D :].astype(f32)
+        shift = tail[0:1] + tail[1:2] + tail[2:3]
+        part = back(kv_ref[slot], block[:D], block[D : 2 * D], shift, grads_ref[r])
+        acc_ref[slot] = acc_ref[slot] + part
+        return carry
+
+    lax.fori_loop(0, early_ref.shape[0], sent_step, 0, unroll=4)
     rows = acc_ref[...].reshape(norm_ref.shape[0], 2 * D).astype(bf16)
+    copy.wait()
     shards, height = out_ref.shape[0], out_ref.shape[1]
     tile = 256
     for c in range(C // tile):
-        part = dot(rows, norm_ref[:, c * tile : (c + 1) * tile], TN).T
+        part = dot(rows, held_ref[:, c * tile : (c + 1) * tile], TN).T
         per = tile // height
         out_ref[c * per : (c + 1) * per] = part.astype(bf16).reshape(per, height, 2 * D)
 
 
-def output_kernel(heads_ref, weight_ref, tail_ref, out_ref):
+def output_kernel(me_ref, heads_ref, mine_ref, other_ref, tail_ref, out_ref):
     total = tail_ref[: out_ref.shape[0]]
+    even = lax.rem(me_ref[0], 2) == 0
+    half = D // 2
     for h in range(heads_ref.shape[0]):
-        total = total + dot(heads_ref[h, 2 * D :][:, :D], weight_ref[h, D : 2 * D])
+        rows = heads_ref[h, 2 * D :][:, :D]
+        low = jnp.where(even, mine_ref[h], other_ref[h])
+        high = jnp.where(even, other_ref[h], mine_ref[h])
+        total = total + dot(rows[:, :half], low) + dot(rows[:, half:], high)
     out_ref[...] = total.astype(bf16)
 
 
@@ -412,12 +493,17 @@
     forward = [(i, (i + 1) % shards) for i in range(shards)]
     backward = [(t, s) for s, t in forward]
 
-    gathered = lax.all_gather(
-        jnp.concatenate([enc_out_weight, layer_out_weight, cotangent], axis=0),
-        "head",
-        axis=0,
-        tiled=False,
-    )
+    half = D // 2
+    shared_rows = call(
+        rows_kernel,
+        struct((D + half + share, C), bf16),
+        [HBM] * 3,
+        [pltpu.SemaphoreType.DMA((3,))],
+        name="rows_part",
+        mib=61,
+        out_specs=HBM,
+    )(enc_out_weight, layer_out_weight, cotangent)
+    gathered = lax.all_gather(shared_rows, "head", axis=0, tiled=False)
     query_weight, key_weight, value_weight, layer_query, layer_key, layer_value = (
         weight.T
         for weight in (query_weight, key_weight, value_weight, layer_query, layer_key, layer_value)
@@ -428,13 +514,19 @@
     queries = call(
         query_kernel, struct((2, D, B), bf16), [VMEM] * 2, name="query_part", data=1 << 20
     )(mesh_feat, query_weight)
-    wide_heads, enc_heads, lse = call(
+    tables = [pltpu.SMEM((own + shards,), jnp.int32), pltpu.SMEM((own + shards,), f32)]
+    enc_heads, lse, early = call(
         encoder_kernel,
-        (struct((2, D, B), f32), struct((2, D, B), bf16), struct((2, 8, B), f32)),
-        [SMEM] * 3 + [VMEM] * 3,
-        [pltpu.VMEM((own + shards, B, 2 * D), bf16), pltpu.VMEM((FULL, B, B), f32)],
+        (
+            struct((2, D, B), bf16),
+            struct((2, 8, B), f32),
+            struct((shards, 2 * D + 16, B), bf16),
+        ),
+        [SMEM] * 4 + [VMEM] * 3,
+        [pltpu.VMEM((own + shards, B, 2 * D), bf16), pltpu.VMEM((FULL, B, B), f32)] + tables,
         name="encoder_part",
-    )(edge_slot, edge_count, enc_table, own_kv, arrived_kv, queries)
+    )(edge_slot, edge_count, enc_table, shard_at, own_kv, arrived_kv, queries)
+    arrived_early = exchange(early, "grid")
     all_heads = lax.all_gather(enc_heads, "head", axis=0, tiled=False)
     pack, tail, unit = call(
         middle_kernel,
@@ -443,59 +535,74 @@
             struct((share + 8, C), f32),
             struct((2 * B, C), bf16),
         ),
-        [SMEM] * 2 + [VMEM] * 7,
-        [pltpu.VMEM((2 * B, C), f32)],
+        [SMEM] * 2 + [VMEM, HBM] + [VMEM] * 5,
+        [
+            pltpu.VMEM((2 * B, C), f32),
+            pltpu.VMEM((parts, D, C), bf16),
+            pltpu.VMEM((parts, share, C), bf16),
+            pltpu.SemaphoreType.DMA((3,)),
+        ],
         name="middle_part",
+        mib=61,
     )(
         head_at, layer_table, all_heads, gathered, mesh_feat, layer_query, layer_key, layer_value, layer_out_weight
     )
     left = lax.ppermute(pack, "grid", forward)
     right = lax.ppermute(pack, "grid", backward)
-    cot_part, unit_part, inverse_row, weight_sum = call(
+    arrived_early, left, right = lax.optimization_barrier((arrived_early, left, right))
+    cot_part, unit_part, inverse_row, weight_sum, half_mine = call(
         side_kernel,
         (
             struct((2, D, B), f32),
             struct((2, D, B), f32),
             struct((2, 8, B), f32),
             struct((D, B), f32),
+            struct((parts, half, C), bf16),
         ),
         [VMEM] * 4,
         name="side_part",
     )(gathered, unit, tail, enc_out_weight)
+    half_other = lax.ppermute(half_mine, "grid", [(i, i ^ 1) for i in range(shards)])
     mixed = call(
-        layer_kernel, struct((parts, 2 * D + share, B), bf16), [VMEM] * 8, name="layer_part"
+        layer_kernel,
+        struct((parts, 2 * D + share, B), bf16),
+        [VMEM] * 7 + [HBM],
+        [pltpu.VMEM((parts, D, C), bf16), pltpu.SemaphoreType.DMA],
+        name="layer_part",
+        mib=61,
     )(pack, left, right, unit, layer_query, layer_key, layer_value, gathered)
     arrived_grad = exchange(mixed, "head")
-    own_grad, send_grad = call(
-        back_kernel,
-        (struct((own, B, 2 * D), f32), struct((shards, B, 2 * D), bf16)),
-        [SMEM] * 4 + [VMEM] * 10,
-        [
-            pltpu.VMEM((own + shards, B, 2 * D), bf16),
-            pltpu.VMEM((own + shards, B, 2 * D), f32),
-            pltpu.VMEM((2, 2 * D, 2 * B), bf16),
-            pltpu.VMEM((2, 8, B), f32),
-        ],
-        name="back_part",
+    grads, send_grads = call(
+        grad_kernel,
+        (struct((2, D, B), bf16), struct((shards, D, B), bf16)),
+        [SMEM] * 4 + [VMEM] * 5,
+        tables,
+        name="grad_part",
     )(
         edge_slot, edge_count, enc_table, shard_at, arrived_grad, cot_part, unit_part,
-        inverse_row, weight_sum, wide_heads, lse, queries, own_kv, arrived_kv,
-    )
-    back_grad = exchange(send_grad, "grid")
+        inverse_row, weight_sum,
+    )
+    arrived_grads = exchange(send_grads, "grid")
     product = call(
         final_kernel,
         struct((shards, C // shards, 2 * D), bf16),
-        [SMEM] + [VMEM] * 3,
-        [pltpu.VMEM((own, B, 2 * D), f32)],
+        [SMEM] * 4 + [HBM] + [VMEM] * 7,
+        [pltpu.VMEM((own, B, 2 * D), f32)]
+        + tables
+        + [pltpu.VMEM(grid_norm.shape, bf16), pltpu.SemaphoreType.DMA],
         name="final_part",
-    )(send, grid_norm, own_grad, back_grad)
+        mib=61,
+    )(
+        send, edge_slot, edge_count, enc_table, grid_norm, own_kv, arrived_early, arrived_grads,
+        queries, enc_heads, lse, grads,
+    )
     pieces = exchange(product, "grid")
     mesh_out = call(
         output_kernel,
         struct((share, C), bf16),
-        [VMEM] * 3,
+        [SMEM] + [VMEM] * 4,
         name="output_part",
-    )(arrived_grad, gathered, tail)
+    )(shard_at, arrived_grad, half_mine, half_other, tail)
     key_grad, value_grad = call(
         sum_kernel,
         (struct((C // shards, D), f32), struct((C // shards, D), f32)),

time: 206 us -> 209 us (1.015)
  Pallas kernels: 28.8 us -> 44.6 us
  waiting for transfers between devices: 52.8 us -> 38.3 us
  starting transfers between devices: 32.2 us -> 44.3 us
  local copies, waits for them, and re-layouts: 8.33 us -> 3.35 us
  blocking collectives: 67.1 us -> 62.9 us
    pallas_call x5 -> x6, Pallas kernels: 19.2 us -> 32 us  [the longest x1 8.08 us: on_device(): call(rows_kernel, struct((D + half + share, C), bf16), [HBM] * 3, [pltpu....]
    all_gather x1, waiting for transfers between devices: 8.77 us -> 0.01 us  [on_device(): gathered = lax.all_gather(shared_rows, 'head', axis=0, tiled=False)]
    ppermute x0 -> x1, starting transfers between devices: none -> 7 us  [on_device(): lax.ppermute(half_mine, 'grid', [(i, i ^ 1) for i in range(shards)])]
    all_to_all x3 -> x4, waiting for transfers between devices: 42 us -> 36 us  [exchange(): return lax.all_to_all(array, axis, split_axis=0, concat_axis=0, tiled=True)]
    unnamed x44 -> x34, local copies, waits for them, and re-layouts: 8.33 us -> 3.35 us
    all_to_all x1, blocking collectives: 32.3 us -> 27.5 us  [exchange(): return lax.all_to_all(array, axis, split_axis=0, concat_axis=0, tiled=True)]
    all_to_all x3 -> x4, starting transfers between devices: 20.7 us -> 25 us  [exchange(): return lax.all_to_all(array, axis, split_axis=0, concat_axis=0, tiled=True)]
    pallas_call x1, Pallas kernels: 2.33 us -> 5.21 us  [on_device(): call(middle_kernel, (struct((4 * B + 32, 2 * D), bf16), struct((share + 8...]
  transfers between devices with their start and end apart: 6 -> 8, of which waited for: 6 -> 5; matrix products, arithmetic and copies ran while one was open for 0% -> 0% of each run, Pallas kernels for 6% -> 14%
where the time goes in v4:
time: 209 us; the launch traced here: 208 us
  blocking collectives  62.9 us (30%)
  Pallas kernels  44.6 us (21%)
  starting transfers between devices  44.3 us (21%)
  waiting for transfers between devices  38.3 us (18%)
  between operations  14.3 us (7%)
  local copies, waits for them, and re-layouts  3.35 us (2%)
    all_to_all x4, waiting for transfers between devices, exchange(): return lax.all_to_all(array, axis, split_axis=0, concat_axis=0, tiled=True)  36 us
    all_gather x1, blocking collectives, on_device(): all_heads = lax.all_gather(enc_heads, 'head', axis=0, tiled=False)  35.4 us
    all_to_all x1, blocking collectives, exchange(): return lax.all_to_all(array, axis, split_axis=0, concat_axis=0, tiled=True)  27.5 us
    all_to_all x4, starting transfers between devices, exchange(): return lax.all_to_all(array, axis, split_axis=0, concat_axis=0, tiled=True)  25 us
    ppermute x1, starting transfers between devices, on_device(): right = lax.ppermute(pack, 'grid', backward)  9.17 us
    pallas_call x1, Pallas kernels, on_device(): call(rows_kernel, struct((D + half + share, C), bf16), [HBM] * 3, [pltpu....  8.08 us
    pallas_call x1, Pallas kernels, on_device(): call(encoder_kernel, (struct((2, D, B), bf16), struct((2, 8, B), f32), st...  7.05 us
    ppermute x1, starting transfers between devices, on_device(): lax.ppermute(half_mine, 'grid', [(i, i ^ 1) for i in range(shards)])  7 us
  transfers between devices with their start and end apart: 8, of which 5 were waited for; matrix products, arithmetic and copies ran while one was open for 0% of the time, Pallas kernels for 14%

profile of v4, /device:TPU:1, one launch (start us, length us, event | category | flops | bytes accessed | tf_op | source)
XLA Modules:
  0.0 207.7 jit_solution(17805938171170607290)
XLA Ops:
  7.2 8.1 %rows_part.1 = bf16[112,1024]{1,0:T(8,128)(2,1)} custom-call(bf16[64,1024]{1,0:T(8,128)(2,1)} %wo_ref.3, bf16[64,1024]{1,0:T(8,128)(2,1)} %wl_ref.3, bf16[16,1024]{1,0:T(8,128)(2,1)} %cot_ref.1), custom_call_target="tpu_custom_call" | custom-call | flops 67108864 | bytes 4194304 | tf_op jit(solution)/shard_map/rows_part/pallas_call | solution.py:497
  15.4 5.5 %grid_part.1 = (bf16[1024,1024]{1,0:T(8,128)(2,1)}, bf16[8,128,128]{2,1,0:T(8,128)(2,1)}, bf16[32,128,128]{2,1,0:T(8,128)(2,1)}) custom-call(s32[32]{0:T(128)} %bitcast.29, bf16[1024,1024]{1,0:T(8,128)(2,1)} %feat_ref.1, bf16[64,1024]{1,0:T(8,128)(2,1)} %bitcast.27, bf16[64,1024]{1,0:T(8,128)(2,1)} %bitcast.28), custom_call_target="tpu_custom_call" | custom-call | flops 268435456 | bytes 6291456 | tf_op jit(solution)/shard_map/grid_part/pallas_call | solution.py:75
  20.9 10.6 %all-to-all-start = ((bf16[32,128,128]{2,1,0:T(8,128)(2,1)}), bf16[32,128,128]{2,1,0:T(8,128)(2,1)S(1)}, u32[]{:S(2)}, u32[]{:S(2)}) async-start(bf16[32,128,128]{2,1,0:T(8,128)(2,1)} %get-tuple-element.25), calls=%async_computation | async-start | bytes 2097152 | tf_op jit(solution)/shard_map/all_to_all | solution.py:463
  32.2 16.6 %all-to-all-done.arrived_ref = bf16[32,128,128]{2,1,0:T(8,128)(2,1)S(1)} async-done(((bf16[32,128,128]{2,1,0:T(8,128)(2,1)}), bf16[32,128,128]{2,1,0:T(8,128)(2,1)S(1)}, u32[]{:S(2)}, u32[]{:S(2)}) %all-to-all-start) | async-done | bytes 1048608 | tf_op jit(solution)/shard_map/all_to_all | solution.py:463
  48.8 7.0 %encoder_part.1 = (bf16[2,64,128]{2,1,0:T(8,128)(2,1)S(1)}, f32[2,8,128]{2,1,0:T(8,128)S(1)}, bf16[32,144,128]{2,1,0:T(8,128)(2,1)}) custom-call(s32[2,30]{1,0:T(2,128)S(1)} %copy-done.10, s32[2]{0:T(128)S(1)} %copy-done.13, f32[2,30]{1,0:T(2,128)S(1)} %bitcast.18, s32[1]{0:T(128)} %bitcast.me_ref, bf16[8,128,128]{2,1,0:T(8,128)(2,1)S(1)} %copy-done.3, ...), custom_call_target="tpu_custom_call" | custom-call | flops 67108864 | bytes 4194304 | tf_op jit(solution)/shard_map/encoder_part/pallas_call | solution.py:518
  56.5 4.0 %all-to-all-start.1 = ((bf16[32,144,128]{2,1,0:T(8,128)(2,1)}), bf16[32,144,128]{2,1,0:T(8,128)(2,1)S(1)}, u32[]{:S(2)}, u32[]{:S(2)}) async-start(bf16[32,144,128]{2,1,0:T(8,128)(2,1)} %get-tuple-element.28), calls=%async_computation.1 | async-start | bytes 2359296 | tf_op jit(solution)/shard_map/all_to_all | solution.py:463
  60.5 35.4 %all-gather = bf16[32,64,128]{2,1,0:T(8,128)(2,1)} all-gather(bf16[2,64,128]{2,1,0:T(8,128)(2,1)S(1)} %get-tuple-element.26.heads_ref), channel_id=2, replica_groups=mesh['grid'=32,'head'=16] {'head'}, dimensions={0}, use_global_device_ids=true | all-gather | bytes 557056 | tf_op jit(solution)/shard_map/all_gather | solution.py:530
  95.9 5.2 %middle_part.1 = (bf16[544,128]{1,0:T(8,128)(2,1)}, f32[24,1024]{1,0:T(8,128)}, bf16[256,1024]{1,0:T(8,128)(2,1)}) custom-call(s32[1]{0:T(128)} %bitcast.1.at_ref, f32[2,3]{1,0:T(2,128)} %bitcast.31, bf16[16,2,64,128]{3,2,1,0:T(8,128)(2,1)} %bitcast.20, bf16[16,112,1024]{2,1,0:T(8,128)(2,1)} %bitcast.13, bf16[256,1024]{1,0:T(8,128)(2,1)} %mesh_ref.3, ...), custom_call_target="tpu_custom_call" | custom-call | flops 67108864 | bytes 4194304 | tf_op jit(solution)/shard_map/middle_part/pallas_call | solution.py:531
  101.1 9.2 %collective-permute-start.1 = (bf16[544,128]{1,0:T(8,128)(2,1)}, bf16[544,128]{1,0:T(8,128)(2,1)S(1)}, u32[]{:S(2)}, u32[]{:S(2)}) collective-permute-start(bf16[544,128]{1,0:T(8,128)(2,1)} %get-tuple-element.27.own_ref), channel_id=1, source_target_pairs={{16,0},{32,16},{48,32},{64,48},{80,64},{96,80},{112,96},{128,112},... | collective-permute-start | bytes 417800 | tf_op jit(solution)/shard_map/ppermute | solution.py:551
  110.3 3.1 %collective-permute-start = (bf16[544,128]{1,0:T(8,128)(2,1)}, bf16[544,128]{1,0:T(8,128)(2,1)S(1)}, u32[]{:S(2)}, u32[]{:S(2)}) collective-permute-start(bf16[544,128]{1,0:T(8,128)(2,1)} %get-tuple-element.27.own_ref), channel_id=1, source_target_pairs={{0,16},{16,32},{32,48},{48,64},{64,80},{80,96},{96,112},{112,128},... | collective-permute-start | bytes 417800 | tf_op jit(solution)/shard_map/ppermute | solution.py:550
  113.4 1.0 collective-permute-done.1.right_ref
  114.4 1.3 collective-permute-done.left_ref
  116.4 6.6 %layer_part.1 = bf16[16,144,128]{2,1,0:T(8,128)(2,1)} custom-call(bf16[544,128]{1,0:T(8,128)(2,1)} %get-tuple-element.27.own_ref, bf16[544,128]{1,0:T(8,128)(2,1)} %copy-done.16, bf16[544,128]{1,0:T(8,128)(2,1)} %copy-done.15, bf16[256,1024]{1,0:T(8,128)(2,1)} %get-tuple-element.31.unit_ref, bf16[64,1024]{1,0:T(8,128)(2,1)} %bitcast.22, ...), custom_call_target="tpu_custom_call" | custom-call | flops 67108864 | bytes 4194304 | tf_op jit(solution)/shard_map/layer_part/pallas_call | solution.py:566
  123.0 6.4 %all-to-all-start.2 = ((bf16[16,144,128]{2,1,0:T(8,128)(2,1)}), bf16[16,144,128]{2,1,0:T(8,128)(2,1)S(1)}, u32[]{:S(2)}, u32[]{:S(2)}) async-start(bf16[16,144,128]{2,1,0:T(8,128)(2,1)} %layer_part.1), calls=%async_computation.2 | async-start | bytes 1179648 | tf_op jit(solution)/shard_map/all_to_all | solution.py:463
  129.5 2.0 copy-done
  132.0 7.0 %collective-permute-start.2 = (bf16[16,32,1024]{2,1,0:T(8,128)(2,1)S(1)}, bf16[16,32,1024]{2,1,0:T(8,128)(2,1)}, u32[]{:S(2)}, u32[]{:S(2)}) collective-permute-start(bf16[16,32,1024]{2,1,0:T(8,128)(2,1)S(1)} %get-tuple-element.33.mine_ref), channel_id=1, source_target_pairs={{0,16},{16,0},{32,48},{48,32},{64,80},{80,64},{96,112},{112,96},{1... | collective-permute-start | bytes 3145736 | tf_op jit(solution)/shard_map/ppermute | solution.py:565
  139.0 12.7 %all-to-all-done.2.heads_ref.arrived_ref = bf16[16,144,128]{2,1,0:T(8,128)(2,1)S(1)} async-done(((bf16[16,144,128]{2,1,0:T(8,128)(2,1)}), bf16[16,144,128]{2,1,0:T(8,128)(2,1)S(1)}, u32[]{:S(2)}, u32[]{:S(2)}) %all-to-all-start.2) | async-done | bytes 589856 | tf_op jit(solution)/shard_map/all_to_all | solution.py:463
  151.7 1.0 grad_part.1
  152.7 27.5 %all_to_all.25.grads_ref = bf16[32,64,128]{2,1,0:T(8,128)(2,1)} all-to-all(bf16[32,64,128]{2,1,0:T(8,128)(2,1)S(1)} %get-tuple-element.40), channel_id=1, replica_groups=mesh['grid'=32,'head'=16] {'grid'}, dimensions={0} | all-to-all | bytes 1048576 | tf_op jit(solution)/shard_map/all_to_all | solution.py:463
  180.2 7.0 %final_part.1 = bf16[32,32,128]{2,1,0:T(8,128)(2,1)} custom-call(s32[32]{0:T(128)} %bitcast.30, s32[2,30]{1,0:T(2,128)} %slot_ref.5, s32[2]{0:T(128)} %count_ref.5, f32[2,30]{1,0:T(2,128)} %bitcast.17, bf16[1024,1024]{1,0:T(8,128)(2,1)} %get-tuple-element.34.norm_ref, bf16[8,128,128]{2,1,0:T(8,128)(2,1)} %get-tuple-element.24.own_ref.kv_ref, ...), custom_call_target="tpu_custom_call" | custom-call | flops 67108864 | bytes 4194304 | tf_op jit(solution)/shard_map/final_part/pallas_call | solution.py:586
  187.1 4.0 %all-to-all-start.4 = ((bf16[32,32,128]{2,1,0:T(8,128)(2,1)}), bf16[32,32,128]{2,1,0:T(8,128)(2,1)S(1)}, u32[]{:S(2)}, u32[]{:S(2)}) async-start(bf16[32,32,128]{2,1,0:T(8,128)(2,1)} %final_part.1), calls=%async_computation.4 | async-start | bytes 524288 | tf_op jit(solution)/shard_map/all_to_all | solution.py:463
  191.1 2.3 %output_part.1 = bf16[16,1024]{1,0:T(8,128)(2,1)} custom-call(s32[1]{0:T(128)} %bitcast.me_ref, bf16[16,144,128]{2,1,0:T(8,128)(2,1)S(1)} %all-to-all-done.2.heads_ref.arrived_ref, bf16[16,32,1024]{2,1,0:T(8,128)(2,1)S(1)} %get-tuple-element.33.mine_ref, bf16[16,32,1024]{2,1,0:T(8,128)(2,1)} %collective-permute-done.2.other_ref, f32[24,1024]{1,0:T(8,128)S(1)} %copy-done.5), custom_call_target="tpu_custom_call" | custom-call | flops 67108864 | bytes 4194304 | tf_op jit(solution)/shard_map/output_part/pallas_call | solution.py:600
  193.5 6.7 %all-to-all-done.4.parts_ref = bf16[32,32,128]{2,1,0:T(8,128)(2,1)S(1)} async-done(((bf16[32,32,128]{2,1,0:T(8,128)(2,1)}), bf16[32,32,128]{2,1,0:T(8,128)(2,1)S(1)}, u32[]{:S(2)}, u32[]{:S(2)}) %all-to-all-start.4) | async-done | bytes 262176 | tf_op jit(solution)/shard_map/all_to_all | solution.py:463
  200.1 0.7 sum_part.1
  (40 shorter events, 2.4 us)
Async XLA Ops:
  7.2 88.7 %all-gather.4.cloned.1.call-start = ((), (), s32[]{:S(2)}) async-start(), calls=%async_computation.5 | async-start | bytes 3899392 | tf_op jit(solution)/shard_map/all_gather | solution.py:506
  15.3 16.2 %copy-start.1 = (bf16[256,1024]{1,0:T(8,128)(2,1)S(1)}, bf16[256,1024]{1,0:T(8,128)(2,1)}, u32[]{:S(2)}) copy-start(bf16[256,1024]{1,0:T(8,128)(2,1)} %mesh_ref.3) | copy-start | bytes 1572868
  15.3 16.2 %copy-start.8 = (bf16[1024,64]{0,1:T(8,128)(2,1)S(1)}, bf16[1024,64]{0,1:T(8,128)(2,1)}, u32[]{:S(2)}) copy-start(bf16[1024,64]{0,1:T(8,128)(2,1)} %param.18) | copy-start | bytes 393220
  15.3 33.5 %copy-start.10 = (s32[2,30]{1,0:T(2,128)S(1)}, s32[2,30]{1,0:T(2,128)}, u32[]{:S(2)}) copy-start(s32[2,30]{1,0:T(2,128)} %slot_ref.5) | copy-start | bytes 724
  15.4 33.5 %copy-start.11 = (f32[2,30,1]{1,2,0:T(1,128)S(1)}, f32[2,30,1]{1,2,0:T(1,128)}, u32[]{:S(2)}) copy-start(f32[2,30,1]{1,2,0:T(1,128)} %param.26) | copy-start | bytes 724
  15.4 33.5 %copy-start.13 = (s32[2]{0:T(128)S(1)}, s32[2]{0:T(128)}, u32[]{:S(2)}) copy-start(s32[2]{0:T(128)} %count_ref.5) | copy-start | bytes 28
  20.9 27.9 %copy-start.3 = (bf16[8,128,128]{2,1,0:T(8,128)(2,1)S(1)}, bf16[8,128,128]{2,1,0:T(8,128)(2,1)}, u32[]{:S(2)}) copy-start(bf16[8,128,128]{2,1,0:T(8,128)(2,1)} %get-tuple-element.24.own_ref.kv_ref) | copy-start | bytes 786436
  20.9 27.9 %all-to-all-start = ((bf16[32,128,128]{2,1,0:T(8,128)(2,1)}), bf16[32,128,128]{2,1,0:T(8,128)(2,1)S(1)}, u32[]{:S(2)}, u32[]{:S(2)}) async-start(bf16[32,128,128]{2,1,0:T(8,128)(2,1)} %get-tuple-element.25), calls=%async_computation | async-start | bytes 2097152 | tf_op jit(solution)/shard_map/all_to_all | solution.py:463
  32.2 63.7 %copy-start.6 = (bf16[2,64,128]{2,1,0:T(8,128)(2,1)}, bf16[2,64,128]{2,1,0:T(8,128)(2,1)S(1)}, u32[]{:S(2)}) copy-start(bf16[2,64,128]{2,1,0:T(8,128)(2,1)S(1)} %query_part.1.query_ref) | copy-start | bytes 98308
  56.5 44.6 %copy-start.7 = (bf16[2,64,128]{2,1,0:T(8,128)(2,1)}, bf16[2,64,128]{2,1,0:T(8,128)(2,1)S(1)}, u32[]{:S(2)}) copy-start(bf16[2,64,128]{2,1,0:T(8,128)(2,1)S(1)} %get-tuple-element.26.heads_ref) | copy-start | bytes 98308
  56.5 56.9 %all-to-all-start.1 = ((bf16[32,144,128]{2,1,0:T(8,128)(2,1)}), bf16[32,144,128]{2,1,0:T(8,128)(2,1)S(1)}, u32[]{:S(2)}, u32[]{:S(2)}) async-start(bf16[32,144,128]{2,1,0:T(8,128)(2,1)} %get-tuple-element.28), calls=%async_computation.1 | async-start | bytes 2359296 | tf_op jit(solution)/shard_map/all_to_all | solution.py:463
  101.1 13.3 %collective-permute-start.1 = (bf16[544,128]{1,0:T(8,128)(2,1)}, bf16[544,128]{1,0:T(8,128)(2,1)S(1)}, u32[]{:S(2)}, u32[]{:S(2)}) collective-permute-start(bf16[544,128]{1,0:T(8,128)(2,1)} %get-tuple-element.27.own_ref), channel_id=1, source_target_pairs={{16,0},{32,16},{48,32},{64,48},{80,64},{96,80},{112,96},{128,112},... | collective-permute-start | bytes 417800 | tf_op jit(solution)/shard_map/ppermute | solution.py:551
  110.3 5.4 %collective-permute-start = (bf16[544,128]{1,0:T(8,128)(2,1)}, bf16[544,128]{1,0:T(8,128)(2,1)S(1)}, u32[]{:S(2)}, u32[]{:S(2)}) collective-permute-start(bf16[544,128]{1,0:T(8,128)(2,1)} %get-tuple-element.27.own_ref), channel_id=1, source_target_pairs={{0,16},{16,32},{32,48},{48,64},{64,80},{80,96},{96,112},{112,128},... | collective-permute-start | bytes 417800 | tf_op jit(solution)/shard_map/ppermute | solution.py:550
  113.4 2.3 %copy-start.14 = (bf16[32,144,128]{2,1,0:T(8,128)(2,1)}, bf16[32,144,128]{2,1,0:T(8,128)(2,1)S(1)}, u32[]{:S(2)}) copy-start(bf16[32,144,128]{2,1,0:T(8,128)(2,1)S(1)} %all-to-all-done.1.early_ref) | copy-start | bytes 3538948
  114.4 1.3 copy-start.15
  115.7 0.7 copy-start.16
  116.4 13.1 %copy-start.2 = (bf16[256,1024]{1,0:T(8,128)(2,1)S(1)}, bf16[256,1024]{1,0:T(8,128)(2,1)}, u32[]{:S(2)}) copy-start(bf16[256,1024]{1,0:T(8,128)(2,1)} %get-tuple-element.31.unit_ref) | copy-start | bytes 1572868
  116.4 13.1 %copy-start.4 = (bf16[64,1024]{1,0:T(8,128)(2,1)S(1)}, bf16[64,1024]{1,0:T(8,128)(2,1)}, u32[]{:S(2)}) copy-start(bf16[64,1024]{1,0:T(8,128)(2,1)} %wo_ref.3) | copy-start | bytes 393220
  116.4 13.1 %copy-start.5 = (f32[24,1024]{1,0:T(8,128)S(1)}, f32[24,1024]{1,0:T(8,128)}, u32[]{:S(2)}) copy-start(f32[24,1024]{1,0:T(8,128)} %get-tuple-element.32.tail_ref) | copy-start | bytes 294916
  123.0 28.7 %all-to-all-start.2 = ((bf16[16,144,128]{2,1,0:T(8,128)(2,1)}), bf16[16,144,128]{2,1,0:T(8,128)(2,1)S(1)}, u32[]{:S(2)}, u32[]{:S(2)}) async-start(bf16[16,144,128]{2,1,0:T(8,128)(2,1)} %layer_part.1), calls=%async_computation.2 | async-start | bytes 1179648 | tf_op jit(solution)/shard_map/all_to_all | solution.py:463
  129.5 2.0 copy-start
  132.0 59.1 %collective-permute-start.2 = (bf16[16,32,1024]{2,1,0:T(8,128)(2,1)S(1)}, bf16[16,32,1024]{2,1,0:T(8,128)(2,1)}, u32[]{:S(2)}, u32[]{:S(2)}) collective-permute-start(bf16[16,32,1024]{2,1,0:T(8,128)(2,1)S(1)} %get-tuple-element.33.mine_ref), channel_id=1, source_target_pairs={{0,16},{16,0},{32,48},{48,32},{64,80},{80,64},{96,112},{112,96},{1... | collective-permute-start | bytes 3145736 | tf_op jit(solution)/shard_map/ppermute | solution.py:565
  152.7 27.5 %copy-start.9 = (bf16[2,64,128]{2,1,0:T(8,128)(2,1)}, bf16[2,64,128]{2,1,0:T(8,128)(2,1)S(1)}, u32[]{:S(2)}) copy-start(bf16[2,64,128]{2,1,0:T(8,128)(2,1)S(1)} %get-tuple-element.42.grad_ref) | copy-start | bytes 98308
  187.1 13.0 %all-to-all-start.4 = ((bf16[32,32,128]{2,1,0:T(8,128)(2,1)}), bf16[32,32,128]{2,1,0:T(8,128)(2,1)S(1)}, u32[]{:S(2)}, u32[]{:S(2)}) async-start(bf16[32,32,128]{2,1,0:T(8,128)(2,1)} %final_part.1), calls=%async_computation.4 | async-start | bytes 524288 | tf_op jit(solution)/shard_map/all_to_all | solution.py:463
  (1 other events, 0.6 us)
Sparse Core Ops, SparseCore 0:
  15.4 76.4 all-gather.3

commit v5 on v3

--- a/solution.py
+++ b/solution.py
@@ -22,6 +22,7 @@
 
 VMEM = pl.BlockSpec(memory_space=pltpu.VMEM)
 SMEM = pl.BlockSpec(memory_space=pltpu.SMEM)
+HBM = pl.BlockSpec(memory_space=pltpu.HBM)
 
 
 def dot(left, right, dims=NN):
@@ -98,6 +99,14 @@
     )(send, feat, wk, wv)
 
 
+def rows_kernel(wo_ref, wl_ref, cot_ref, out_ref):
+    half = D // 2
+    start = pl.multiple_of(lax.rem(lax.axis_index("grid"), 2) * half, half)
+    out_ref[0:D] = wo_ref[...]
+    out_ref[D : D + half] = wl_ref[pl.ds(start, half)]
+    out_ref[D + half :] = cot_ref[...]
+
+
 def query_kernel(mesh_ref, wq_ref, out_ref):
     for b in range(out_ref.shape[0]):
         unit, _ = normalize(mesh_ref[b * B : (b + 1) * B].astype(f32))
@@ -179,7 +188,7 @@
         both = dot(unit, w_layer, NT).astype(bf16)
         pack_ref[rows] = both[:, : 2 * D]
         queries.append((both[:, 2 * D :].astype(f32) * score_scale).astype(bf16))
-        cot = gathered_ref[half * b : half * (b + 1), 2 * D :, :].reshape(B, C)
+        cot = gathered_ref[half * b : half * (b + 1), D + D // 2 :, :].reshape(B, C)
         grads.append(dot(cot, wl_ref[...], NT).astype(bf16))
     tail_ref[:height] = enc_ref[pl.ds(pl.multiple_of(at_ref[0] * height, height), height), :]
     pack_ref[2 * B : 3 * B] = jnp.concatenate(queries, axis=1)
@@ -196,18 +205,24 @@
     pack_ref[4 * B : 4 * B + 32] = jnp.concatenate(tail, axis=0).astype(bf16)
 
 
-def side_kernel(gathered_ref, unit_ref, tail_ref, wo_ref, cot_ref, unit_out_ref, inv_out_ref, sum_ref):
+def side_kernel(
+    gathered_ref, unit_ref, tail_ref, wo_ref,
+    cot_ref, unit_out_ref, inv_out_ref, sum_ref, half_ref, sem_ref,
+):
+    copy = pltpu.make_async_copy(gathered_ref.at[:, D : D + D // 2, :], half_ref, sem_ref)
+    copy.start()
     half = gathered_ref.shape[0] // 2
     weight = wo_ref[...]
     for b in range(2):
         rows = slice(b * B, (b + 1) * B)
-        cot = gathered_ref[half * b : half * (b + 1), 2 * D :, :].reshape(B, C)
+        cot = gathered_ref[half * b : half * (b + 1), D + D // 2 :, :].reshape(B, C)
         cot_ref[b] = dot(weight, cot, NT)
         unit_out_ref[b] = dot(weight, unit_ref[rows], NT)
         inv_out_ref[b] = tail_ref[tail_ref.shape[0] - 8 :, b * B : (b + 1) * B]
     sum_ref[...] = jnp.broadcast_to(
         jnp.sum(weight.astype(f32), axis=1, keepdims=True), sum_ref.shape
     )
+    copy.wait()
 
 
 def layer_kernel(
@@ -363,10 +378,15 @@
         out_ref[c * per : (c + 1) * per] = part.astype(bf16).reshape(per, height, 2 * D)
 
 
-def output_kernel(heads_ref, weight_ref, tail_ref, out_ref):
+def output_kernel(me_ref, heads_ref, mine_ref, other_ref, tail_ref, out_ref):
     total = tail_ref[: out_ref.shape[0]]
+    even = lax.rem(me_ref[0], 2) == 0
+    half = D // 2
     for h in range(heads_ref.shape[0]):
-        total = total + dot(heads_ref[h, 2 * D :][:, :D], weight_ref[h, D : 2 * D])
+        rows = heads_ref[h, 2 * D :][:, :D]
+        low = jnp.where(even, mine_ref[h], other_ref[h])
+        high = jnp.where(even, other_ref[h], mine_ref[h])
+        total = total + dot(rows[:, :half], low) + dot(rows[:, half:], high)
     out_ref[...] = total.astype(bf16)
 
 
@@ -412,12 +432,11 @@
     forward = [(i, (i + 1) % shards) for i in range(shards)]
     backward = [(t, s) for s, t in forward]
 
-    gathered = lax.all_gather(
-        jnp.concatenate([enc_out_weight, layer_out_weight, cotangent], axis=0),
-        "head",
-        axis=0,
-        tiled=False,
-    )
+    half = D // 2
+    shared_rows = call(
+        rows_kernel, struct((D + half + share, C), bf16), [VMEM] * 3, name="rows_part", mib=61
+    )(enc_out_weight, layer_out_weight, cotangent)
+    gathered = lax.all_gather(shared_rows, "head", axis=0, tiled=False)
     query_weight, key_weight, value_weight, layer_query, layer_key, layer_value = (
         weight.T
         for weight in (query_weight, key_weight, value_weight, layer_query, layer_key, layer_value)
@@ -451,15 +470,18 @@
     )
     left = lax.ppermute(pack, "grid", forward)
     right = lax.ppermute(pack, "grid", backward)
-    cot_part, unit_part, inverse_row, weight_sum = call(
+    cot_part, unit_part, inverse_row, weight_sum, half_mine = call(
         side_kernel,
         (
             struct((2, D, B), f32),
             struct((2, D, B), f32),
             struct((2, 8, B), f32),
             struct((D, B), f32),
+            struct((parts, half, C), bf16),
         ),
         [VMEM] * 4,
+        [pltpu.SemaphoreType.DMA],
+        out_specs=(VMEM, VMEM, VMEM, VMEM, HBM),
         name="side_part",
     )(gathered, unit, tail, enc_out_weight)
     mixed = call(
@@ -481,7 +503,10 @@
         edge_slot, edge_count, enc_table, shard_at, arrived_grad, cot_part, unit_part,
         inverse_row, weight_sum, wide_heads, lse, queries, own_kv, arrived_kv,
     )
+    half_mine, _ = lax.optimization_barrier((half_mine, send_grad))
+    half_other = lax.ppermute(half_mine, "grid", [(i, i ^ 1) for i in range(shards)])
     back_grad = exchange(send_grad, "grid")
+    back_grad, half_other = lax.optimization_barrier((back_grad, half_other))
     product = call(
         final_kernel,
         struct((shards, C // shards, 2 * D), bf16),
@@ -493,9 +518,9 @@
     mesh_out = call(
         output_kernel,
         struct((share, C), bf16),
-        [VMEM] * 3,
+        [SMEM] + [VMEM] * 4,
         name="output_part",
-    )(arrived_grad, gathered, tail)
+    )(shard_at, arrived_grad, half_mine, half_other, tail)
     key_grad, value_grad = call(
         sum_kernel,
         (struct((C // shards, D), f32), struct((C // shards, D), f32)),

time: 206 us -> 205 us (level)
  starting transfers between devices: 32.2 us -> 47 us
  blocking collectives: 67.1 us -> 58.5 us
  waiting for transfers between devices: 52.8 us -> 47.4 us
    ppermute x0 -> x1, starting transfers between devices: none -> 12.2 us  [on_device(): lax.ppermute(half_mine, 'grid', [(i, i ^ 1) for i in range(shards)])]
    all_to_all x1, blocking collectives: 32.3 us -> 22.6 us  [exchange(): return lax.all_to_all(array, axis, split_axis=0, concat_axis=0, tiled=True)]
    all_gather x1, waiting for transfers between devices: 8.77 us -> 2.03 us  [on_device(): gathered = lax.all_gather(shared_rows, 'head', axis=0, tiled=False)]
    unnamed x44 -> x46, local copies, waits for them, and re-layouts: 8.33 us -> 6.37 us
  transfers between devices with their start and end apart: 6 -> 7, of which waited for: 6 -> 6; matrix products, arithmetic and copies ran while one was open for 0% -> 0% of each run, Pallas kernels for 6% -> 7%
where the time goes in v5:
time: 205 us; the launch traced here: 204 us
  blocking collectives  58.5 us (29%)
  waiting for transfers between devices  47.4 us (23%)
  starting transfers between devices  47 us (23%)
  Pallas kernels  30.7 us (15%)
  between operations  14.3 us (7%)
  local copies, waits for them, and re-layouts  6.37 us (3%)
    all_to_all x3, waiting for transfers between devices, exchange(): return lax.all_to_all(array, axis, split_axis=0, concat_axis=0, tiled=True)  43.3 us
    all_gather x1, blocking collectives, on_device(): all_heads = lax.all_gather(enc_heads, 'head', axis=0, tiled=False)  35.9 us
    all_to_all x1, blocking collectives, exchange(): return lax.all_to_all(array, axis, split_axis=0, concat_axis=0, tiled=True)  22.6 us
    all_to_all x3, starting transfers between devices, exchange(): return lax.all_to_all(array, axis, split_axis=0, concat_axis=0, tiled=True)  21.3 us
    ppermute x1, starting transfers between devices, on_device(): lax.ppermute(half_mine, 'grid', [(i, i ^ 1) for i in range(shards)])  12.2 us
    ppermute x1, starting transfers between devices, on_device(): right = lax.ppermute(pack, 'grid', backward)  10.1 us
    unnamed x46, local copies, waits for them, and re-layouts  6.37 us
    pallas_call x1, Pallas kernels, on_device(): call(encoder_kernel, (struct((2, D, B), f32), struct((2, D, B), bf16), st...  5.59 us
  transfers between devices with their start and end apart: 7, of which 6 were waited for; matrix products, arithmetic and copies ran while one was open for 0% of the time, Pallas kernels for 7%

profile of v5, /device:TPU:1, one launch (start us, length us, event | category | flops | bytes accessed | tf_op | source)
XLA Modules:
  0.0 204.3 jit_solution(10447842957513012379)
XLA Ops:
  7.2 1.7 rows_part.1
  9.0 5.6 %grid_part.1 = (bf16[1024,1024]{1,0:T(8,128)(2,1)}, bf16[8,128,128]{2,1,0:T(8,128)(2,1)}, bf16[32,128,128]{2,1,0:T(8,128)(2,1)}) custom-call(s32[32]{0:T(128)} %bitcast.26, bf16[1024,1024]{1,0:T(8,128)(2,1)} %feat_ref.1, bf16[64,1024]{1,0:T(8,128)(2,1)} %bitcast.29, bf16[64,1024]{1,0:T(8,128)(2,1)} %bitcast.30), custom_call_target="tpu_custom_call" | custom-call | flops 268435456 | bytes 6291456 | tf_op jit(solution)/shard_map/grid_part/pallas_call | solution.py:75
  14.6 10.6 %all-to-all-start = ((bf16[32,128,128]{2,1,0:T(8,128)(2,1)}), bf16[32,128,128]{2,1,0:T(8,128)(2,1)S(1)}, u32[]{:S(2)}, u32[]{:S(2)}) async-start(bf16[32,128,128]{2,1,0:T(8,128)(2,1)} %get-tuple-element.25), calls=%async_computation | async-start | bytes 2097152 | tf_op jit(solution)/shard_map/all_to_all | solution.py:402
  25.8 16.7 %all-to-all-done.arrived_ref = bf16[32,128,128]{2,1,0:T(8,128)(2,1)S(1)} async-done(((bf16[32,128,128]{2,1,0:T(8,128)(2,1)}), bf16[32,128,128]{2,1,0:T(8,128)(2,1)S(1)}, u32[]{:S(2)}, u32[]{:S(2)}) %all-to-all-start) | async-done | bytes 1048608 | tf_op jit(solution)/shard_map/all_to_all | solution.py:402
  42.5 5.6 %encoder_part.1 = (f32[2,64,128]{2,1,0:T(8,128)S(1)}, bf16[2,64,128]{2,1,0:T(8,128)(2,1)S(1)}, f32[2,8,128]{2,1,0:T(8,128)S(1)}) custom-call(s32[2,30]{1,0:T(2,128)S(1)} %copy-done.18, s32[2]{0:T(128)S(1)} %copy-done.20, f32[2,30]{1,0:T(2,128)S(1)} %bitcast.24, bf16[8,128,128]{2,1,0:T(8,128)(2,1)S(1)} %copy-done.7, ...), custom_call_target="tpu_custom_call" | custom-call | flops 67108864 | bytes 4194304 | tf_op jit(solution)/shard_map/encoder_part/pallas_call | solution.py:450
  48.7 35.9 %all-gather = bf16[32,64,128]{2,1,0:T(8,128)(2,1)S(1)} all-gather(bf16[2,64,128]{2,1,0:T(8,128)(2,1)S(1)} %get-tuple-element.26), channel_id=2, replica_groups=mesh['grid'=32,'head'=16] {'head'}, dimensions={0}, use_global_device_ids=true | all-gather | bytes 557056 | tf_op jit(solution)/shard_map/all_gather | solution.py:457
  84.6 2.0 all-gather.4.cloned.1.call-done
  86.7 2.0 copy-done
  88.7 2.3 %middle_part.1 = (bf16[544,128]{1,0:T(8,128)(2,1)S(1)}, f32[24,1024]{1,0:T(8,128)S(1)}, bf16[256,1024]{1,0:T(8,128)(2,1)S(1)}) custom-call(s32[1]{0:T(128)} %bitcast.1.at_ref, f32[2,3]{1,0:T(2,128)S(1)} %bitcast.28, bf16[16,2,64,128]{3,2,1,0:T(8,128)(2,1)S(1)} %bitcast.16, bf16[16,112,1024]{2,1,0:T(8,128)(2,1)S(1)} %bitcast.13, ...), custom_call_target="tpu_custom_call" | custom-call | flops 67108864 | bytes 4194304 | tf_op jit(solution)/shard_map/middle_part/pallas_call | solution.py:458
  91.7 10.1 %collective-permute-start.1 = (bf16[544,128]{1,0:T(8,128)(2,1)S(1)}, bf16[544,128]{1,0:T(8,128)(2,1)S(1)}, u32[]{:S(2)}, u32[]{:S(2)}) collective-permute-start(bf16[544,128]{1,0:T(8,128)(2,1)S(1)} %get-tuple-element.27.own_ref), channel_id=1, source_target_pairs={{16,0},{32,16},{48,32},{64,48},{80,64},{96,80},{112,96},{128,112},... | collective-permute-start | bytes 417800 | tf_op jit(solution)/shard_map/ppermute | solution.py:472
  101.9 3.3 %collective-permute-start = (bf16[544,128]{1,0:T(8,128)(2,1)S(1)}, bf16[544,128]{1,0:T(8,128)(2,1)S(1)}, u32[]{:S(2)}, u32[]{:S(2)}) collective-permute-start(bf16[544,128]{1,0:T(8,128)(2,1)S(1)} %get-tuple-element.27.own_ref), channel_id=1, source_target_pairs={{0,16},{16,32},{32,48},{48,64},{64,80},{80,96},{96,112},{112,128},... | collective-permute-start | bytes 417800 | tf_op jit(solution)/shard_map/ppermute | solution.py:471
  106.0 1.2 collective-permute-done.left_ref
  107.2 4.9 %layer_part.1 = bf16[16,144,128]{2,1,0:T(8,128)(2,1)} custom-call(bf16[544,128]{1,0:T(8,128)(2,1)S(1)} %get-tuple-element.27.own_ref, bf16[544,128]{1,0:T(8,128)(2,1)S(1)} %collective-permute-done.left_ref, bf16[544,128]{1,0:T(8,128)(2,1)S(1)} %collective-permute-done.1.right_ref, bf16[256,1024]{1,0:T(8,128)(2,1)S(1)} %get-tuple-element.28.unit_ref, ...), custom_call_target="tpu_custom_call" | custom-call | flops 67108864 | bytes 4194304 | tf_op jit(solution)/shard_map/layer_part/pallas_call | solution.py:487
  112.1 6.8 %all-to-all-start.1 = ((bf16[16,144,128]{2,1,0:T(8,128)(2,1)}), bf16[16,144,128]{2,1,0:T(8,128)(2,1)S(1)}, u32[]{:S(2)}, u32[]{:S(2)}) async-start(bf16[16,144,128]{2,1,0:T(8,128)(2,1)} %layer_part.1), calls=%async_computation.1 | async-start | bytes 1179648 | tf_op jit(solution)/shard_map/all_to_all | solution.py:402
  118.9 2.0 copy-done.2
  121.5 1.0 copy-done.5
  122.5 18.8 %all-to-all-done.1.arrived_grad_ref.heads_ref = bf16[16,144,128]{2,1,0:T(8,128)(2,1)S(1)} async-done(((bf16[16,144,128]{2,1,0:T(8,128)(2,1)}), bf16[16,144,128]{2,1,0:T(8,128)(2,1)S(1)}, u32[]{:S(2)}, u32[]{:S(2)}) %all-to-all-start.1) | async-done | bytes 589856 | tf_op jit(solution)/shard_map/all_to_all | solution.py:402
  141.3 5.6 %back_part.1 = (f32[8,128,128]{2,1,0:T(8,128)S(1)}, bf16[32,128,128]{2,1,0:T(8,128)(2,1)S(1)}) custom-call(s32[2,30]{1,0:T(2,128)S(1)} %copy-done.18, s32[2]{0:T(128)S(1)} %copy-done.20, f32[2,30]{1,0:T(2,128)S(1)} %bitcast.25, s32[1]{0:T(128)} %bitcast.me_ref, bf16[16,144,128]{2,1,0:T(8,128)(2,1)S(1)} %all-to-all-done.1.arrived_grad_ref.heads_ref, ...), custom_call_target="tpu_custom_call" | custom-call | flops 67108864 | bytes 4194304 | tf_op jit(solution)/shard_map/back_part/pallas_call | solution.py:491
  146.9 12.2 %collective-permute-start.2 = (bf16[16,32,1024]{2,1,0:T(8,128)(2,1)S(1)}, bf16[16,32,1024]{2,1,0:T(8,128)(2,1)S(1)}, u32[]{:S(2)}, u32[]{:S(2)}) collective-permute-start(bf16[16,32,1024]{2,1,0:T(8,128)(2,1)S(1)} %copy-done.6), channel_id=1, source_target_pairs={{0,16},{16,0},{32,48},{48,32},{64,80},{80,64},{96,112},{112,96},{1... | collective-permute-start | bytes 3145736 | tf_op jit(solution)/shard_map/ppermute | solution.py:507
  159.0 22.6 %all_to_all.20.back_ref = bf16[32,128,128]{2,1,0:T(8,128)(2,1)S(1)} all-to-all(bf16[32,128,128]{2,1,0:T(8,128)(2,1)S(1)} %get-tuple-element.37), channel_id=1, replica_groups=mesh['grid'=32,'head'=16] {'grid'}, dimensions={0} | all-to-all | bytes 2097152 | tf_op jit(solution)/shard_map/all_to_all | solution.py:402
  181.7 2.1 %final_part.1 = bf16[32,32,128]{2,1,0:T(8,128)(2,1)} custom-call(s32[32]{0:T(128)S(1)} %bitcast.27, bf16[1024,1024]{1,0:T(8,128)(2,1)S(1)} %copy-done.4, f32[8,128,128]{2,1,0:T(8,128)S(1)} %get-tuple-element.41.own_ref, bf16[32,128,128]{2,1,0:T(8,128)(2,1)S(1)} %all_to_all.20.back_ref), custom_call_target="tpu_custom_call" | custom-call | flops 67108864 | bytes 4194304 | tf_op jit(solution)/shard_map/final_part/pallas_call | solution.py:510
  183.8 3.9 %all-to-all-start.3 = ((bf16[32,32,128]{2,1,0:T(8,128)(2,1)}), bf16[32,32,128]{2,1,0:T(8,128)(2,1)S(1)}, u32[]{:S(2)}, u32[]{:S(2)}) async-start(bf16[32,32,128]{2,1,0:T(8,128)(2,1)} %final_part.1), calls=%async_computation.3 | async-start | bytes 524288 | tf_op jit(solution)/shard_map/all_to_all | solution.py:402
  187.7 1.1 output_part.1
  188.8 7.9 %all-to-all-done.3.parts_ref = bf16[32,32,128]{2,1,0:T(8,128)(2,1)S(1)} async-done(((bf16[32,32,128]{2,1,0:T(8,128)(2,1)}), bf16[32,32,128]{2,1,0:T(8,128)(2,1)S(1)}, u32[]{:S(2)}, u32[]{:S(2)}) %all-to-all-start.3) | async-done | bytes 262176 | tf_op jit(solution)/shard_map/all_to_all | solution.py:402
  (50 shorter events, 4.1 us)
Async XLA Ops:
  7.2 79.5 %all-gather.4.cloned.1.call-start = ((), (), s32[]{:S(2)}) async-start(), calls=%async_computation.4 | async-start | bytes 3899392 | tf_op jit(solution)/shard_map/all_gather | solution.py:439
  8.9 16.3 %copy-start.3 = (bf16[256,1024]{1,0:T(8,128)(2,1)S(1)}, bf16[256,1024]{1,0:T(8,128)(2,1)}, u32[]{:S(2)}) copy-start(bf16[256,1024]{1,0:T(8,128)(2,1)} %mesh_ref.3) | copy-start | bytes 1572868
  8.9 16.3 %copy-start.15 = (bf16[1024,64]{0,1:T(8,128)(2,1)S(1)}, bf16[1024,64]{0,1:T(8,128)(2,1)}, u32[]{:S(2)}) copy-start(bf16[1024,64]{0,1:T(8,128)(2,1)} %param.18) | copy-start | bytes 393220
  8.9 33.6 %copy-start.18 = (s32[2,30]{1,0:T(2,128)S(1)}, s32[2,30]{1,0:T(2,128)}, u32[]{:S(2)}) copy-start(s32[2,30]{1,0:T(2,128)} %slot_ref.3) | copy-start | bytes 724
  8.9 33.6 %copy-start.19 = (f32[2,30,1]{1,2,0:T(1,128)S(1)}, f32[2,30,1]{1,2,0:T(1,128)}, u32[]{:S(2)}) copy-start(f32[2,30,1]{1,2,0:T(1,128)} %param.26) | copy-start | bytes 724
  8.9 33.6 %copy-start.20 = (s32[2]{0:T(128)S(1)}, s32[2]{0:T(128)}, u32[]{:S(2)}) copy-start(s32[2]{0:T(128)} %count_ref.3) | copy-start | bytes 28
  14.5 28.0 %copy-start.7 = (bf16[8,128,128]{2,1,0:T(8,128)(2,1)S(1)}, bf16[8,128,128]{2,1,0:T(8,128)(2,1)}, u32[]{:S(2)}) copy-start(bf16[8,128,128]{2,1,0:T(8,128)(2,1)} %get-tuple-element.24.own_ref) | copy-start | bytes 786436
  14.5 72.1 %copy-start.8 = (bf16[1024,64]{0,1:T(8,128)(2,1)S(1)}, bf16[1024,64]{0,1:T(8,128)(2,1)}, u32[]{:S(2)}) copy-start(bf16[1024,64]{0,1:T(8,128)(2,1)} %param.22) | copy-start | bytes 393220
  14.6 72.1 %copy-start.9 = (bf16[1024,64]{0,1:T(8,128)(2,1)S(1)}, bf16[1024,64]{0,1:T(8,128)(2,1)}, u32[]{:S(2)}) copy-start(bf16[1024,64]{0,1:T(8,128)(2,1)} %param.23) | copy-start | bytes 393220
  14.6 72.1 %copy-start.10 = (bf16[1024,64]{0,1:T(8,128)(2,1)S(1)}, bf16[1024,64]{0,1:T(8,128)(2,1)}, u32[]{:S(2)}) copy-start(bf16[1024,64]{0,1:T(8,128)(2,1)} %param.24) | copy-start | bytes 393220
  14.6 72.1 %copy-start.11 = (bf16[64,1024]{1,0:T(8,128)(2,1)S(1)}, bf16[64,1024]{1,0:T(8,128)(2,1)}, u32[]{:S(2)}) copy-start(bf16[64,1024]{1,0:T(8,128)(2,1)} %wl_ref.3) | copy-start | bytes 393220
  14.6 72.1 %copy-start.22 = (f32[2,3,1]{1,2,0:T(1,128)S(1)}, f32[2,3,1]{1,2,0:T(1,128)}, u32[]{:S(2)}) copy-start(f32[2,3,1]{1,2,0:T(1,128)} %param.27) | copy-start | bytes 76
  14.6 27.9 %all-to-all-start = ((bf16[32,128,128]{2,1,0:T(8,128)(2,1)}), bf16[32,128,128]{2,1,0:T(8,128)(2,1)S(1)}, u32[]{:S(2)}, u32[]{:S(2)}) async-start(bf16[32,128,128]{2,1,0:T(8,128)(2,1)} %get-tuple-element.25), calls=%async_computation | async-start | bytes 2097152 | tf_op jit(solution)/shard_map/all_to_all | solution.py:402
  88.7 18.5 %copy-start.1 = (bf16[1792,1024]{1,0:T(8,128)(2,1)S(1)}, bf16[1792,1024]{1,0:T(8,128)(2,1)}, u32[]{:S(2)}) copy-start(bf16[1792,1024]{1,0:T(8,128)(2,1)} %all-gather.4.cloned.1.call-done) | copy-start | bytes 11010052
  91.7 14.3 %collective-permute-start.1 = (bf16[544,128]{1,0:T(8,128)(2,1)S(1)}, bf16[544,128]{1,0:T(8,128)(2,1)S(1)}, u32[]{:S(2)}, u32[]{:S(2)}) collective-permute-start(bf16[544,128]{1,0:T(8,128)(2,1)S(1)} %get-tuple-element.27.own_ref), channel_id=1, source_target_pairs={{16,0},{32,16},{48,32},{64,48},{80,64},{96,80},{112,96},{128,112},... | collective-permute-start | bytes 417800 | tf_op jit(solution)/shard_map/ppermute | solution.py:472
  101.9 5.3 %collective-permute-start = (bf16[544,128]{1,0:T(8,128)(2,1)S(1)}, bf16[544,128]{1,0:T(8,128)(2,1)S(1)}, u32[]{:S(2)}, u32[]{:S(2)}) collective-permute-start(bf16[544,128]{1,0:T(8,128)(2,1)S(1)} %get-tuple-element.27.own_ref), channel_id=1, source_target_pairs={{0,16},{16,32},{32,48},{48,64},{64,80},{80,96},{96,112},{112,128},... | collective-permute-start | bytes 417800 | tf_op jit(solution)/shard_map/ppermute | solution.py:471
  107.2 11.7 %copy-start.12 = (bf16[64,1024]{1,0:T(8,128)(2,1)S(1)}, bf16[64,1024]{1,0:T(8,128)(2,1)}, u32[]{:S(2)}) copy-start(bf16[64,1024]{1,0:T(8,128)(2,1)} %wo_ref.3) | copy-start | bytes 393220
  107.2 11.7 %copy-start.14 = (f32[24,1024]{1,0:T(8,128)S(1)}, f32[24,1024]{1,0:T(8,128)}, u32[]{:S(2)}) copy-start(f32[24,1024]{1,0:T(8,128)} %copy-done.13) | copy-start | bytes 294916
  112.1 29.2 %all-to-all-start.1 = ((bf16[16,144,128]{2,1,0:T(8,128)(2,1)}), bf16[16,144,128]{2,1,0:T(8,128)(2,1)S(1)}, u32[]{:S(2)}, u32[]{:S(2)}) async-start(bf16[16,144,128]{2,1,0:T(8,128)(2,1)} %layer_part.1), calls=%async_computation.1 | async-start | bytes 1179648 | tf_op jit(solution)/shard_map/all_to_all | solution.py:402
  120.9 20.3 %copy-start.17 = (f32[2,64,128]{2,1,0:T(8,128)S(1)}, f32[2,64,128]{2,1,0:T(8,128)}, u32[]{:S(2)}) copy-start(f32[2,64,128]{2,1,0:T(8,128)} %copy-done.16) | copy-start | bytes 196612
  141.3 40.4 %copy-start.4 = (bf16[1024,1024]{1,0:T(8,128)(2,1)S(1)}, bf16[1024,1024]{1,0:T(8,128)(2,1)}, u32[]{:S(2)}) copy-start(bf16[1024,1024]{1,0:T(8,128)(2,1)} %get-tuple-element.40.norm_ref) | copy-start | bytes 6291460
  141.3 40.4 %copy-start.21 = (s32[1,32]{1,0:T(1,128)S(1)}, s32[1,32]{1,0:T(1,128)}, u32[]{:S(2)}) copy-start(s32[1,32]{1,0:T(1,128)} %param.28) | copy-start | bytes 388
  146.9 34.8 %collective-permute-start.2 = (bf16[16,32,1024]{2,1,0:T(8,128)(2,1)S(1)}, bf16[16,32,1024]{2,1,0:T(8,128)(2,1)S(1)}, u32[]{:S(2)}, u32[]{:S(2)}) collective-permute-start(bf16[16,32,1024]{2,1,0:T(8,128)(2,1)S(1)} %copy-done.6), channel_id=1, source_target_pairs={{0,16},{16,0},{32,48},{48,32},{64,80},{80,64},{96,112},{112,96},{1... | collective-permute-start | bytes 3145736 | tf_op jit(solution)/shard_map/ppermute | solution.py:507
  183.8 12.9 %all-to-all-start.3 = ((bf16[32,32,128]{2,1,0:T(8,128)(2,1)}), bf16[32,32,128]{2,1,0:T(8,128)(2,1)S(1)}, u32[]{:S(2)}, u32[]{:S(2)}) async-start(bf16[32,32,128]{2,1,0:T(8,128)(2,1)} %final_part.1), calls=%async_computation.3 | async-start | bytes 524288 | tf_op jit(solution)/shard_map/all_to_all | solution.py:402
  (6 other events, 11.9 us)
Sparse Core Ops, SparseCore 0:
  10.1 76.5 all-gather.3

commit v6 on v4

--- a/solution.py
+++ b/solution.py
@@ -99,20 +99,12 @@
     )(send, feat, wk, wv)
 
 
-def rows_kernel(wo_ref, wl_ref, cot_ref, out_ref, sem_ref):
+def rows_kernel(wo_ref, wl_ref, cot_ref, out_ref):
     half = D // 2
     start = pl.multiple_of(lax.rem(lax.axis_index("grid"), 2) * half, half)
-    copies = [
-        pltpu.make_async_copy(wo_ref, out_ref.at[0:D], sem_ref.at[0]),
-        pltpu.make_async_copy(
-            wl_ref.at[pl.ds(start, half)], out_ref.at[D : D + half], sem_ref.at[1]
-        ),
-        pltpu.make_async_copy(cot_ref, out_ref.at[D + half :], sem_ref.at[2]),
-    ]
-    for copy in copies:
-        copy.start()
-    for copy in copies:
-        copy.wait()
+    out_ref[0:D] = wo_ref[...]
+    out_ref[D : D + half] = wl_ref[pl.ds(start, half)]
+    out_ref[D + half :] = cot_ref[...]
 
 
 def query_kernel(mesh_ref, wq_ref, out_ref):
@@ -203,31 +195,10 @@
 
 def middle_kernel(
     at_ref, bias_ref, heads_ref, gathered_ref, mesh_ref, wq_ref, wk_ref, wv_ref, wl_ref,
-    pack_ref, tail_ref, unit_ref, enc_ref, w_out_ref, cot_ref, sem_ref,
+    pack_ref, tail_ref, unit_ref, enc_ref,
 ):
     parts = heads_ref.shape[0]
-    first = parts // 2
-    copies = [
-        pltpu.make_async_copy(
-            gathered_ref.at[0:first, 0:D, :], w_out_ref.at[0:first], sem_ref.at[0]
-        ),
-        pltpu.make_async_copy(
-            gathered_ref.at[first:parts, 0:D, :], w_out_ref.at[first:parts], sem_ref.at[1]
-        ),
-        pltpu.make_async_copy(
-            gathered_ref.at[:, D + D // 2 :, :], cot_ref, sem_ref.at[2]
-        ),
-    ]
-    for copy in copies:
-        copy.start()
-    copies[0].wait()
-    for b in range(2):
-        rows = slice(b * B, (b + 1) * B)
-        heads = heads_ref[0:first, b].reshape(first * D, B)
-        w_out = w_out_ref[0:first].reshape(first * D, C)
-        enc_ref[rows] = mesh_ref[rows].astype(f32) + dot(heads, w_out, TN)
-    copies[1].wait()
-    copies[2].wait()
+    w_out = gathered_ref[:, 0:D, :].reshape(parts * D, C)
     w_layer = jnp.concatenate([wk_ref[...], wv_ref[...], wq_ref[...]], axis=0)
     half = parts // 2
     height = 2 * B // parts
@@ -235,9 +206,8 @@
     queries, grads = [], []
     for b in range(2):
         rows = slice(b * B, (b + 1) * B)
-        heads = heads_ref[first:, b].reshape((parts - first) * D, B)
-        w_out = w_out_ref[first:].reshape((parts - first) * D, C)
-        enc = enc_ref[rows] + dot(heads, w_out, TN)
+        heads = heads_ref[:, b].reshape(parts * D, B)
+        enc = mesh_ref[rows].astype(f32) + dot(heads, w_out, TN)
         enc_ref[rows] = enc
         unit, inverse = normalize(enc)
         unit = unit.astype(bf16)
@@ -246,7 +216,7 @@
         both = dot(unit, w_layer, NT).astype(bf16)
         pack_ref[rows] = both[:, : 2 * D]
         queries.append((both[:, 2 * D :].astype(f32) * score_scale).astype(bf16))
-        cot = cot_ref[half * b : half * (b + 1)].reshape(B, C)
+        cot = gathered_ref[half * b : half * (b + 1), D + D // 2 :, :].reshape(B, C)
         grads.append(dot(cot, wl_ref[...], NT).astype(bf16))
     tail_ref[:height] = enc_ref[pl.ds(pl.multiple_of(at_ref[0] * height, height), height), :]
     pack_ref[2 * B : 3 * B] = jnp.concatenate(queries, axis=1)
@@ -263,7 +233,12 @@
     pack_ref[4 * B : 4 * B + 32] = jnp.concatenate(tail, axis=0).astype(bf16)
 
 
-def side_kernel(gathered_ref, unit_ref, tail_ref, wo_ref, cot_ref, unit_out_ref, inv_out_ref, sum_ref, half_ref):
+def side_kernel(
+    gathered_ref, unit_ref, tail_ref, wo_ref,
+    cot_ref, unit_out_ref, inv_out_ref, sum_ref, half_ref, sem_ref,
+):
+    copy = pltpu.make_async_copy(gathered_ref.at[:, D : D + D // 2, :], half_ref, sem_ref)
+    copy.start()
     half = gathered_ref.shape[0] // 2
     weight = wo_ref[...]
     for b in range(2):
@@ -275,15 +250,12 @@
     sum_ref[...] = jnp.broadcast_to(
         jnp.sum(weight.astype(f32), axis=1, keepdims=True), sum_ref.shape
     )
-    half_ref[...] = gathered_ref[:, D : D + D // 2, :]
+    copy.wait()
 
 
 def layer_kernel(
-    own_ref, left_ref, right_ref, unit_ref, wq_ref, wk_ref, wv_ref, gathered_ref, send_ref,
-    w_out_ref, sem_ref,
-):
-    copy = pltpu.make_async_copy(gathered_ref.at[:, 0:D, :], w_out_ref, sem_ref)
-    copy.start()
+    own_ref, left_ref, right_ref, unit_ref, wq_ref, wk_ref, wv_ref, gathered_ref, send_ref
+):
     zero = jnp.zeros((B, D), bf16)
 
     def block(ref, b):
@@ -356,9 +328,8 @@
     total = jnp.concatenate(totals, axis=0)
     heads = jnp.concatenate(heads, axis=0)
     share = heads.shape[0] // parts
-    copy.wait()
     for z in range(parts):
-        piece = dot(w_out_ref[z], total, NT).astype(bf16)
+        piece = dot(gathered_ref[z, 0:D, :], total, NT).astype(bf16)
         for b in range(2):
             send_ref[z, b * D : (b + 1) * D] = piece[:, b * B : (b + 1) * B]
         rows = heads[z * share : (z + 1) * share]
@@ -495,13 +466,7 @@
 
     half = D // 2
     shared_rows = call(
-        rows_kernel,
-        struct((D + half + share, C), bf16),
-        [HBM] * 3,
-        [pltpu.SemaphoreType.DMA((3,))],
-        name="rows_part",
-        mib=61,
-        out_specs=HBM,
+        rows_kernel, struct((D + half + share, C), bf16), [VMEM] * 3, name="rows_part", mib=61
     )(enc_out_weight, layer_out_weight, cotangent)
     gathered = lax.all_gather(shared_rows, "head", axis=0, tiled=False)
     query_weight, key_weight, value_weight, layer_query, layer_key, layer_value = (
@@ -535,21 +500,14 @@
             struct((share + 8, C), f32),
             struct((2 * B, C), bf16),
         ),
-        [SMEM] * 2 + [VMEM, HBM] + [VMEM] * 5,
-        [
-            pltpu.VMEM((2 * B, C), f32),
-            pltpu.VMEM((parts, D, C), bf16),
-            pltpu.VMEM((parts, share, C), bf16),
-            pltpu.SemaphoreType.DMA((3,)),
-        ],
+        [SMEM] * 2 + [VMEM] * 7,
+        [pltpu.VMEM((2 * B, C), f32)],
         name="middle_part",
-        mib=61,
     )(
         head_at, layer_table, all_heads, gathered, mesh_feat, layer_query, layer_key, layer_value, layer_out_weight
     )
     left = lax.ppermute(pack, "grid", forward)
     right = lax.ppermute(pack, "grid", backward)
-    arrived_early, left, right = lax.optimization_barrier((arrived_early, left, right))
     cot_part, unit_part, inverse_row, weight_sum, half_mine = call(
         side_kernel,
         (
@@ -560,17 +518,14 @@
             struct((parts, half, C), bf16),
         ),
         [VMEM] * 4,
+        [pltpu.SemaphoreType.DMA],
+        out_specs=(VMEM, VMEM, VMEM, VMEM, HBM),
         name="side_part",
     )(gathered, unit, tail, enc_out_weight)
-    half_other = lax.ppermute(half_mine, "grid", [(i, i ^ 1) for i in range(shards)])
     mixed = call(
-        layer_kernel,
-        struct((parts, 2 * D + share, B), bf16),
-        [VMEM] * 7 + [HBM],
-        [pltpu.VMEM((parts, D, C), bf16), pltpu.SemaphoreType.DMA],
-        name="layer_part",
-        mib=61,
+        layer_kernel, struct((parts, 2 * D + share, B), bf16), [VMEM] * 8, name="layer_part"
     )(pack, left, right, unit, layer_query, layer_key, layer_value, gathered)
+    arrived_early, mixed = lax.optimization_barrier((arrived_early, mixed))
     arrived_grad = exchange(mixed, "head")
     grads, send_grads = call(
         grad_kernel,
@@ -583,6 +538,7 @@
         inverse_row, weight_sum,
     )
     arrived_grads = exchange(send_grads, "grid")
+    half_other = lax.ppermute(half_mine, "grid", [(i, i ^ 1) for i in range(shards)])
     product = call(
         final_kernel,
         struct((shards, C // shards, 2 * D), bf16),

time: 209 us -> 198 us (0.947)
  Pallas kernels: 44.6 us -> 33.8 us
    pallas_call x2, Pallas kernels: 14.7 us -> 6.6 us  [the longest x1 4.92 us: on_device(): call(layer_kernel, struct((parts, 2 * D + share, B), bf16), [VMEM] * 8, n...]
    pallas_call x1, Pallas kernels: 5.21 us -> 2.32 us  [on_device(): call(middle_kernel, (struct((4 * B + 32, 2 * D), bf16), struct((share + 8...]
    unnamed x34 -> x38, local copies, waits for them, and re-layouts: 3.35 us -> 4.75 us
  transfers between devices with their start and end apart: 8 -> 8, of which waited for: 5 -> 5; matrix products, arithmetic and copies ran while one was open for 0% -> 0% of each run, Pallas kernels for 14% -> 16%
where the time goes in v6:
time: 198 us; the launch traced here: 197 us
  blocking collectives  62.1 us (31%)
  starting transfers between devices  43.6 us (22%)
  waiting for transfers between devices  38.1 us (19%)
  Pallas kernels  33.8 us (17%)
  between operations  14.3 us (7%)
  local copies, waits for them, and re-layouts  4.75 us (2%)
    all_to_all x4, waiting for transfers between devices, exchange(): return lax.all_to_all(array, axis, split_axis=0, concat_axis=0, tiled=True)  36.1 us
    all_gather x1, blocking collectives, on_device(): all_heads = lax.all_gather(enc_heads, 'head', axis=0, tiled=False)  34.7 us
    all_to_all x1, blocking collectives, exchange(): return lax.all_to_all(array, axis, split_axis=0, concat_axis=0, tiled=True)  27.3 us
    all_to_all x4, starting transfers between devices, exchange(): return lax.all_to_all(array, axis, split_axis=0, concat_axis=0, tiled=True)  25.5 us
    ppermute x1, starting transfers between devices, on_device(): right = lax.ppermute(pack, 'grid', backward)  7.99 us
    pallas_call x1, Pallas kernels, on_device(): call(encoder_kernel, (struct((2, D, B), bf16), struct((2, 8, B), f32), st...  7.13 us
    pallas_call x1, Pallas kernels, on_device(): call(final_kernel, struct((shards, C // shards, 2 * D), bf16), [SMEM] * 4...  6.96 us
    ppermute x1, starting transfers between devices, on_device(): lax.ppermute(half_mine, 'grid', [(i, i ^ 1) for i in range(shards)])  6.95 us
  transfers between devices with their start and end apart: 8, of which 5 were waited for; matrix products, arithmetic and copies ran while one was open for 0% of the time, Pallas kernels for 16%

profile of v6, /device:TPU:1, one launch (start us, length us, event | category | flops | bytes accessed | tf_op | source)
XLA Modules:
  0.0 196.7 jit_solution(3113675937782063273)
XLA Ops:
  7.2 1.7 rows_part.1
  9.0 5.6 %grid_part.1 = (bf16[1024,1024]{1,0:T(8,128)(2,1)}, bf16[8,128,128]{2,1,0:T(8,128)(2,1)}, bf16[32,128,128]{2,1,0:T(8,128)(2,1)}) custom-call(s32[32]{0:T(128)} %bitcast.30, bf16[1024,1024]{1,0:T(8,128)(2,1)} %feat_ref.1, bf16[64,1024]{1,0:T(8,128)(2,1)} %bitcast.28, bf16[64,1024]{1,0:T(8,128)(2,1)} %bitcast.29), custom_call_target="tpu_custom_call" | custom-call | flops 268435456 | bytes 6291456 | tf_op jit(solution)/shard_map/grid_part/pallas_call | solution.py:75
  14.6 10.6 %all-to-all-start = ((bf16[32,128,128]{2,1,0:T(8,128)(2,1)}), bf16[32,128,128]{2,1,0:T(8,128)(2,1)S(1)}, u32[]{:S(2)}, u32[]{:S(2)}) async-start(bf16[32,128,128]{2,1,0:T(8,128)(2,1)} %get-tuple-element.24), calls=%async_computation | async-start | bytes 2097152 | tf_op jit(solution)/shard_map/all_to_all | solution.py:434
  25.8 16.6 %all-to-all-done.arrived_ref = bf16[32,128,128]{2,1,0:T(8,128)(2,1)S(1)} async-done(((bf16[32,128,128]{2,1,0:T(8,128)(2,1)}), bf16[32,128,128]{2,1,0:T(8,128)(2,1)S(1)}, u32[]{:S(2)}, u32[]{:S(2)}) %all-to-all-start) | async-done | bytes 1048608 | tf_op jit(solution)/shard_map/all_to_all | solution.py:434
  42.6 7.1 %encoder_part.1 = (bf16[2,64,128]{2,1,0:T(8,128)(2,1)S(1)}, f32[2,8,128]{2,1,0:T(8,128)S(1)}, bf16[32,144,128]{2,1,0:T(8,128)(2,1)}) custom-call(s32[2,30]{1,0:T(2,128)S(1)} %copy-done.14, s32[2]{0:T(128)S(1)} %copy-done.17, f32[2,30]{1,0:T(2,128)S(1)} %bitcast.25, s32[1]{0:T(128)} %bitcast.me_ref, bf16[8,128,128]{2,1,0:T(8,128)(2,1)S(1)} %copy-done.4, ...), custom_call_target="tpu_custom_call" | custom-call | flops 67108864 | bytes 4194304 | tf_op jit(solution)/shard_map/encoder_part/pallas_call | solution.py:483
  50.3 4.7 %all-to-all-start.1 = ((bf16[32,144,128]{2,1,0:T(8,128)(2,1)}), bf16[32,144,128]{2,1,0:T(8,128)(2,1)}, u32[]{:S(2)}, u32[]{:S(2)}) async-start(bf16[32,144,128]{2,1,0:T(8,128)(2,1)} %get-tuple-element.25), calls=%async_computation.1 | async-start | bytes 2359296 | tf_op jit(solution)/shard_map/all_to_all | solution.py:434
  55.0 34.7 %all-gather = bf16[32,64,128]{2,1,0:T(8,128)(2,1)S(1)} all-gather(bf16[2,64,128]{2,1,0:T(8,128)(2,1)S(1)} %get-tuple-element.26.heads_ref), channel_id=2, replica_groups=mesh['grid'=32,'head'=16] {'head'}, dimensions={0}, use_global_device_ids=true | all-gather | bytes 557056 | tf_op jit(solution)/shard_map/all_gather | solution.py:495
  89.8 2.0 %copy-done = bf16[1792,1024]{1,0:T(8,128)(2,1)S(1)} copy-done((bf16[1792,1024]{1,0:T(8,128)(2,1)S(1)}, bf16[1792,1024]{1,0:T(8,128)(2,1)}, u32[]{:S(2)}) %copy-start) | copy-done | bytes 3670040
  91.8 2.3 %middle_part.1 = (bf16[544,128]{1,0:T(8,128)(2,1)S(1)}, f32[24,1024]{1,0:T(8,128)S(1)}, bf16[256,1024]{1,0:T(8,128)(2,1)S(1)}) custom-call(s32[1]{0:T(128)} %bitcast.6.at_ref, f32[2,3]{1,0:T(2,128)S(1)} %bitcast.27, bf16[16,2,64,128]{3,2,1,0:T(8,128)(2,1)S(1)} %bitcast.16, bf16[16,112,1024]{2,1,0:T(8,128)(2,1)S(1)} %bitcast.13, ...), custom_call_target="tpu_custom_call" | custom-call | flops 67108864 | bytes 4194304 | tf_op jit(solution)/shard_map/middle_part/pallas_call | solution.py:496
  94.1 8.0 %collective-permute-start.1 = (bf16[544,128]{1,0:T(8,128)(2,1)S(1)}, bf16[544,128]{1,0:T(8,128)(2,1)S(1)}, u32[]{:S(2)}, u32[]{:S(2)}) collective-permute-start(bf16[544,128]{1,0:T(8,128)(2,1)S(1)} %get-tuple-element.27.own_ref), channel_id=1, source_target_pairs={{16,0},{32,16},{48,32},{64,48},{80,64},{96,80},{112,96},{128,112},... | collective-permute-start | bytes 417800 | tf_op jit(solution)/shard_map/ppermute | solution.py:510
  102.1 3.1 %collective-permute-start = (bf16[544,128]{1,0:T(8,128)(2,1)S(1)}, bf16[544,128]{1,0:T(8,128)(2,1)S(1)}, u32[]{:S(2)}, u32[]{:S(2)}) collective-permute-start(bf16[544,128]{1,0:T(8,128)(2,1)S(1)} %get-tuple-element.27.own_ref), channel_id=1, source_target_pairs={{0,16},{16,32},{32,48},{48,64},{64,80},{80,96},{96,112},{112,128},... | collective-permute-start | bytes 417800 | tf_op jit(solution)/shard_map/ppermute | solution.py:509
  105.3 0.8 collective-permute-done.1.right_ref
  106.0 1.2 collective-permute-done.left_ref
  107.3 4.9 %layer_part.1 = bf16[16,144,128]{2,1,0:T(8,128)(2,1)} custom-call(bf16[544,128]{1,0:T(8,128)(2,1)S(1)} %get-tuple-element.27.own_ref, bf16[544,128]{1,0:T(8,128)(2,1)S(1)} %collective-permute-done.left_ref, bf16[544,128]{1,0:T(8,128)(2,1)S(1)} %collective-permute-done.1.right_ref, bf16[256,1024]{1,0:T(8,128)(2,1)S(1)} %get-tuple-element.28.unit_ref, ...), custom_call_target="tpu_custom_call" | custom-call | flops 67108864 | bytes 4194304 | tf_op jit(solution)/shard_map/layer_part/pallas_call | solution.py:525
  112.2 6.2 %all-to-all-start.2 = ((bf16[16,144,128]{2,1,0:T(8,128)(2,1)}), bf16[16,144,128]{2,1,0:T(8,128)(2,1)S(1)}, u32[]{:S(2)}, u32[]{:S(2)}) async-start(bf16[16,144,128]{2,1,0:T(8,128)(2,1)} %layer_part.1), calls=%async_computation.2 | async-start | bytes 1179648 | tf_op jit(solution)/shard_map/all_to_all | solution.py:434
  118.4 2.0 %copy-done.2 = bf16[1792,1024]{1,0:T(8,128)(2,1)S(1)} copy-done((bf16[1792,1024]{1,0:T(8,128)(2,1)S(1)}, bf16[1792,1024]{1,0:T(8,128)(2,1)}, u32[]{:S(2)}) %copy-start.2) | copy-done | bytes 3670040
  121.0 7.0 %collective-permute-start.2 = (bf16[16,32,1024]{2,1,0:T(8,128)(2,1)S(1)}, bf16[16,32,1024]{2,1,0:T(8,128)(2,1)}, u32[]{:S(2)}, u32[]{:S(2)}) collective-permute-start(bf16[16,32,1024]{2,1,0:T(8,128)(2,1)S(1)} %get-tuple-element.31.mine_ref), channel_id=1, source_target_pairs={{0,16},{16,0},{32,48},{48,32},{64,80},{80,64},{96,112},{112,96},{1... | collective-permute-start | bytes 3145736 | tf_op jit(solution)/shard_map/ppermute | solution.py:541
  128.0 12.8 %all-to-all-done.2.heads_ref.arrived_ref = bf16[16,144,128]{2,1,0:T(8,128)(2,1)S(1)} async-done(((bf16[16,144,128]{2,1,0:T(8,128)(2,1)}), bf16[16,144,128]{2,1,0:T(8,128)(2,1)S(1)}, u32[]{:S(2)}, u32[]{:S(2)}) %all-to-all-start.2) | async-done | bytes 589856 | tf_op jit(solution)/shard_map/all_to_all | solution.py:434
  140.8 1.0 grad_part.1
  141.8 27.3 %all_to_all.25.grads_ref = bf16[32,64,128]{2,1,0:T(8,128)(2,1)} all-to-all(bf16[32,64,128]{2,1,0:T(8,128)(2,1)S(1)} %get-tuple-element.38), channel_id=1, replica_groups=mesh['grid'=32,'head'=16] {'grid'}, dimensions={0} | all-to-all | bytes 1048576 | tf_op jit(solution)/shard_map/all_to_all | solution.py:434
  169.1 7.0 %final_part.1 = bf16[32,32,128]{2,1,0:T(8,128)(2,1)} custom-call(s32[32]{0:T(128)} %bitcast.31, s32[2,30]{1,0:T(2,128)} %slot_ref.5, s32[2]{0:T(128)} %count_ref.5, f32[2,30]{1,0:T(2,128)} %bitcast.24, bf16[1024,1024]{1,0:T(8,128)(2,1)} %get-tuple-element.32.norm_ref, bf16[8,128,128]{2,1,0:T(8,128)(2,1)} %get-tuple-element.23.own_ref.kv_ref, ...), custom_call_target="tpu_custom_call" | custom-call | flops 67108864 | bytes 4194304 | tf_op jit(solution)/shard_map/final_part/pallas_call | solution.py:542
  176.1 4.0 %all-to-all-start.4 = ((bf16[32,32,128]{2,1,0:T(8,128)(2,1)}), bf16[32,32,128]{2,1,0:T(8,128)(2,1)S(1)}, u32[]{:S(2)}, u32[]{:S(2)}) async-start(bf16[32,32,128]{2,1,0:T(8,128)(2,1)} %final_part.1), calls=%async_computation.4 | async-start | bytes 524288 | tf_op jit(solution)/shard_map/all_to_all | solution.py:434
  180.1 2.3 %output_part.1 = bf16[16,1024]{1,0:T(8,128)(2,1)} custom-call(s32[1]{0:T(128)} %bitcast.me_ref, bf16[16,144,128]{2,1,0:T(8,128)(2,1)S(1)} %all-to-all-done.2.heads_ref.arrived_ref, bf16[16,32,1024]{2,1,0:T(8,128)(2,1)S(1)} %get-tuple-element.31.mine_ref, bf16[16,32,1024]{2,1,0:T(8,128)(2,1)} %collective-permute-done.2.other_ref, ...), custom_call_target="tpu_custom_call" | custom-call | flops 67108864 | bytes 4194304 | tf_op jit(solution)/shard_map/output_part/pallas_call | solution.py:556
  182.5 6.7 %all-to-all-done.4.parts_ref = bf16[32,32,128]{2,1,0:T(8,128)(2,1)S(1)} async-done(((bf16[32,32,128]{2,1,0:T(8,128)(2,1)}), bf16[32,32,128]{2,1,0:T(8,128)(2,1)S(1)}, u32[]{:S(2)}, u32[]{:S(2)}) %all-to-all-start.4) | async-done | bytes 262176 | tf_op jit(solution)/shard_map/all_to_all | solution.py:434
  (44 shorter events, 2.6 us)
Async XLA Ops:
  7.2 82.5 %all-gather.4.cloned.1.call-start = ((), (), s32[]{:S(2)}) async-start(), calls=%async_computation.5 | async-start | bytes 3899392 | tf_op jit(solution)/shard_map/all_gather | solution.py:471
  8.9 16.3 %copy-start.3 = (bf16[256,1024]{1,0:T(8,128)(2,1)S(1)}, bf16[256,1024]{1,0:T(8,128)(2,1)}, u32[]{:S(2)}) copy-start(bf16[256,1024]{1,0:T(8,128)(2,1)} %mesh_ref.3) | copy-start | bytes 1572868
  8.9 16.3 %copy-start.12 = (bf16[1024,64]{0,1:T(8,128)(2,1)S(1)}, bf16[1024,64]{0,1:T(8,128)(2,1)}, u32[]{:S(2)}) copy-start(bf16[1024,64]{0,1:T(8,128)(2,1)} %param.18) | copy-start | bytes 393220
  8.9 33.5 %copy-start.14 = (s32[2,30]{1,0:T(2,128)S(1)}, s32[2,30]{1,0:T(2,128)}, u32[]{:S(2)}) copy-start(s32[2,30]{1,0:T(2,128)} %slot_ref.5) | copy-start | bytes 724
  9.0 33.5 %copy-start.15 = (f32[2,30,1]{1,2,0:T(1,128)S(1)}, f32[2,30,1]{1,2,0:T(1,128)}, u32[]{:S(2)}) copy-start(f32[2,30,1]{1,2,0:T(1,128)} %param.26) | copy-start | bytes 724
  9.0 33.5 %copy-start.17 = (s32[2]{0:T(128)S(1)}, s32[2]{0:T(128)}, u32[]{:S(2)}) copy-start(s32[2]{0:T(128)} %count_ref.5) | copy-start | bytes 28
  14.6 27.9 %copy-start.4 = (bf16[8,128,128]{2,1,0:T(8,128)(2,1)S(1)}, bf16[8,128,128]{2,1,0:T(8,128)(2,1)}, u32[]{:S(2)}) copy-start(bf16[8,128,128]{2,1,0:T(8,128)(2,1)} %get-tuple-element.23.own_ref.kv_ref) | copy-start | bytes 786436
  14.6 27.9 %all-to-all-start = ((bf16[32,128,128]{2,1,0:T(8,128)(2,1)}), bf16[32,128,128]{2,1,0:T(8,128)(2,1)S(1)}, u32[]{:S(2)}, u32[]{:S(2)}) async-start(bf16[32,128,128]{2,1,0:T(8,128)(2,1)} %get-tuple-element.24), calls=%async_computation | async-start | bytes 2097152 | tf_op jit(solution)/shard_map/all_to_all | solution.py:434
  25.8 63.9 %copy-start.10 = (bf16[2,64,128]{2,1,0:T(8,128)(2,1)}, bf16[2,64,128]{2,1,0:T(8,128)(2,1)S(1)}, u32[]{:S(2)}) copy-start(bf16[2,64,128]{2,1,0:T(8,128)(2,1)S(1)} %query_part.1.query_ref) | copy-start | bytes 98308
  42.5 47.2 %copy-start.5 = (bf16[1024,64]{0,1:T(8,128)(2,1)S(1)}, bf16[1024,64]{0,1:T(8,128)(2,1)}, u32[]{:S(2)}) copy-start(bf16[1024,64]{0,1:T(8,128)(2,1)} %param.22) | copy-start | bytes 393220
  42.5 47.2 %copy-start.6 = (bf16[1024,64]{0,1:T(8,128)(2,1)S(1)}, bf16[1024,64]{0,1:T(8,128)(2,1)}, u32[]{:S(2)}) copy-start(bf16[1024,64]{0,1:T(8,128)(2,1)} %param.23) | copy-start | bytes 393220
  42.5 47.2 %copy-start.7 = (bf16[1024,64]{0,1:T(8,128)(2,1)S(1)}, bf16[1024,64]{0,1:T(8,128)(2,1)}, u32[]{:S(2)}) copy-start(bf16[1024,64]{0,1:T(8,128)(2,1)} %param.24) | copy-start | bytes 393220
  42.5 47.2 %copy-start.8 = (bf16[64,1024]{1,0:T(8,128)(2,1)S(1)}, bf16[64,1024]{1,0:T(8,128)(2,1)}, u32[]{:S(2)}) copy-start(bf16[64,1024]{1,0:T(8,128)(2,1)} %wl_ref.3) | copy-start | bytes 393220
  42.5 47.2 %copy-start.18 = (f32[2,3,1]{1,2,0:T(1,128)S(1)}, f32[2,3,1]{1,2,0:T(1,128)}, u32[]{:S(2)}) copy-start(f32[2,3,1]{1,2,0:T(1,128)} %param.27) | copy-start | bytes 76
  50.3 43.8 %copy-start.11 = (bf16[2,64,128]{2,1,0:T(8,128)(2,1)}, bf16[2,64,128]{2,1,0:T(8,128)(2,1)S(1)}, u32[]{:S(2)}) copy-start(bf16[2,64,128]{2,1,0:T(8,128)(2,1)S(1)} %get-tuple-element.26.heads_ref) | copy-start | bytes 98308
  50.3 61.9 %all-to-all-start.1 = ((bf16[32,144,128]{2,1,0:T(8,128)(2,1)}), bf16[32,144,128]{2,1,0:T(8,128)(2,1)}, u32[]{:S(2)}, u32[]{:S(2)}) async-start(bf16[32,144,128]{2,1,0:T(8,128)(2,1)} %get-tuple-element.25), calls=%async_computation.1 | async-start | bytes 2359296 | tf_op jit(solution)/shard_map/all_to_all | solution.py:434
  91.8 15.5 %copy-start.1 = (bf16[1792,1024]{1,0:T(8,128)(2,1)S(1)}, bf16[1792,1024]{1,0:T(8,128)(2,1)}, u32[]{:S(2)}) copy-start(bf16[1792,1024]{1,0:T(8,128)(2,1)} %all-gather.4.cloned.1.call-done) | copy-start | bytes 11010052
  94.1 11.9 %collective-permute-start.1 = (bf16[544,128]{1,0:T(8,128)(2,1)S(1)}, bf16[544,128]{1,0:T(8,128)(2,1)S(1)}, u32[]{:S(2)}, u32[]{:S(2)}) collective-permute-start(bf16[544,128]{1,0:T(8,128)(2,1)S(1)} %get-tuple-element.27.own_ref), channel_id=1, source_target_pairs={{16,0},{32,16},{48,32},{64,48},{80,64},{96,80},{112,96},{128,112},... | collective-permute-start | bytes 417800 | tf_op jit(solution)/shard_map/ppermute | solution.py:510
  102.1 5.1 %collective-permute-start = (bf16[544,128]{1,0:T(8,128)(2,1)S(1)}, bf16[544,128]{1,0:T(8,128)(2,1)S(1)}, u32[]{:S(2)}, u32[]{:S(2)}) collective-permute-start(bf16[544,128]{1,0:T(8,128)(2,1)S(1)} %get-tuple-element.27.own_ref), channel_id=1, source_target_pairs={{0,16},{16,32},{32,48},{48,64},{64,80},{80,96},{96,112},{112,128},... | collective-permute-start | bytes 417800 | tf_op jit(solution)/shard_map/ppermute | solution.py:509
  107.3 11.1 %copy-start.9 = (bf16[64,1024]{1,0:T(8,128)(2,1)S(1)}, bf16[64,1024]{1,0:T(8,128)(2,1)}, u32[]{:S(2)}) copy-start(bf16[64,1024]{1,0:T(8,128)(2,1)} %wo_ref.3) | copy-start | bytes 393220
  112.2 28.6 %all-to-all-start.2 = ((bf16[16,144,128]{2,1,0:T(8,128)(2,1)}), bf16[16,144,128]{2,1,0:T(8,128)(2,1)S(1)}, u32[]{:S(2)}, u32[]{:S(2)}) async-start(bf16[16,144,128]{2,1,0:T(8,128)(2,1)} %layer_part.1), calls=%async_computation.2 | async-start | bytes 1179648 | tf_op jit(solution)/shard_map/all_to_all | solution.py:434
  121.0 59.1 %collective-permute-start.2 = (bf16[16,32,1024]{2,1,0:T(8,128)(2,1)S(1)}, bf16[16,32,1024]{2,1,0:T(8,128)(2,1)}, u32[]{:S(2)}, u32[]{:S(2)}) collective-permute-start(bf16[16,32,1024]{2,1,0:T(8,128)(2,1)S(1)} %get-tuple-element.31.mine_ref), channel_id=1, source_target_pairs={{0,16},{16,0},{32,48},{48,32},{64,80},{80,64},{96,112},{112,96},{1... | collective-permute-start | bytes 3145736 | tf_op jit(solution)/shard_map/ppermute | solution.py:541
  141.8 27.3 %copy-start.13 = (bf16[2,64,128]{2,1,0:T(8,128)(2,1)}, bf16[2,64,128]{2,1,0:T(8,128)(2,1)S(1)}, u32[]{:S(2)}) copy-start(bf16[2,64,128]{2,1,0:T(8,128)(2,1)S(1)} %get-tuple-element.40.grad_ref) | copy-start | bytes 98308
  176.1 13.0 %all-to-all-start.4 = ((bf16[32,32,128]{2,1,0:T(8,128)(2,1)}), bf16[32,32,128]{2,1,0:T(8,128)(2,1)S(1)}, u32[]{:S(2)}, u32[]{:S(2)}) async-start(bf16[32,32,128]{2,1,0:T(8,128)(2,1)} %final_part.1), calls=%async_computation.4 | async-start | bytes 524288 | tf_op jit(solution)/shard_map/all_to_all | solution.py:434
  (3 other events, 4.7 us)
Sparse Core Ops, SparseCore 0:
  10.1 76.8 all-gather.3

commit v7 on v6

--- a/solution.py
+++ b/solution.py
@@ -359,49 +359,84 @@
         send_ref[p] = jnp.where(me_ref[0] != p, block, jnp.zeros((D, B), bf16))
 
 
-def final_kernel(
-    send_ref, slot_ref, count_ref, bias_ref, norm_ref, kv_ref, early_ref, grads_ref,
-    query_ref, heads_ref, lse_ref, grad_ref, out_ref, acc_ref, reader_ref, edge_ref,
-    held_ref, sem_ref,
-):
-    copy = pltpu.make_async_copy(norm_ref, held_ref, sem_ref)
-    copy.start()
+def stacked_pair(query, grad):
+    zero = jnp.zeros((D, B), bf16)
+    return jnp.concatenate(
+        [jnp.concatenate([query, zero], axis=1), jnp.concatenate([zero, grad], axis=1)], axis=0
+    )
+
+
+def row_products(grad, heads):
+    return jnp.sum(grad.astype(f32) * heads.astype(f32), axis=0, keepdims=True)
+
+
+def joined(soft, grad_soft, inner):
+    return jnp.concatenate([(soft * (grad_soft - inner)).astype(bf16), soft.astype(bf16)], axis=1)
+
+
+def ready_kernel(
+    send_ref, slot_ref, count_ref, bias_ref, kv_ref, early_ref,
+    query_ref, heads_ref, lse_ref, grad_ref, acc_ref, soft_ref, reader_ref, edge_ref,
+):
     full = jnp.where(count_ref[0] == FULL, 0, 1)
     fill_tables(slot_ref, bias_ref, full, reader_ref, edge_ref)
     zero = jnp.zeros((D, B), bf16)
 
-    def back(keys, query, heads, shift, grad):
-        inner = jnp.sum(grad.astype(f32) * heads.astype(f32), axis=0, keepdims=True)
-        pair = jnp.concatenate(
-            [jnp.concatenate([query, zero], axis=1), jnp.concatenate([zero, grad], axis=1)], axis=0
-        )
-        both = dot(keys, pair)
-        soft = jnp.exp(both[:, :B] - shift)
-        mixed = jnp.concatenate(
-            [(soft * (both[:, B:] - inner)).astype(bf16), soft.astype(bf16)], axis=1
-        )
-        return dot(mixed, pair, NT)
-
     def own_step(v, carry):
         m = reader_ref[v]
-        shift = lse_ref[m][0:1] - edge_ref[v]
-        acc_ref[v] = back(kv_ref[v], query_ref[m], heads_ref[m], shift, grad_ref[m])
+        pair = stacked_pair(query_ref[m], grad_ref[m])
+        both = dot(kv_ref[v], pair)
+        soft = jnp.exp(both[:, :B] - (lse_ref[m][0:1] - edge_ref[v]))
+        inner = row_products(grad_ref[m], heads_ref[m])
+        acc_ref[v] = dot(joined(soft, both[:, B:], inner), pair, NT)
         return carry
 
     lax.fori_loop(0, kv_ref.shape[0], own_step, 0, unroll=4)
 
     def sent_step(r, carry):
-        slot = send_ref[r]
         block = early_ref[r]
         tail = block[2 * D :].astype(f32)
         shift = tail[0:1] + tail[1:2] + tail[2:3]
-        part = back(kv_ref[slot], block[:D], block[D : 2 * D], shift, grads_ref[r])
+        query = jnp.concatenate([block[:D], zero], axis=0)
+        soft_ref[r] = jnp.exp(dot(kv_ref[send_ref[r]], query) - shift)
+        return carry
+
+    lax.fori_loop(0, early_ref.shape[0], sent_step, 0, unroll=4)
+
+
+def final_kernel(
+    send_ref, norm_ref, kv_ref, early_ref, grads_ref, own_ref, soft_ref, out_ref, acc_ref,
+    held_ref, weight_ref, sem_ref,
+):
+    pieces = 4
+    each = soft_ref.shape[0] // pieces
+    copies = [
+        pltpu.make_async_copy(
+            soft_ref.at[i * each : (i + 1) * each],
+            weight_ref.at[i * each : (i + 1) * each],
+            sem_ref.at[i],
+        )
+        for i in range(pieces)
+    ]
+    copies.append(pltpu.make_async_copy(norm_ref, held_ref, sem_ref.at[pieces]))
+    for copy in copies:
+        copy.start()
+    acc_ref[...] = own_ref[...]
+
+    def sent_step(r, carry):
+        slot = send_ref[r]
+        pair = stacked_pair(early_ref[r, :D], grads_ref[r])
+        inner = row_products(grads_ref[r], early_ref[r, D : 2 * D])
+        grad_soft = dot(kv_ref[slot], pair[:, B:])
+        part = dot(joined(weight_ref[r], grad_soft, inner), pair, NT)
         acc_ref[slot] = acc_ref[slot] + part
         return carry
 
-    lax.fori_loop(0, early_ref.shape[0], sent_step, 0, unroll=4)
+    for i in range(pieces):
+        copies[i].wait()
+        lax.fori_loop(i * each, (i + 1) * each, sent_step, 0, unroll=8)
+    copies[pieces].wait()
     rows = acc_ref[...].reshape(norm_ref.shape[0], 2 * D).astype(bf16)
-    copy.wait()
     shards, height = out_ref.shape[0], out_ref.shape[1]
     tile = 256
     for c in range(C // tile):
@@ -539,19 +574,29 @@
     )
     arrived_grads = exchange(send_grads, "grid")
     half_other = lax.ppermute(half_mine, "grid", [(i, i ^ 1) for i in range(shards)])
+    own_grad, soft = call(
+        ready_kernel,
+        (struct((own, B, 2 * D), f32), struct((shards, B, B), f32)),
+        [SMEM] * 4 + [VMEM] * 6,
+        tables,
+        name="ready_part",
+    )(
+        send, edge_slot, edge_count, enc_table, own_kv, arrived_early,
+        queries, enc_heads, lse, grads,
+    )
     product = call(
         final_kernel,
         struct((shards, C // shards, 2 * D), bf16),
-        [SMEM] * 4 + [HBM] + [VMEM] * 7,
-        [pltpu.VMEM((own, B, 2 * D), f32)]
-        + tables
-        + [pltpu.VMEM(grid_norm.shape, bf16), pltpu.SemaphoreType.DMA],
+        [SMEM, HBM] + [VMEM] * 4 + [HBM],
+        [
+            pltpu.VMEM((own, B, 2 * D), f32),
+            pltpu.VMEM(grid_norm.shape, bf16),
+            pltpu.VMEM((shards, B, B), f32),
+            pltpu.SemaphoreType.DMA((5,)),
+        ],
         name="final_part",
         mib=61,
-    )(
-        send, edge_slot, edge_count, enc_table, grid_norm, own_kv, arrived_early, arrived_grads,
-        queries, enc_heads, lse, grads,
-    )
+    )(send, grid_norm, own_kv, arrived_early, arrived_grads, own_grad, soft)
     pieces = exchange(product, "grid")
     mesh_out = call(
         output_kernel,

time: 198 us -> 200 us (1.010)
  blocking collectives: 62.1 us -> 34.4 us
  starting transfers between devices: 43.6 us -> 60.1 us
  waiting for transfers between devices: 38.1 us -> 43.9 us
  Pallas kernels: 33.8 us -> 37.6 us
  local copies, waits for them, and re-layouts: 4.75 us -> 8.45 us
    all_to_all x1 -> x0, blocking collectives: 27.3 us -> none  [exchange(): return lax.all_to_all(array, axis, split_axis=0, concat_axis=0, tiled=True)]
    all_to_all x4 -> x5, starting transfers between devices: 25.5 us -> 41.3 us  [exchange(): return lax.all_to_all(array, axis, split_axis=0, concat_axis=0, tiled=True)]
    all_to_all x4 -> x5, waiting for transfers between devices: 36.1 us -> 41.9 us  [exchange(): return lax.all_to_all(array, axis, split_axis=0, concat_axis=0, tiled=True)]
    unnamed x38 -> x54, local copies, waits for them, and re-layouts: 4.75 us -> 8.45 us
    pallas_call x1 -> x2, Pallas kernels: 6.96 us -> 10.2 us  [the longest x1 7.24 us: on_device(): call(final_kernel, struct((shards, C // shards, 2 * D), bf16), [SMEM, HBM...]
  transfers between devices with their start and end apart: 8 -> 9, of which waited for: 5 -> 6; matrix products, arithmetic and copies ran while one was open for 0% -> 0% of each run, Pallas kernels for 16% -> 18%
where the time goes in v7:
time: 200 us; the launch traced here: 199 us
  starting transfers between devices  60.1 us (30%)
  waiting for transfers between devices  43.9 us (22%)
  Pallas kernels  37.6 us (19%)
  blocking collectives  34.4 us (17%)
  between operations  14.4 us (7%)
  local copies, waits for them, and re-layouts  8.45 us (4%)
    all_to_all x5, waiting for transfers between devices, exchange(): return lax.all_to_all(array, axis, split_axis=0, concat_axis=0, tiled=True)  41.9 us
    all_to_all x5, starting transfers between devices, exchange(): return lax.all_to_all(array, axis, split_axis=0, concat_axis=0, tiled=True)  41.3 us
    all_gather x1, blocking collectives, on_device(): all_heads = lax.all_gather(enc_heads, 'head', axis=0, tiled=False)  34.4 us
    ppermute x1, starting transfers between devices, on_device(): right = lax.ppermute(pack, 'grid', backward)  9.11 us
    unnamed x54, local copies, waits for them, and re-layouts  8.45 us
    pallas_call x1, Pallas kernels, on_device(): call(final_kernel, struct((shards, C // shards, 2 * D), bf16), [SMEM, HBM...  7.24 us
    pallas_call x1, Pallas kernels, on_device(): call(encoder_kernel, (struct((2, D, B), bf16), struct((2, 8, B), f32), st...  7.06 us
    ppermute x1, starting transfers between devices, on_device(): lax.ppermute(half_mine, 'grid', [(i, i ^ 1) for i in range(shards)])  6.89 us
  transfers between devices with their start and end apart: 9, of which 6 were waited for; matrix products, arithmetic and copies ran while one was open for 0% of the time, Pallas kernels for 18%

profile of v7, /device:TPU:1, one launch (start us, length us, event | category | flops | bytes accessed | tf_op | source)
XLA Modules:
  0.0 198.9 jit_solution(4057868471467382211)
XLA Ops:
  7.2 1.7 rows_part.1
  9.0 5.6 %grid_part.1 = (bf16[1024,1024]{1,0:T(8,128)(2,1)}, bf16[8,128,128]{2,1,0:T(8,128)(2,1)}, bf16[32,128,128]{2,1,0:T(8,128)(2,1)}) custom-call(s32[32]{0:T(128)} %bitcast.27, bf16[1024,1024]{1,0:T(8,128)(2,1)} %feat_ref.1, bf16[64,1024]{1,0:T(8,128)(2,1)} %bitcast.31, bf16[64,1024]{1,0:T(8,128)(2,1)} %bitcast.32), custom_call_target="tpu_custom_call" | custom-call | flops 268435456 | bytes 6291456 | tf_op jit(solution)/shard_map/grid_part/pallas_call | solution.py:75
  14.5 10.6 %all-to-all-start = ((bf16[32,128,128]{2,1,0:T(8,128)(2,1)}), bf16[32,128,128]{2,1,0:T(8,128)(2,1)S(1)}, u32[]{:S(2)}, u32[]{:S(2)}) async-start(bf16[32,128,128]{2,1,0:T(8,128)(2,1)} %get-tuple-element.26), calls=%async_computation | async-start | bytes 2097152 | tf_op jit(solution)/shard_map/all_to_all | solution.py:469
  25.8 16.6 %all-to-all-done.arrived_ref = bf16[32,128,128]{2,1,0:T(8,128)(2,1)S(1)} async-done(((bf16[32,128,128]{2,1,0:T(8,128)(2,1)}), bf16[32,128,128]{2,1,0:T(8,128)(2,1)S(1)}, u32[]{:S(2)}, u32[]{:S(2)}) %all-to-all-start) | async-done | bytes 1048608 | tf_op jit(solution)/shard_map/all_to_all | solution.py:469
  42.5 7.1 %encoder_part.1 = (bf16[2,64,128]{2,1,0:T(8,128)(2,1)S(1)}, f32[2,8,128]{2,1,0:T(8,128)S(1)}, bf16[32,144,128]{2,1,0:T(8,128)(2,1)}) custom-call(s32[2,30]{1,0:T(2,128)S(1)} %copy-done.21, s32[2]{0:T(128)S(1)} %copy-done.23, f32[2,30]{1,0:T(2,128)S(1)} %bitcast.24, s32[1]{0:T(128)} %bitcast.me_ref, bf16[8,128,128]{2,1,0:T(8,128)(2,1)S(1)} %copy-done.4, ...), custom_call_target="tpu_custom_call" | custom-call | flops 67108864 | bytes 4194304 | tf_op jit(solution)/shard_map/encoder_part/pallas_call | solution.py:518
  49.5 4.0 %all-to-all-start.1 = ((bf16[32,144,128]{2,1,0:T(8,128)(2,1)}), bf16[32,144,128]{2,1,0:T(8,128)(2,1)S(1)}, u32[]{:S(2)}, u32[]{:S(2)}) async-start(bf16[32,144,128]{2,1,0:T(8,128)(2,1)} %get-tuple-element.27), calls=%async_computation.1 | async-start | bytes 2359296 | tf_op jit(solution)/shard_map/all_to_all | solution.py:469
  53.5 34.4 %all-gather = bf16[32,64,128]{2,1,0:T(8,128)(2,1)S(1)} all-gather(bf16[2,64,128]{2,1,0:T(8,128)(2,1)S(1)} %get-tuple-element.28.heads_ref), channel_id=2, replica_groups=mesh['grid'=32,'head'=16] {'head'}, dimensions={0}, use_global_device_ids=true | all-gather | bytes 557056 | tf_op jit(solution)/shard_map/all_gather | solution.py:530
  88.0 2.0 %copy-done = bf16[1792,1024]{1,0:T(8,128)(2,1)S(1)} copy-done((bf16[1792,1024]{1,0:T(8,128)(2,1)S(1)}, bf16[1792,1024]{1,0:T(8,128)(2,1)}, u32[]{:S(2)}) %copy-start) | copy-done | bytes 3670040
  90.7 2.3 %middle_part.1 = (bf16[544,128]{1,0:T(8,128)(2,1)S(1)}, f32[24,1024]{1,0:T(8,128)S(1)}, bf16[256,1024]{1,0:T(8,128)(2,1)S(1)}) custom-call(s32[1]{0:T(128)} %bitcast.6.at_ref, f32[2,3]{1,0:T(2,128)S(1)} %bitcast.30, bf16[16,2,64,128]{3,2,1,0:T(8,128)(2,1)S(1)} %bitcast.16, bf16[16,112,1024]{2,1,0:T(8,128)(2,1)S(1)} %bitcast.13, ...), custom_call_target="tpu_custom_call" | custom-call | flops 67108864 | bytes 4194304 | tf_op jit(solution)/shard_map/middle_part/pallas_call | solution.py:531
  93.7 9.1 %collective-permute-start.1 = (bf16[544,128]{1,0:T(8,128)(2,1)S(1)}, bf16[544,128]{1,0:T(8,128)(2,1)S(1)}, u32[]{:S(2)}, u32[]{:S(2)}) collective-permute-start(bf16[544,128]{1,0:T(8,128)(2,1)S(1)} %get-tuple-element.29.own_ref), channel_id=1, source_target_pairs={{16,0},{32,16},{48,32},{64,48},{80,64},{96,80},{112,96},{128,112},... | collective-permute-start | bytes 417800 | tf_op jit(solution)/shard_map/ppermute | solution.py:545
  102.8 2.7 %collective-permute-start = (bf16[544,128]{1,0:T(8,128)(2,1)S(1)}, bf16[544,128]{1,0:T(8,128)(2,1)S(1)}, u32[]{:S(2)}, u32[]{:S(2)}) collective-permute-start(bf16[544,128]{1,0:T(8,128)(2,1)S(1)} %get-tuple-element.29.own_ref), channel_id=1, source_target_pairs={{0,16},{16,32},{32,48},{48,64},{64,80},{80,96},{96,112},{112,128},... | collective-permute-start | bytes 417800 | tf_op jit(solution)/shard_map/ppermute | solution.py:544
  107.6 4.8 %layer_part.1 = bf16[16,144,128]{2,1,0:T(8,128)(2,1)} custom-call(bf16[544,128]{1,0:T(8,128)(2,1)S(1)} %get-tuple-element.29.own_ref, bf16[544,128]{1,0:T(8,128)(2,1)S(1)} %collective-permute-done.left_ref, bf16[544,128]{1,0:T(8,128)(2,1)S(1)} %collective-permute-done.1.right_ref, bf16[256,1024]{1,0:T(8,128)(2,1)S(1)} %get-tuple-element.30.unit_ref, ...), custom_call_target="tpu_custom_call" | custom-call | flops 67108864 | bytes 4194304 | tf_op jit(solution)/shard_map/layer_part/pallas_call | solution.py:560
  112.4 6.8 %all-to-all-start.2 = ((bf16[16,144,128]{2,1,0:T(8,128)(2,1)}), bf16[16,144,128]{2,1,0:T(8,128)(2,1)S(1)}, u32[]{:S(2)}, u32[]{:S(2)}) async-start(bf16[16,144,128]{2,1,0:T(8,128)(2,1)} %layer_part.1), calls=%async_computation.2 | async-start | bytes 1179648 | tf_op jit(solution)/shard_map/all_to_all | solution.py:469
  119.3 2.0 %copy-done.2 = bf16[1792,1024]{1,0:T(8,128)(2,1)S(1)} copy-done((bf16[1792,1024]{1,0:T(8,128)(2,1)S(1)}, bf16[1792,1024]{1,0:T(8,128)(2,1)}, u32[]{:S(2)}) %copy-start.2) | copy-done | bytes 3670040
  121.3 1.4 side_part.1
  122.7 6.9 %collective-permute-start.2 = (bf16[16,32,1024]{2,1,0:T(8,128)(2,1)}, bf16[16,32,1024]{2,1,0:T(8,128)(2,1)S(1)}, u32[]{:S(2)}, u32[]{:S(2)}) collective-permute-start(bf16[16,32,1024]{2,1,0:T(8,128)(2,1)} %get-tuple-element.33.mine_ref), channel_id=1, source_target_pairs={{0,16},{16,0},{32,48},{48,32},{64,80},{80,64},{96,112},{112,96},{1... | collective-permute-start | bytes 3145736 | tf_op jit(solution)/shard_map/ppermute | solution.py:576
  129.6 12.1 %all-to-all-done.2.heads_ref.arrived_ref = bf16[16,144,128]{2,1,0:T(8,128)(2,1)S(1)} async-done(((bf16[16,144,128]{2,1,0:T(8,128)(2,1)}), bf16[16,144,128]{2,1,0:T(8,128)(2,1)S(1)}, u32[]{:S(2)}, u32[]{:S(2)}) %all-to-all-start.2) | async-done | bytes 589856 | tf_op jit(solution)/shard_map/all_to_all | solution.py:469
  143.5 15.9 %all-to-all-start.3 = ((bf16[32,64,128]{2,1,0:T(8,128)(2,1)}), bf16[32,64,128]{2,1,0:T(8,128)(2,1)}, u32[]{:S(2)}, u32[]{:S(2)}) async-start(bf16[32,64,128]{2,1,0:T(8,128)(2,1)} %copy-done.10), calls=%async_computation.3 | async-start | bytes 1048576 | tf_op jit(solution)/shard_map/all_to_all | solution.py:469
  159.5 3.0 %ready_part.1 = (f32[8,128,128]{2,1,0:T(8,128)S(1)}, f32[32,128,128]{2,1,0:T(8,128)S(1)}) custom-call(s32[32]{0:T(128)S(1)} %bitcast.29, s32[2,30]{1,0:T(2,128)S(1)} %copy-done.21, s32[2]{0:T(128)S(1)} %copy-done.24, f32[2,30]{1,0:T(2,128)S(1)} %bitcast.26, bf16[8,128,128]{2,1,0:T(8,128)(2,1)S(1)} %copy-done.4, ...), custom_call_target="tpu_custom_call" | custom-call | flops 67108864 | bytes 4194304 | tf_op jit(solution)/shard_map/ready_part/pallas_call | solution.py:577
  164.6 6.5 %all-to-all-done.3.grads_ref = bf16[32,64,128]{2,1,0:T(8,128)(2,1)} async-done(((bf16[32,64,128]{2,1,0:T(8,128)(2,1)}), bf16[32,64,128]{2,1,0:T(8,128)(2,1)}, u32[]{:S(2)}, u32[]{:S(2)}) %all-to-all-start.3) | async-done | bytes 524320 | tf_op jit(solution)/shard_map/all_to_all | solution.py:469
  171.1 7.2 %final_part.1 = bf16[32,32,128]{2,1,0:T(8,128)(2,1)} custom-call(s32[32]{0:T(128)} %bitcast.28, bf16[1024,1024]{1,0:T(8,128)(2,1)} %get-tuple-element.34.norm_ref, bf16[8,128,128]{2,1,0:T(8,128)(2,1)} %get-tuple-element.25.own_ref.kv_ref, bf16[32,144,128]{2,1,0:T(8,128)(2,1)} %copy-done.3, bf16[32,64,128]{2,1,0:T(8,128)(2,1)} %all-to-all-done.3.grads_ref, ...), custom_call_target="tpu_custom_call" | custom-call | flops 67108864 | bytes 4194304 | tf_op jit(solution)/shard_map/final_part/pallas_call | solution.py:587
  178.3 4.0 %all-to-all-start.4 = ((bf16[32,32,128]{2,1,0:T(8,128)(2,1)}), bf16[32,32,128]{2,1,0:T(8,128)(2,1)S(1)}, u32[]{:S(2)}, u32[]{:S(2)}) async-start(bf16[32,32,128]{2,1,0:T(8,128)(2,1)} %final_part.1), calls=%async_computation.4 | async-start | bytes 524288 | tf_op jit(solution)/shard_map/all_to_all | solution.py:469
  182.3 2.3 %output_part.1 = bf16[16,1024]{1,0:T(8,128)(2,1)} custom-call(s32[1]{0:T(128)} %bitcast.me_ref, bf16[16,144,128]{2,1,0:T(8,128)(2,1)S(1)} %all-to-all-done.2.heads_ref.arrived_ref, bf16[16,32,1024]{2,1,0:T(8,128)(2,1)} %get-tuple-element.33.mine_ref, bf16[16,32,1024]{2,1,0:T(8,128)(2,1)S(1)} %collective-permute-done.2.other_ref, f32[24,1024]{1,0:T(8,128)S(1)} %copy-done.15), custom_call_target="tpu_custom_call" | custom-call | flops 67108864 | bytes 4194304 | tf_op jit(solution)/shard_map/output_part/pallas_call | solution.py:601
  184.6 6.7 %all-to-all-done.4.parts_ref = bf16[32,32,128]{2,1,0:T(8,128)(2,1)S(1)} async-done(((bf16[32,32,128]{2,1,0:T(8,128)(2,1)}), bf16[32,32,128]{2,1,0:T(8,128)(2,1)S(1)}, u32[]{:S(2)}, u32[]{:S(2)}) %all-to-all-start.4) | async-done | bytes 262176 | tf_op jit(solution)/shard_map/all_to_all | solution.py:469
  (62 shorter events, 8.8 us)
Async XLA Ops:
  7.2 80.8 %all-gather.4.cloned.1.call-start = ((), (), s32[]{:S(2)}) async-start(), calls=%async_computation.5 | async-start | bytes 3899392 | tf_op jit(solution)/shard_map/all_gather | solution.py:506
  8.9 33.5 %copy-start.21 = (s32[2,30]{1,0:T(2,128)S(1)}, s32[2,30]{1,0:T(2,128)}, u32[]{:S(2)}) copy-start(s32[2,30]{1,0:T(2,128)} %slot_ref.5) | copy-start | bytes 724
  8.9 33.5 %copy-start.22 = (f32[2,30,1]{1,2,0:T(1,128)S(1)}, f32[2,30,1]{1,2,0:T(1,128)}, u32[]{:S(2)}) copy-start(f32[2,30,1]{1,2,0:T(1,128)} %param.26) | copy-start | bytes 724
  8.9 33.5 %copy-start.23 = (s32[2]{0:T(128)S(1)}, s32[2]{0:T(128)}, u32[]{:S(2)}) copy-start(s32[2]{0:T(128)} %count_ref.5) | copy-start | bytes 28
  14.5 27.9 %copy-start.4 = (bf16[8,128,128]{2,1,0:T(8,128)(2,1)S(1)}, bf16[8,128,128]{2,1,0:T(8,128)(2,1)}, u32[]{:S(2)}) copy-start(bf16[8,128,128]{2,1,0:T(8,128)(2,1)} %get-tuple-element.25.own_ref.kv_ref) | copy-start | bytes 786436
  14.5 27.9 %all-to-all-start = ((bf16[32,128,128]{2,1,0:T(8,128)(2,1)}), bf16[32,128,128]{2,1,0:T(8,128)(2,1)S(1)}, u32[]{:S(2)}, u32[]{:S(2)}) async-start(bf16[32,128,128]{2,1,0:T(8,128)(2,1)} %get-tuple-element.26), calls=%async_computation | async-start | bytes 2097152 | tf_op jit(solution)/shard_map/all_to_all | solution.py:469
  25.8 62.2 %copy-start.16 = (bf16[2,64,128]{2,1,0:T(8,128)(2,1)}, bf16[2,64,128]{2,1,0:T(8,128)(2,1)S(1)}, u32[]{:S(2)}) copy-start(bf16[2,64,128]{2,1,0:T(8,128)(2,1)S(1)} %query_part.1.query_ref) | copy-start | bytes 98308
  42.4 45.5 %copy-start.7 = (bf16[1024,64]{0,1:T(8,128)(2,1)S(1)}, bf16[1024,64]{0,1:T(8,128)(2,1)}, u32[]{:S(2)}) copy-start(bf16[1024,64]{0,1:T(8,128)(2,1)} %param.22) | copy-start | bytes 393220
  42.4 45.5 %copy-start.8 = (bf16[1024,64]{0,1:T(8,128)(2,1)S(1)}, bf16[1024,64]{0,1:T(8,128)(2,1)}, u32[]{:S(2)}) copy-start(bf16[1024,64]{0,1:T(8,128)(2,1)} %param.23) | copy-start | bytes 393220
  42.5 45.5 %copy-start.9 = (bf16[1024,64]{0,1:T(8,128)(2,1)S(1)}, bf16[1024,64]{0,1:T(8,128)(2,1)}, u32[]{:S(2)}) copy-start(bf16[1024,64]{0,1:T(8,128)(2,1)} %param.24) | copy-start | bytes 393220
  42.5 45.5 %copy-start.11 = (bf16[64,1024]{1,0:T(8,128)(2,1)S(1)}, bf16[64,1024]{1,0:T(8,128)(2,1)}, u32[]{:S(2)}) copy-start(bf16[64,1024]{1,0:T(8,128)(2,1)} %wl_ref.3) | copy-start | bytes 393220
  49.5 38.4 %copy-start.18 = (bf16[2,64,128]{2,1,0:T(8,128)(2,1)}, bf16[2,64,128]{2,1,0:T(8,128)(2,1)S(1)}, u32[]{:S(2)}) copy-start(bf16[2,64,128]{2,1,0:T(8,128)(2,1)S(1)} %get-tuple-element.28.heads_ref) | copy-start | bytes 98308
  49.5 62.9 %all-to-all-start.1 = ((bf16[32,144,128]{2,1,0:T(8,128)(2,1)}), bf16[32,144,128]{2,1,0:T(8,128)(2,1)S(1)}, u32[]{:S(2)}, u32[]{:S(2)}) async-start(bf16[32,144,128]{2,1,0:T(8,128)(2,1)} %get-tuple-element.27), calls=%async_computation.1 | async-start | bytes 2359296 | tf_op jit(solution)/shard_map/all_to_all | solution.py:469
  93.7 12.7 %collective-permute-start.1 = (bf16[544,128]{1,0:T(8,128)(2,1)S(1)}, bf16[544,128]{1,0:T(8,128)(2,1)S(1)}, u32[]{:S(2)}, u32[]{:S(2)}) collective-permute-start(bf16[544,128]{1,0:T(8,128)(2,1)S(1)} %get-tuple-element.29.own_ref), channel_id=1, source_target_pairs={{16,0},{32,16},{48,32},{64,48},{80,64},{96,80},{112,96},{128,112},... | collective-permute-start | bytes 417800 | tf_op jit(solution)/shard_map/ppermute | solution.py:545
  102.8 4.7 %collective-permute-start = (bf16[544,128]{1,0:T(8,128)(2,1)S(1)}, bf16[544,128]{1,0:T(8,128)(2,1)S(1)}, u32[]{:S(2)}, u32[]{:S(2)}) collective-permute-start(bf16[544,128]{1,0:T(8,128)(2,1)S(1)} %get-tuple-element.29.own_ref), channel_id=1, source_target_pairs={{0,16},{16,32},{32,48},{48,64},{64,80},{80,96},{96,112},{112,128},... | collective-permute-start | bytes 417800 | tf_op jit(solution)/shard_map/ppermute | solution.py:544
  112.4 47.1 %copy-start.3 = (bf16[32,144,128]{2,1,0:T(8,128)(2,1)}, bf16[32,144,128]{2,1,0:T(8,128)(2,1)S(1)}, u32[]{:S(2)}) copy-start(bf16[32,144,128]{2,1,0:T(8,128)(2,1)S(1)} %all-to-all-done.1.early_ref) | copy-start | bytes 3538948
  112.4 29.3 %all-to-all-start.2 = ((bf16[16,144,128]{2,1,0:T(8,128)(2,1)}), bf16[16,144,128]{2,1,0:T(8,128)(2,1)S(1)}, u32[]{:S(2)}, u32[]{:S(2)}) async-start(bf16[16,144,128]{2,1,0:T(8,128)(2,1)} %layer_part.1), calls=%async_computation.2 | async-start | bytes 1179648 | tf_op jit(solution)/shard_map/all_to_all | solution.py:469
  121.3 20.4 %copy-start.24 = (s32[2]{0:T(128)S(1)}, s32[2]{0:T(128)}, u32[]{:S(2)}) copy-start(s32[2]{0:T(128)} %count_ref.5) | copy-start | bytes 28
  121.3 38.2 %copy-start.17 = (bf16[2,64,128]{2,1,0:T(8,128)(2,1)S(1)}, bf16[2,64,128]{2,1,0:T(8,128)(2,1)}, u32[]{:S(2)}) copy-start(bf16[2,64,128]{2,1,0:T(8,128)(2,1)} %copy-done.16) | copy-start | bytes 98308
  121.3 38.2 %copy-start.19 = (bf16[2,64,128]{2,1,0:T(8,128)(2,1)S(1)}, bf16[2,64,128]{2,1,0:T(8,128)(2,1)}, u32[]{:S(2)}) copy-start(bf16[2,64,128]{2,1,0:T(8,128)(2,1)} %copy-done.18) | copy-start | bytes 98308
  121.3 38.2 %copy-start.25 = (s32[1,32]{1,0:T(1,128)S(1)}, s32[1,32]{1,0:T(1,128)}, u32[]{:S(2)}) copy-start(s32[1,32]{1,0:T(1,128)} %param.28) | copy-start | bytes 388
  122.7 59.7 %collective-permute-start.2 = (bf16[16,32,1024]{2,1,0:T(8,128)(2,1)}, bf16[16,32,1024]{2,1,0:T(8,128)(2,1)S(1)}, u32[]{:S(2)}, u32[]{:S(2)}) collective-permute-start(bf16[16,32,1024]{2,1,0:T(8,128)(2,1)} %get-tuple-element.33.mine_ref), channel_id=1, source_target_pairs={{0,16},{16,0},{32,48},{48,32},{64,80},{80,64},{96,112},{112,96},{1... | collective-permute-start | bytes 3145736 | tf_op jit(solution)/shard_map/ppermute | solution.py:576
  143.5 27.5 %all-to-all-start.3 = ((bf16[32,64,128]{2,1,0:T(8,128)(2,1)}), bf16[32,64,128]{2,1,0:T(8,128)(2,1)}, u32[]{:S(2)}, u32[]{:S(2)}) async-start(bf16[32,64,128]{2,1,0:T(8,128)(2,1)} %copy-done.10), calls=%async_computation.3 | async-start | bytes 1048576 | tf_op jit(solution)/shard_map/all_to_all | solution.py:469
  178.3 13.0 %all-to-all-start.4 = ((bf16[32,32,128]{2,1,0:T(8,128)(2,1)}), bf16[32,32,128]{2,1,0:T(8,128)(2,1)S(1)}, u32[]{:S(2)}, u32[]{:S(2)}) async-start(bf16[32,32,128]{2,1,0:T(8,128)(2,1)} %final_part.1), calls=%async_computation.4 | async-start | bytes 524288 | tf_op jit(solution)/shard_map/all_to_all | solution.py:469
  (12 other events, 81.0 us)
Sparse Core Ops, SparseCore 0:
  10.1 76.9 all-gather.3

commit v8 on v6

--- a/solution.py
+++ b/solution.py
@@ -195,7 +195,7 @@
 
 def middle_kernel(
     at_ref, bias_ref, heads_ref, gathered_ref, mesh_ref, wq_ref, wk_ref, wv_ref, wl_ref,
-    pack_ref, tail_ref, unit_ref, enc_ref,
+    left_ref, right_ref, tail_ref, unit_ref, enc_ref,
 ):
     parts = heads_ref.shape[0]
     w_out = gathered_ref[:, 0:D, :].reshape(parts * D, C)
@@ -203,7 +203,7 @@
     half = parts // 2
     height = 2 * B // parts
     tail_ref[height:] = jnp.zeros((8, C), f32)
-    queries, grads = [], []
+    messages = (left_ref, right_ref)
     for b in range(2):
         rows = slice(b * B, (b + 1) * B)
         heads = heads_ref[:, b].reshape(parts * D, B)
@@ -214,13 +214,13 @@
         unit_ref[rows] = unit
         tail_ref[height:, b * B : (b + 1) * B] = jnp.broadcast_to(inverse, (B, 128)).T[0:8]
         both = dot(unit, w_layer, NT).astype(bf16)
-        pack_ref[rows] = both[:, : 2 * D]
-        queries.append((both[:, 2 * D :].astype(f32) * score_scale).astype(bf16))
+        for message in messages:
+            message[rows] = both[:, : 2 * D]
+        queries = (both[:, 2 * D :].astype(f32) * score_scale).astype(bf16)
         cot = gathered_ref[half * b : half * (b + 1), D + D // 2 :, :].reshape(B, C)
-        grads.append(dot(cot, wl_ref[...], NT).astype(bf16))
+        grads = dot(cot, wl_ref[...], NT).astype(bf16)
+        messages[b][2 * B : 3 * B] = jnp.concatenate([queries, grads], axis=1)
     tail_ref[:height] = enc_ref[pl.ds(pl.multiple_of(at_ref[0] * height, height), height), :]
-    pack_ref[2 * B : 3 * B] = jnp.concatenate(queries, axis=1)
-    pack_ref[3 * B : 4 * B] = jnp.concatenate(grads, axis=1)
     row = lax.broadcasted_iota(jnp.int32, (8, 128), 0)
     table = jnp.zeros((8, 128), f32)
     for b in range(2):
@@ -230,7 +230,8 @@
     rest = table - high
     middle = rest.astype(bf16).astype(f32)
     tail = [high, middle, rest - middle, jnp.zeros((8, 128), f32)]
-    pack_ref[4 * B : 4 * B + 32] = jnp.concatenate(tail, axis=0).astype(bf16)
+    for message in messages:
+        message[3 * B : 3 * B + 32] = jnp.concatenate(tail, axis=0).astype(bf16)
 
 
 def side_kernel(
@@ -254,34 +255,32 @@
 
 
 def layer_kernel(
-    own_ref, left_ref, right_ref, unit_ref, wq_ref, wk_ref, wv_ref, gathered_ref, send_ref
+    low_ref, high_ref, left_ref, right_ref, unit_ref, wq_ref, wk_ref, wv_ref, gathered_ref,
+    send_ref,
 ):
-    zero = jnp.zeros((B, D), bf16)
+    zero = jnp.zeros((B, 2 * D), bf16)
+    first = lax.broadcasted_iota(jnp.int32, (B, 2 * D), 1) < D
 
     def block(ref, b):
         return ref[b * B : (b + 1) * B]
 
-    def stacked(ref, b):
-        lanes = slice(b * D, (b + 1) * D)
-        query = ref[2 * B : 3 * B][:, lanes]
-        grad = ref[3 * B : 4 * B][:, lanes]
-        return jnp.concatenate(
-            [jnp.concatenate([query, zero], axis=1), jnp.concatenate([zero, grad], axis=1)], axis=0
-        )
+    def stacked(ref):
+        rows = block(ref, 2)
+        return jnp.concatenate([jnp.where(first, rows, zero), jnp.where(first, zero, rows)], axis=0)
 
     def table(ref):
-        tail = ref[4 * B : 4 * B + 32].astype(f32)
+        tail = ref[3 * B : 3 * B + 32].astype(f32)
         return tail[0:8] + tail[8:16] + tail[16:24]
 
-    kv = [block(ref, b) for ref in (left_ref, own_ref, right_ref) for b in range(2)]
-    own_bias = table(own_ref)
-    queries = [(left_ref, 1, table(left_ref)), (own_ref, 0, own_bias), (own_ref, 1, own_bias)]
+    kv = [block(ref, b) for ref in (left_ref, low_ref, right_ref) for b in range(2)]
+    own_bias = table(low_ref)
+    queries = [(left_ref, 1, table(left_ref)), (low_ref, 0, own_bias), (high_ref, 1, own_bias)]
     queries.append((right_ref, 0, table(right_ref)))
     heads = []
     grad_kv = [jnp.zeros((B, 2 * D), f32), jnp.zeros((B, 2 * D), f32)]
     grad_q = []
     for j, (ref, b, bias) in enumerate(queries):
-        pair = stacked(ref, b)
+        pair = stacked(ref)
         window = kv[j : j + 3]
         both = [dot(rows, pair, NT) for rows in window]
         scores = [both[n][:, :B] + bias[3 * b + n : 3 * b + n + 1] for n in range(3)]
@@ -362,10 +361,15 @@
 def final_kernel(
     send_ref, slot_ref, count_ref, bias_ref, norm_ref, kv_ref, early_ref, grads_ref,
     query_ref, heads_ref, lse_ref, grad_ref, out_ref, acc_ref, reader_ref, edge_ref,
-    held_ref, sem_ref,
+    held_ref, block_ref, part_ref, sem_ref,
 ):
-    copy = pltpu.make_async_copy(norm_ref, held_ref, sem_ref)
-    copy.start()
+    copies = [
+        pltpu.make_async_copy(early_ref, block_ref, sem_ref.at[0]),
+        pltpu.make_async_copy(grads_ref, part_ref, sem_ref.at[1]),
+        pltpu.make_async_copy(norm_ref, held_ref, sem_ref.at[2]),
+    ]
+    for copy in copies:
+        copy.start()
     full = jnp.where(count_ref[0] == FULL, 0, 1)
     fill_tables(slot_ref, bias_ref, full, reader_ref, edge_ref)
     zero = jnp.zeros((D, B), bf16)
@@ -392,16 +396,18 @@
 
     def sent_step(r, carry):
         slot = send_ref[r]
-        block = early_ref[r]
+        block = block_ref[r]
         tail = block[2 * D :].astype(f32)
         shift = tail[0:1] + tail[1:2] + tail[2:3]
-        part = back(kv_ref[slot], block[:D], block[D : 2 * D], shift, grads_ref[r])
+        part = back(kv_ref[slot], block[:D], block[D : 2 * D], shift, part_ref[r])
         acc_ref[slot] = acc_ref[slot] + part
         return carry
 
-    lax.fori_loop(0, early_ref.shape[0], sent_step, 0, unroll=4)
+    copies[0].wait()
+    copies[1].wait()
+    lax.fori_loop(0, block_ref.shape[0], sent_step, 0, unroll=4)
     rows = acc_ref[...].reshape(norm_ref.shape[0], 2 * D).astype(bf16)
-    copy.wait()
+    copies[2].wait()
     shards, height = out_ref.shape[0], out_ref.shape[1]
     tile = 256
     for c in range(C // tile):
@@ -493,10 +499,11 @@
     )(edge_slot, edge_count, enc_table, shard_at, own_kv, arrived_kv, queries)
     arrived_early = exchange(early, "grid")
     all_heads = lax.all_gather(enc_heads, "head", axis=0, tiled=False)
-    pack, tail, unit = call(
+    low, high, tail, unit = call(
         middle_kernel,
         (
-            struct((4 * B + 32, 2 * D), bf16),
+            struct((3 * B + 32, 2 * D), bf16),
+            struct((3 * B + 32, 2 * D), bf16),
             struct((share + 8, C), f32),
             struct((2 * B, C), bf16),
         ),
@@ -506,8 +513,8 @@
     )(
         head_at, layer_table, all_heads, gathered, mesh_feat, layer_query, layer_key, layer_value, layer_out_weight
     )
-    left = lax.ppermute(pack, "grid", forward)
-    right = lax.ppermute(pack, "grid", backward)
+    left = lax.ppermute(high, "grid", forward)
+    right = lax.ppermute(low, "grid", backward)
     cot_part, unit_part, inverse_row, weight_sum, half_mine = call(
         side_kernel,
         (
@@ -523,8 +530,8 @@
         name="side_part",
     )(gathered, unit, tail, enc_out_weight)
     mixed = call(
-        layer_kernel, struct((parts, 2 * D + share, B), bf16), [VMEM] * 8, name="layer_part"
-    )(pack, left, right, unit, layer_query, layer_key, layer_value, gathered)
+        layer_kernel, struct((parts, 2 * D + share, B), bf16), [VMEM] * 9, name="layer_part"
+    )(low, high, left, right, unit, layer_query, layer_key, layer_value, gathered)
     arrived_early, mixed = lax.optimization_barrier((arrived_early, mixed))
     arrived_grad = exchange(mixed, "head")
     grads, send_grads = call(
@@ -542,10 +549,15 @@
     product = call(
         final_kernel,
         struct((shards, C // shards, 2 * D), bf16),
-        [SMEM] * 4 + [HBM] + [VMEM] * 7,
+        [SMEM] * 4 + [HBM, VMEM, HBM, HBM] + [VMEM] * 4,
         [pltpu.VMEM((own, B, 2 * D), f32)]
         + tables
-        + [pltpu.VMEM(grid_norm.shape, bf16), pltpu.SemaphoreType.DMA],
+        + [
+            pltpu.VMEM(grid_norm.shape, bf16),
+            pltpu.VMEM((shards, 2 * D + 16, B), bf16),
+            pltpu.VMEM((shards, D, B), bf16),
+            pltpu.SemaphoreType.DMA((3,)),
+        ],
         name="final_part",
         mib=61,
     )(

time: 198 us -> 197 us (level)
  no operation moved by 1% of the time
where the time goes in v8:
time: 197 us; the launch traced here: 196 us
  blocking collectives  62.3 us (32%)
  starting transfers between devices  43.6 us (22%)
  waiting for transfers between devices  37.4 us (19%)
  Pallas kernels  33.6 us (17%)
  between operations  14.3 us (7%)
  local copies, waits for them, and re-layouts  4.75 us (2%)
    all_to_all x4, waiting for transfers between devices, exchange(): return lax.all_to_all(array, axis, split_axis=0, concat_axis=0, tiled=True)  35.7 us
    all_gather x1, blocking collectives, on_device(): all_heads = lax.all_gather(enc_heads, 'head', axis=0, tiled=False)  34.7 us
    all_to_all x1, blocking collectives, exchange(): return lax.all_to_all(array, axis, split_axis=0, concat_axis=0, tiled=True)  27.6 us
    all_to_all x4, starting transfers between devices, exchange(): return lax.all_to_all(array, axis, split_axis=0, concat_axis=0, tiled=True)  25.4 us
    ppermute x1, starting transfers between devices, on_device(): right = lax.ppermute(low, 'grid', backward)  8.19 us
    pallas_call x1, Pallas kernels, on_device(): call(encoder_kernel, (struct((2, D, B), bf16), struct((2, 8, B), f32), st...  7.13 us
    ppermute x1, starting transfers between devices, on_device(): lax.ppermute(half_mine, 'grid', [(i, i ^ 1) for i in range(shards)])  7.06 us
    pallas_call x1, Pallas kernels, on_device(): call(final_kernel, struct((shards, C // shards, 2 * D), bf16), [SMEM] * 4...  6.85 us
  transfers between devices with their start and end apart: 8, of which 5 were waited for; matrix products, arithmetic and copies ran while one was open for 0% of the time, Pallas kernels for 16%

profile of v8, /device:TPU:1, one launch (start us, length us, event | category | flops | bytes accessed | tf_op | source)
XLA Modules:
  0.0 196.1 jit_solution(7640406957141247102)
XLA Ops:
  7.2 1.7 rows_part.1
  9.0 5.6 %grid_part.1 = (bf16[1024,1024]{1,0:T(8,128)(2,1)}, bf16[8,128,128]{2,1,0:T(8,128)(2,1)}, bf16[32,128,128]{2,1,0:T(8,128)(2,1)}) custom-call(s32[32]{0:T(128)} %bitcast.30, bf16[1024,1024]{1,0:T(8,128)(2,1)} %feat_ref.1, bf16[64,1024]{1,0:T(8,128)(2,1)} %bitcast.28, bf16[64,1024]{1,0:T(8,128)(2,1)} %bitcast.29), custom_call_target="tpu_custom_call" | custom-call | flops 268435456 | bytes 6291456 | tf_op jit(solution)/shard_map/grid_part/pallas_call | solution.py:75
  14.6 10.6 %all-to-all-start = ((bf16[32,128,128]{2,1,0:T(8,128)(2,1)}), bf16[32,128,128]{2,1,0:T(8,128)(2,1)S(1)}, u32[]{:S(2)}, u32[]{:S(2)}) async-start(bf16[32,128,128]{2,1,0:T(8,128)(2,1)} %get-tuple-element.25), calls=%async_computation | async-start | bytes 2097152 | tf_op jit(solution)/shard_map/all_to_all | solution.py:440
  25.8 16.6 %all-to-all-done.arrived_ref = bf16[32,128,128]{2,1,0:T(8,128)(2,1)S(1)} async-done(((bf16[32,128,128]{2,1,0:T(8,128)(2,1)}), bf16[32,128,128]{2,1,0:T(8,128)(2,1)S(1)}, u32[]{:S(2)}, u32[]{:S(2)}) %all-to-all-start) | async-done | bytes 1048608 | tf_op jit(solution)/shard_map/all_to_all | solution.py:440
  42.6 7.1 %encoder_part.1 = (bf16[2,64,128]{2,1,0:T(8,128)(2,1)S(1)}, f32[2,8,128]{2,1,0:T(8,128)S(1)}, bf16[32,144,128]{2,1,0:T(8,128)(2,1)}) custom-call(s32[2,30]{1,0:T(2,128)S(1)} %copy-done.14, s32[2]{0:T(128)S(1)} %copy-done.17, f32[2,30]{1,0:T(2,128)S(1)} %bitcast.25, s32[1]{0:T(128)} %bitcast.me_ref, bf16[8,128,128]{2,1,0:T(8,128)(2,1)S(1)} %copy-done.4, ...), custom_call_target="tpu_custom_call" | custom-call | flops 67108864 | bytes 4194304 | tf_op jit(solution)/shard_map/encoder_part/pallas_call | solution.py:489
  50.3 4.7 %all-to-all-start.1 = ((bf16[32,144,128]{2,1,0:T(8,128)(2,1)}), bf16[32,144,128]{2,1,0:T(8,128)(2,1)}, u32[]{:S(2)}, u32[]{:S(2)}) async-start(bf16[32,144,128]{2,1,0:T(8,128)(2,1)} %get-tuple-element.26), calls=%async_computation.1 | async-start | bytes 2359296 | tf_op jit(solution)/shard_map/all_to_all | solution.py:440
  55.0 34.7 %all-gather = bf16[32,64,128]{2,1,0:T(8,128)(2,1)S(1)} all-gather(bf16[2,64,128]{2,1,0:T(8,128)(2,1)S(1)} %get-tuple-element.27.heads_ref), channel_id=2, replica_groups=mesh['grid'=32,'head'=16] {'head'}, dimensions={0}, use_global_device_ids=true | all-gather | bytes 557056 | tf_op jit(solution)/shard_map/all_gather | solution.py:501
  89.7 2.0 %copy-done = bf16[1792,1024]{1,0:T(8,128)(2,1)S(1)} copy-done((bf16[1792,1024]{1,0:T(8,128)(2,1)S(1)}, bf16[1792,1024]{1,0:T(8,128)(2,1)}, u32[]{:S(2)}) %copy-start) | copy-done | bytes 3670040
  91.7 2.3 %middle_part.1 = (bf16[416,128]{1,0:T(8,128)(2,1)S(1)}, bf16[416,128]{1,0:T(8,128)(2,1)S(1)}, f32[24,1024]{1,0:T(8,128)S(1)}, bf16[256,1024]{1,0:T(8,128)(2,1)S(1)}) custom-call(s32[1]{0:T(128)} %bitcast.6.at_ref, f32[2,3]{1,0:T(2,128)S(1)} %bitcast.27, bf16[16,2,64,128]{3,2,1,0:T(8,128)(2,1)S(1)} %bitcast.16, bf16[16,112,1024]{2,1,0:T(8,128)(2,1)S(1)} %bitcast.13, ...), custom_call_target="tpu_custom_call" | custom-call | flops 67108864 | bytes 4194304 | tf_op jit(solution)/shard_map/middle_part/pallas_call | solution.py:502
  94.0 8.2 %collective-permute-start.1 = (bf16[416,128]{1,0:T(8,128)(2,1)S(1)}, bf16[416,128]{1,0:T(8,128)(2,1)S(1)}, u32[]{:S(2)}, u32[]{:S(2)}) collective-permute-start(bf16[416,128]{1,0:T(8,128)(2,1)S(1)} %get-tuple-element.28.low_ref), channel_id=1, source_target_pairs={{16,0},{32,16},{48,32},{64,48},{80,64},{96,80},{112,96},{128,112},... | collective-permute-start | bytes 319496 | tf_op jit(solution)/shard_map/ppermute | solution.py:517
  102.2 3.0 %collective-permute-start = (bf16[416,128]{1,0:T(8,128)(2,1)S(1)}, bf16[416,128]{1,0:T(8,128)(2,1)S(1)}, u32[]{:S(2)}, u32[]{:S(2)}) collective-permute-start(bf16[416,128]{1,0:T(8,128)(2,1)S(1)} %get-tuple-element.29.high_ref), channel_id=1, source_target_pairs={{0,16},{16,32},{32,48},{48,64},{64,80},{80,96},{96,112},{112,128},... | collective-permute-start | bytes 319496 | tf_op jit(solution)/shard_map/ppermute | solution.py:516
  105.6 1.2 collective-permute-done.left_ref
  106.9 4.9 %layer_part.1 = bf16[16,144,128]{2,1,0:T(8,128)(2,1)} custom-call(bf16[416,128]{1,0:T(8,128)(2,1)S(1)} %get-tuple-element.28.low_ref, bf16[416,128]{1,0:T(8,128)(2,1)S(1)} %get-tuple-element.29.high_ref, bf16[416,128]{1,0:T(8,128)(2,1)S(1)} %collective-permute-done.left_ref, bf16[416,128]{1,0:T(8,128)(2,1)S(1)} %collective-permute-done.1.right_ref, ...), custom_call_target="tpu_custom_call" | custom-call | flops 67108864 | bytes 4194304 | tf_op jit(solution)/shard_map/layer_part/pallas_call | solution.py:532
  111.7 6.1 %all-to-all-start.2 = ((bf16[16,144,128]{2,1,0:T(8,128)(2,1)}), bf16[16,144,128]{2,1,0:T(8,128)(2,1)S(1)}, u32[]{:S(2)}, u32[]{:S(2)}) async-start(bf16[16,144,128]{2,1,0:T(8,128)(2,1)} %layer_part.1), calls=%async_computation.2 | async-start | bytes 1179648 | tf_op jit(solution)/shard_map/all_to_all | solution.py:440
  117.9 2.0 %copy-done.2 = bf16[1792,1024]{1,0:T(8,128)(2,1)S(1)} copy-done((bf16[1792,1024]{1,0:T(8,128)(2,1)S(1)}, bf16[1792,1024]{1,0:T(8,128)(2,1)}, u32[]{:S(2)}) %copy-start.2) | copy-done | bytes 3670040
  120.5 7.1 %collective-permute-start.2 = (bf16[16,32,1024]{2,1,0:T(8,128)(2,1)S(1)}, bf16[16,32,1024]{2,1,0:T(8,128)(2,1)}, u32[]{:S(2)}, u32[]{:S(2)}) collective-permute-start(bf16[16,32,1024]{2,1,0:T(8,128)(2,1)S(1)} %get-tuple-element.33.mine_ref), channel_id=1, source_target_pairs={{0,16},{16,0},{32,48},{48,32},{64,80},{80,64},{96,112},{112,96},{1... | collective-permute-start | bytes 3145736 | tf_op jit(solution)/shard_map/ppermute | solution.py:548
  127.6 12.4 %all-to-all-done.2.heads_ref.arrived_ref = bf16[16,144,128]{2,1,0:T(8,128)(2,1)S(1)} async-done(((bf16[16,144,128]{2,1,0:T(8,128)(2,1)}), bf16[16,144,128]{2,1,0:T(8,128)(2,1)S(1)}, u32[]{:S(2)}, u32[]{:S(2)}) %all-to-all-start.2) | async-done | bytes 589856 | tf_op jit(solution)/shard_map/all_to_all | solution.py:440
  140.0 1.0 grad_part.1
  141.0 27.6 %all_to_all.25.grads_ref = bf16[32,64,128]{2,1,0:T(8,128)(2,1)} all-to-all(bf16[32,64,128]{2,1,0:T(8,128)(2,1)S(1)} %get-tuple-element.40), channel_id=1, replica_groups=mesh['grid'=32,'head'=16] {'grid'}, dimensions={0} | all-to-all | bytes 1048576 | tf_op jit(solution)/shard_map/all_to_all | solution.py:440
  168.6 6.9 %final_part.1 = bf16[32,32,128]{2,1,0:T(8,128)(2,1)} custom-call(s32[32]{0:T(128)} %bitcast.31, s32[2,30]{1,0:T(2,128)} %slot_ref.5, s32[2]{0:T(128)} %count_ref.5, f32[2,30]{1,0:T(2,128)} %bitcast.24, bf16[1024,1024]{1,0:T(8,128)(2,1)} %get-tuple-element.34.norm_ref, bf16[8,128,128]{2,1,0:T(8,128)(2,1)} %get-tuple-element.24.own_ref.kv_ref, ...), custom_call_target="tpu_custom_call" | custom-call | flops 67108864 | bytes 4194304 | tf_op jit(solution)/shard_map/final_part/pallas_call | solution.py:549
  175.5 4.0 %all-to-all-start.4 = ((bf16[32,32,128]{2,1,0:T(8,128)(2,1)}), bf16[32,32,128]{2,1,0:T(8,128)(2,1)S(1)}, u32[]{:S(2)}, u32[]{:S(2)}) async-start(bf16[32,32,128]{2,1,0:T(8,128)(2,1)} %final_part.1), calls=%async_computation.4 | async-start | bytes 524288 | tf_op jit(solution)/shard_map/all_to_all | solution.py:440
  179.5 2.3 %output_part.1 = bf16[16,1024]{1,0:T(8,128)(2,1)} custom-call(s32[1]{0:T(128)} %bitcast.me_ref, bf16[16,144,128]{2,1,0:T(8,128)(2,1)S(1)} %all-to-all-done.2.heads_ref.arrived_ref, bf16[16,32,1024]{2,1,0:T(8,128)(2,1)S(1)} %get-tuple-element.33.mine_ref, bf16[16,32,1024]{2,1,0:T(8,128)(2,1)} %collective-permute-done.2.other_ref, ...), custom_call_target="tpu_custom_call" | custom-call | flops 67108864 | bytes 4194304 | tf_op jit(solution)/shard_map/output_part/pallas_call | solution.py:568
  181.8 6.7 %all-to-all-done.4.parts_ref = bf16[32,32,128]{2,1,0:T(8,128)(2,1)S(1)} async-done(((bf16[32,32,128]{2,1,0:T(8,128)(2,1)}), bf16[32,32,128]{2,1,0:T(8,128)(2,1)S(1)}, u32[]{:S(2)}, u32[]{:S(2)}) %all-to-all-start.4) | async-done | bytes 262176 | tf_op jit(solution)/shard_map/all_to_all | solution.py:440
  188.5 0.7 sum_part.1
  (44 shorter events, 2.4 us)
Async XLA Ops:
  7.2 82.5 %all-gather.4.cloned.1.call-start = ((), (), s32[]{:S(2)}) async-start(), calls=%async_computation.5 | async-start | bytes 3899392 | tf_op jit(solution)/shard_map/all_gather | solution.py:477
  8.9 16.3 %copy-start.3 = (bf16[256,1024]{1,0:T(8,128)(2,1)S(1)}, bf16[256,1024]{1,0:T(8,128)(2,1)}, u32[]{:S(2)}) copy-start(bf16[256,1024]{1,0:T(8,128)(2,1)} %mesh_ref.3) | copy-start | bytes 1572868
  8.9 16.3 %copy-start.12 = (bf16[1024,64]{0,1:T(8,128)(2,1)S(1)}, bf16[1024,64]{0,1:T(8,128)(2,1)}, u32[]{:S(2)}) copy-start(bf16[1024,64]{0,1:T(8,128)(2,1)} %param.18) | copy-start | bytes 393220
  8.9 33.5 %copy-start.14 = (s32[2,30]{1,0:T(2,128)S(1)}, s32[2,30]{1,0:T(2,128)}, u32[]{:S(2)}) copy-start(s32[2,30]{1,0:T(2,128)} %slot_ref.5) | copy-start | bytes 724
  9.0 33.5 %copy-start.15 = (f32[2,30,1]{1,2,0:T(1,128)S(1)}, f32[2,30,1]{1,2,0:T(1,128)}, u32[]{:S(2)}) copy-start(f32[2,30,1]{1,2,0:T(1,128)} %param.26) | copy-start | bytes 724
  9.0 33.5 %copy-start.17 = (s32[2]{0:T(128)S(1)}, s32[2]{0:T(128)}, u32[]{:S(2)}) copy-start(s32[2]{0:T(128)} %count_ref.5) | copy-start | bytes 28
  14.6 27.9 %copy-start.4 = (bf16[8,128,128]{2,1,0:T(8,128)(2,1)S(1)}, bf16[8,128,128]{2,1,0:T(8,128)(2,1)}, u32[]{:S(2)}) copy-start(bf16[8,128,128]{2,1,0:T(8,128)(2,1)} %get-tuple-element.24.own_ref.kv_ref) | copy-start | bytes 786436
  14.6 27.9 %all-to-all-start = ((bf16[32,128,128]{2,1,0:T(8,128)(2,1)}), bf16[32,128,128]{2,1,0:T(8,128)(2,1)S(1)}, u32[]{:S(2)}, u32[]{:S(2)}) async-start(bf16[32,128,128]{2,1,0:T(8,128)(2,1)} %get-tuple-element.25), calls=%async_computation | async-start | bytes 2097152 | tf_op jit(solution)/shard_map/all_to_all | solution.py:440
  25.8 63.8 %copy-start.10 = (bf16[2,64,128]{2,1,0:T(8,128)(2,1)}, bf16[2,64,128]{2,1,0:T(8,128)(2,1)S(1)}, u32[]{:S(2)}) copy-start(bf16[2,64,128]{2,1,0:T(8,128)(2,1)S(1)} %query_part.1.query_ref) | copy-start | bytes 98308
  42.5 47.1 %copy-start.5 = (bf16[1024,64]{0,1:T(8,128)(2,1)S(1)}, bf16[1024,64]{0,1:T(8,128)(2,1)}, u32[]{:S(2)}) copy-start(bf16[1024,64]{0,1:T(8,128)(2,1)} %param.22) | copy-start | bytes 393220
  42.5 47.1 %copy-start.6 = (bf16[1024,64]{0,1:T(8,128)(2,1)S(1)}, bf16[1024,64]{0,1:T(8,128)(2,1)}, u32[]{:S(2)}) copy-start(bf16[1024,64]{0,1:T(8,128)(2,1)} %param.23) | copy-start | bytes 393220
  42.5 47.1 %copy-start.7 = (bf16[1024,64]{0,1:T(8,128)(2,1)S(1)}, bf16[1024,64]{0,1:T(8,128)(2,1)}, u32[]{:S(2)}) copy-start(bf16[1024,64]{0,1:T(8,128)(2,1)} %param.24) | copy-start | bytes 393220
  42.5 47.1 %copy-start.8 = (bf16[64,1024]{1,0:T(8,128)(2,1)S(1)}, bf16[64,1024]{1,0:T(8,128)(2,1)}, u32[]{:S(2)}) copy-start(bf16[64,1024]{1,0:T(8,128)(2,1)} %wl_ref.3) | copy-start | bytes 393220
  42.5 47.1 %copy-start.18 = (f32[2,3,1]{1,2,0:T(1,128)S(1)}, f32[2,3,1]{1,2,0:T(1,128)}, u32[]{:S(2)}) copy-start(f32[2,3,1]{1,2,0:T(1,128)} %param.27) | copy-start | bytes 76
  50.3 43.7 %copy-start.11 = (bf16[2,64,128]{2,1,0:T(8,128)(2,1)}, bf16[2,64,128]{2,1,0:T(8,128)(2,1)S(1)}, u32[]{:S(2)}) copy-start(bf16[2,64,128]{2,1,0:T(8,128)(2,1)S(1)} %get-tuple-element.27.heads_ref) | copy-start | bytes 98308
  50.3 61.5 %all-to-all-start.1 = ((bf16[32,144,128]{2,1,0:T(8,128)(2,1)}), bf16[32,144,128]{2,1,0:T(8,128)(2,1)}, u32[]{:S(2)}, u32[]{:S(2)}) async-start(bf16[32,144,128]{2,1,0:T(8,128)(2,1)} %get-tuple-element.26), calls=%async_computation.1 | async-start | bytes 2359296 | tf_op jit(solution)/shard_map/all_to_all | solution.py:440
  91.7 15.2 %copy-start.1 = (bf16[1792,1024]{1,0:T(8,128)(2,1)S(1)}, bf16[1792,1024]{1,0:T(8,128)(2,1)}, u32[]{:S(2)}) copy-start(bf16[1792,1024]{1,0:T(8,128)(2,1)} %all-gather.4.cloned.1.call-done) | copy-start | bytes 11010052
  94.0 11.6 %collective-permute-start.1 = (bf16[416,128]{1,0:T(8,128)(2,1)S(1)}, bf16[416,128]{1,0:T(8,128)(2,1)S(1)}, u32[]{:S(2)}, u32[]{:S(2)}) collective-permute-start(bf16[416,128]{1,0:T(8,128)(2,1)S(1)} %get-tuple-element.28.low_ref), channel_id=1, source_target_pairs={{16,0},{32,16},{48,32},{64,48},{80,64},{96,80},{112,96},{128,112},... | collective-permute-start | bytes 319496 | tf_op jit(solution)/shard_map/ppermute | solution.py:517
  102.2 4.7 %collective-permute-start = (bf16[416,128]{1,0:T(8,128)(2,1)S(1)}, bf16[416,128]{1,0:T(8,128)(2,1)S(1)}, u32[]{:S(2)}, u32[]{:S(2)}) collective-permute-start(bf16[416,128]{1,0:T(8,128)(2,1)S(1)} %get-tuple-element.29.high_ref), channel_id=1, source_target_pairs={{0,16},{16,32},{32,48},{48,64},{64,80},{80,96},{96,112},{112,128},... | collective-permute-start | bytes 319496 | tf_op jit(solution)/shard_map/ppermute | solution.py:516
  106.9 11.0 %copy-start.9 = (bf16[64,1024]{1,0:T(8,128)(2,1)S(1)}, bf16[64,1024]{1,0:T(8,128)(2,1)}, u32[]{:S(2)}) copy-start(bf16[64,1024]{1,0:T(8,128)(2,1)} %wo_ref.3) | copy-start | bytes 393220
  111.7 28.3 %all-to-all-start.2 = ((bf16[16,144,128]{2,1,0:T(8,128)(2,1)}), bf16[16,144,128]{2,1,0:T(8,128)(2,1)S(1)}, u32[]{:S(2)}, u32[]{:S(2)}) async-start(bf16[16,144,128]{2,1,0:T(8,128)(2,1)} %layer_part.1), calls=%async_computation.2 | async-start | bytes 1179648 | tf_op jit(solution)/shard_map/all_to_all | solution.py:440
  120.5 59.0 %collective-permute-start.2 = (bf16[16,32,1024]{2,1,0:T(8,128)(2,1)S(1)}, bf16[16,32,1024]{2,1,0:T(8,128)(2,1)}, u32[]{:S(2)}, u32[]{:S(2)}) collective-permute-start(bf16[16,32,1024]{2,1,0:T(8,128)(2,1)S(1)} %get-tuple-element.33.mine_ref), channel_id=1, source_target_pairs={{0,16},{16,0},{32,48},{48,32},{64,80},{80,64},{96,112},{112,96},{1... | collective-permute-start | bytes 3145736 | tf_op jit(solution)/shard_map/ppermute | solution.py:548
  141.0 27.6 %copy-start.13 = (bf16[2,64,128]{2,1,0:T(8,128)(2,1)}, bf16[2,64,128]{2,1,0:T(8,128)(2,1)S(1)}, u32[]{:S(2)}) copy-start(bf16[2,64,128]{2,1,0:T(8,128)(2,1)S(1)} %get-tuple-element.42.grad_ref) | copy-start | bytes 98308
  175.5 13.0 %all-to-all-start.4 = ((bf16[32,32,128]{2,1,0:T(8,128)(2,1)}), bf16[32,32,128]{2,1,0:T(8,128)(2,1)S(1)}, u32[]{:S(2)}, u32[]{:S(2)}) async-start(bf16[32,32,128]{2,1,0:T(8,128)(2,1)} %final_part.1), calls=%async_computation.4 | async-start | bytes 524288 | tf_op jit(solution)/shard_map/all_to_all | solution.py:440
  (3 other events, 4.7 us)
Sparse Core Ops, SparseCore 0:
  10.1 76.9 all-gather.3

commit v9 on v8

--- a/solution.py
+++ b/solution.py
@@ -157,12 +157,17 @@
     for m, total in ((full, FULL), (1 - full, REST)):
         stack = jnp.concatenate([query_ref[m], jnp.zeros((D, B), bf16)], axis=0)
 
-        def scores(e, top, m=m, stack=stack):
-            value = dot(pool_ref[slot_ref[m, e]], stack) + bias_ref[m, e]
-            score_ref[e] = value
-            return jnp.maximum(top, folded(jnp.maximum, value))
-
-        top = lax.fori_loop(0, total, scores, jnp.full((8, B), -jnp.inf, f32), unroll=3)
+        def scores(i, top, m=m, stack=stack):
+            values = []
+            for k in range(3):
+                e = 3 * i + k
+                values.append(dot(pool_ref[slot_ref[m, e]], stack) + bias_ref[m, e])
+            for k in range(3):
+                score_ref[3 * i + k] = values[k]
+                top = jnp.maximum(top, folded(jnp.maximum, values[k]))
+            return top
+
+        top = lax.fori_loop(0, total // 3, scores, jnp.full((8, B), -jnp.inf, f32))
         top = jnp.max(top, axis=0, keepdims=True)
 
         def mix(e, carry, m=m, top=top):
@@ -386,26 +391,38 @@
         )
         return dot(mixed, pair, NT)
 
-    def own_step(v, carry):
-        m = reader_ref[v]
-        shift = lse_ref[m][0:1] - edge_ref[v]
-        acc_ref[v] = back(kv_ref[v], query_ref[m], heads_ref[m], shift, grad_ref[m])
+    group = 4
+
+    def own_step(i, carry):
+        parts = []
+        for k in range(group):
+            v = i * group + k
+            m = reader_ref[v]
+            shift = lse_ref[m][0:1] - edge_ref[v]
+            parts.append(back(kv_ref[v], query_ref[m], heads_ref[m], shift, grad_ref[m]))
+        for k in range(group):
+            acc_ref[i * group + k] = parts[k]
         return carry
 
-    lax.fori_loop(0, kv_ref.shape[0], own_step, 0, unroll=4)
-
-    def sent_step(r, carry):
-        slot = send_ref[r]
-        block = block_ref[r]
-        tail = block[2 * D :].astype(f32)
-        shift = tail[0:1] + tail[1:2] + tail[2:3]
-        part = back(kv_ref[slot], block[:D], block[D : 2 * D], shift, part_ref[r])
-        acc_ref[slot] = acc_ref[slot] + part
+    lax.fori_loop(0, kv_ref.shape[0] // group, own_step, 0)
+
+    def sent_step(i, carry):
+        parts = []
+        for k in range(group):
+            r = i * group + k
+            block = block_ref[r]
+            tail = block[2 * D :].astype(f32)
+            shift = tail[0:1] + tail[1:2] + tail[2:3]
+            keys = kv_ref[send_ref[r]]
+            parts.append(back(keys, block[:D], block[D : 2 * D], shift, part_ref[r]))
+        for k in range(group):
+            slot = send_ref[i * group + k]
+            acc_ref[slot] = acc_ref[slot] + parts[k]
         return carry
 
     copies[0].wait()
     copies[1].wait()
-    lax.fori_loop(0, block_ref.shape[0], sent_step, 0, unroll=4)
+    lax.fori_loop(0, block_ref.shape[0] // group, sent_step, 0)
     rows = acc_ref[...].reshape(norm_ref.shape[0], 2 * D).astype(bf16)
     copies[2].wait()
     shards, height = out_ref.shape[0], out_ref.shape[1]

time: 197 us -> 197 us (level)
  no operation moved by 1% of the time
where the time goes in v9:
time: 197 us; the launch traced here: 196 us
  blocking collectives  62.3 us (32%)
  starting transfers between devices  43.2 us (22%)
  waiting for transfers between devices  37.9 us (19%)
  Pallas kernels  33.7 us (17%)
  between operations  14.3 us (7%)
  local copies, waits for them, and re-layouts  4.75 us (2%)
    all_to_all x4, waiting for transfers between devices, exchange(): return lax.all_to_all(array, axis, split_axis=0, concat_axis=0, tiled=True)  36.2 us
    all_gather x1, blocking collectives, on_device(): all_heads = lax.all_gather(enc_heads, 'head', axis=0, tiled=False)  34.9 us
    all_to_all x1, blocking collectives, exchange(): return lax.all_to_all(array, axis, split_axis=0, concat_axis=0, tiled=True)  27.4 us
    all_to_all x4, starting transfers between devices, exchange(): return lax.all_to_all(array, axis, split_axis=0, concat_axis=0, tiled=True)  25.3 us
    ppermute x1, starting transfers between devices, on_device(): right = lax.ppermute(low, 'grid', backward)  7.82 us
    pallas_call x1, Pallas kernels, on_device(): call(encoder_kernel, (struct((2, D, B), bf16), struct((2, 8, B), f32), st...  7.16 us
    ppermute x1, starting transfers between devices, on_device(): lax.ppermute(half_mine, 'grid', [(i, i ^ 1) for i in range(shards)])  6.92 us
    pallas_call x1, Pallas kernels, on_device(): call(final_kernel, struct((shards, C // shards, 2 * D), bf16), [SMEM] * 4...  6.85 us
  transfers between devices with their start and end apart: 8, of which 5 were waited for; matrix products, arithmetic and copies ran while one was open for 0% of the time, Pallas kernels for 16%

profile of v9, /device:TPU:1, one launch (start us, length us, event | category | flops | bytes accessed | tf_op | source)
XLA Modules:
  0.0 196.2 jit_solution(16672738901813356970)
XLA Ops:
  7.2 1.7 rows_part.1
  9.0 5.6 %grid_part.1 = (bf16[1024,1024]{1,0:T(8,128)(2,1)}, bf16[8,128,128]{2,1,0:T(8,128)(2,1)}, bf16[32,128,128]{2,1,0:T(8,128)(2,1)}) custom-call(s32[32]{0:T(128)} %bitcast.30, bf16[1024,1024]{1,0:T(8,128)(2,1)} %feat_ref.1, bf16[64,1024]{1,0:T(8,128)(2,1)} %bitcast.28, bf16[64,1024]{1,0:T(8,128)(2,1)} %bitcast.29), custom_call_target="tpu_custom_call" | custom-call | flops 268435456 | bytes 6291456 | tf_op jit(solution)/shard_map/grid_part/pallas_call | solution.py:75
  14.6 10.6 %all-to-all-start = ((bf16[32,128,128]{2,1,0:T(8,128)(2,1)}), bf16[32,128,128]{2,1,0:T(8,128)(2,1)S(1)}, u32[]{:S(2)}, u32[]{:S(2)}) async-start(bf16[32,128,128]{2,1,0:T(8,128)(2,1)} %get-tuple-element.25), calls=%async_computation | async-start | bytes 2097152 | tf_op jit(solution)/shard_map/all_to_all | solution.py:457
  25.8 16.6 %all-to-all-done.arrived_ref = bf16[32,128,128]{2,1,0:T(8,128)(2,1)S(1)} async-done(((bf16[32,128,128]{2,1,0:T(8,128)(2,1)}), bf16[32,128,128]{2,1,0:T(8,128)(2,1)S(1)}, u32[]{:S(2)}, u32[]{:S(2)}) %all-to-all-start) | async-done | bytes 1048608 | tf_op jit(solution)/shard_map/all_to_all | solution.py:457
  42.6 7.2 %encoder_part.1 = (bf16[2,64,128]{2,1,0:T(8,128)(2,1)S(1)}, f32[2,8,128]{2,1,0:T(8,128)S(1)}, bf16[32,144,128]{2,1,0:T(8,128)(2,1)}) custom-call(s32[2,30]{1,0:T(2,128)S(1)} %copy-done.14, s32[2]{0:T(128)S(1)} %copy-done.17, f32[2,30]{1,0:T(2,128)S(1)} %bitcast.25, s32[1]{0:T(128)} %bitcast.me_ref, bf16[8,128,128]{2,1,0:T(8,128)(2,1)S(1)} %copy-done.4, ...), custom_call_target="tpu_custom_call" | custom-call | flops 67108864 | bytes 4194304 | tf_op jit(solution)/shard_map/encoder_part/pallas_call | solution.py:506
  50.3 4.7 %all-to-all-start.1 = ((bf16[32,144,128]{2,1,0:T(8,128)(2,1)}), bf16[32,144,128]{2,1,0:T(8,128)(2,1)}, u32[]{:S(2)}, u32[]{:S(2)}) async-start(bf16[32,144,128]{2,1,0:T(8,128)(2,1)} %get-tuple-element.26), calls=%async_computation.1 | async-start | bytes 2359296 | tf_op jit(solution)/shard_map/all_to_all | solution.py:457
  55.0 34.9 %all-gather = bf16[32,64,128]{2,1,0:T(8,128)(2,1)S(1)} all-gather(bf16[2,64,128]{2,1,0:T(8,128)(2,1)S(1)} %get-tuple-element.27.heads_ref), channel_id=2, replica_groups=mesh['grid'=32,'head'=16] {'head'}, dimensions={0}, use_global_device_ids=true | all-gather | bytes 557056 | tf_op jit(solution)/shard_map/all_gather | solution.py:518
  89.9 2.0 %copy-done = bf16[1792,1024]{1,0:T(8,128)(2,1)S(1)} copy-done((bf16[1792,1024]{1,0:T(8,128)(2,1)S(1)}, bf16[1792,1024]{1,0:T(8,128)(2,1)}, u32[]{:S(2)}) %copy-start) | copy-done | bytes 3670040
  92.0 2.3 %middle_part.1 = (bf16[416,128]{1,0:T(8,128)(2,1)S(1)}, bf16[416,128]{1,0:T(8,128)(2,1)S(1)}, f32[24,1024]{1,0:T(8,128)S(1)}, bf16[256,1024]{1,0:T(8,128)(2,1)S(1)}) custom-call(s32[1]{0:T(128)} %bitcast.6.at_ref, f32[2,3]{1,0:T(2,128)S(1)} %bitcast.27, bf16[16,2,64,128]{3,2,1,0:T(8,128)(2,1)S(1)} %bitcast.16, bf16[16,112,1024]{2,1,0:T(8,128)(2,1)S(1)} %bitcast.13, ...), custom_call_target="tpu_custom_call" | custom-call | flops 67108864 | bytes 4194304 | tf_op jit(solution)/shard_map/middle_part/pallas_call | solution.py:519
  94.2 7.8 %collective-permute-start.1 = (bf16[416,128]{1,0:T(8,128)(2,1)S(1)}, bf16[416,128]{1,0:T(8,128)(2,1)S(1)}, u32[]{:S(2)}, u32[]{:S(2)}) collective-permute-start(bf16[416,128]{1,0:T(8,128)(2,1)S(1)} %get-tuple-element.28.low_ref), channel_id=1, source_target_pairs={{16,0},{32,16},{48,32},{64,48},{80,64},{96,80},{112,96},{128,112},... | collective-permute-start | bytes 319496 | tf_op jit(solution)/shard_map/ppermute | solution.py:534
  102.1 3.1 %collective-permute-start = (bf16[416,128]{1,0:T(8,128)(2,1)S(1)}, bf16[416,128]{1,0:T(8,128)(2,1)S(1)}, u32[]{:S(2)}, u32[]{:S(2)}) collective-permute-start(bf16[416,128]{1,0:T(8,128)(2,1)S(1)} %get-tuple-element.29.high_ref), channel_id=1, source_target_pairs={{0,16},{16,32},{32,48},{48,64},{64,80},{80,96},{96,112},{112,128},... | collective-permute-start | bytes 319496 | tf_op jit(solution)/shard_map/ppermute | solution.py:533
  105.7 1.2 collective-permute-done.left_ref
  106.9 4.9 %layer_part.1 = bf16[16,144,128]{2,1,0:T(8,128)(2,1)} custom-call(bf16[416,128]{1,0:T(8,128)(2,1)S(1)} %get-tuple-element.28.low_ref, bf16[416,128]{1,0:T(8,128)(2,1)S(1)} %get-tuple-element.29.high_ref, bf16[416,128]{1,0:T(8,128)(2,1)S(1)} %collective-permute-done.left_ref, bf16[416,128]{1,0:T(8,128)(2,1)S(1)} %collective-permute-done.1.right_ref, ...), custom_call_target="tpu_custom_call" | custom-call | flops 67108864 | bytes 4194304 | tf_op jit(solution)/shard_map/layer_part/pallas_call | solution.py:549
  111.8 6.1 %all-to-all-start.2 = ((bf16[16,144,128]{2,1,0:T(8,128)(2,1)}), bf16[16,144,128]{2,1,0:T(8,128)(2,1)S(1)}, u32[]{:S(2)}, u32[]{:S(2)}) async-start(bf16[16,144,128]{2,1,0:T(8,128)(2,1)} %layer_part.1), calls=%async_computation.2 | async-start | bytes 1179648 | tf_op jit(solution)/shard_map/all_to_all | solution.py:457
  117.9 2.0 %copy-done.2 = bf16[1792,1024]{1,0:T(8,128)(2,1)S(1)} copy-done((bf16[1792,1024]{1,0:T(8,128)(2,1)S(1)}, bf16[1792,1024]{1,0:T(8,128)(2,1)}, u32[]{:S(2)}) %copy-start.2) | copy-done | bytes 3670040
  120.5 6.9 %collective-permute-start.2 = (bf16[16,32,1024]{2,1,0:T(8,128)(2,1)S(1)}, bf16[16,32,1024]{2,1,0:T(8,128)(2,1)}, u32[]{:S(2)}, u32[]{:S(2)}) collective-permute-start(bf16[16,32,1024]{2,1,0:T(8,128)(2,1)S(1)} %get-tuple-element.33.mine_ref), channel_id=1, source_target_pairs={{0,16},{16,0},{32,48},{48,32},{64,80},{80,64},{96,112},{112,96},{1... | collective-permute-start | bytes 3145736 | tf_op jit(solution)/shard_map/ppermute | solution.py:565
  127.4 12.9 %all-to-all-done.2.heads_ref.arrived_ref = bf16[16,144,128]{2,1,0:T(8,128)(2,1)S(1)} async-done(((bf16[16,144,128]{2,1,0:T(8,128)(2,1)}), bf16[16,144,128]{2,1,0:T(8,128)(2,1)S(1)}, u32[]{:S(2)}, u32[]{:S(2)}) %all-to-all-start.2) | async-done | bytes 589856 | tf_op jit(solution)/shard_map/all_to_all | solution.py:457
  140.3 1.0 grad_part.1
  141.3 27.4 %all_to_all.25.grads_ref = bf16[32,64,128]{2,1,0:T(8,128)(2,1)} all-to-all(bf16[32,64,128]{2,1,0:T(8,128)(2,1)S(1)} %get-tuple-element.40), channel_id=1, replica_groups=mesh['grid'=32,'head'=16] {'grid'}, dimensions={0} | all-to-all | bytes 1048576 | tf_op jit(solution)/shard_map/all_to_all | solution.py:457
  168.7 6.9 %final_part.1 = bf16[32,32,128]{2,1,0:T(8,128)(2,1)} custom-call(s32[32]{0:T(128)} %bitcast.31, s32[2,30]{1,0:T(2,128)} %slot_ref.5, s32[2]{0:T(128)} %count_ref.5, f32[2,30]{1,0:T(2,128)} %bitcast.24, bf16[1024,1024]{1,0:T(8,128)(2,1)} %get-tuple-element.34.norm_ref, bf16[8,128,128]{2,1,0:T(8,128)(2,1)} %get-tuple-element.24.own_ref.kv_ref, ...), custom_call_target="tpu_custom_call" | custom-call | flops 67108864 | bytes 4194304 | tf_op jit(solution)/shard_map/final_part/pallas_call | solution.py:566
  175.6 4.0 %all-to-all-start.4 = ((bf16[32,32,128]{2,1,0:T(8,128)(2,1)}), bf16[32,32,128]{2,1,0:T(8,128)(2,1)S(1)}, u32[]{:S(2)}, u32[]{:S(2)}) async-start(bf16[32,32,128]{2,1,0:T(8,128)(2,1)} %final_part.1), calls=%async_computation.4 | async-start | bytes 524288 | tf_op jit(solution)/shard_map/all_to_all | solution.py:457
  179.6 2.3 %output_part.1 = bf16[16,1024]{1,0:T(8,128)(2,1)} custom-call(s32[1]{0:T(128)} %bitcast.me_ref, bf16[16,144,128]{2,1,0:T(8,128)(2,1)S(1)} %all-to-all-done.2.heads_ref.arrived_ref, bf16[16,32,1024]{2,1,0:T(8,128)(2,1)S(1)} %get-tuple-element.33.mine_ref, bf16[16,32,1024]{2,1,0:T(8,128)(2,1)} %collective-permute-done.2.other_ref, ...), custom_call_target="tpu_custom_call" | custom-call | flops 67108864 | bytes 4194304 | tf_op jit(solution)/shard_map/output_part/pallas_call | solution.py:585
  181.9 6.7 %all-to-all-done.4.parts_ref = bf16[32,32,128]{2,1,0:T(8,128)(2,1)S(1)} async-done(((bf16[32,32,128]{2,1,0:T(8,128)(2,1)}), bf16[32,32,128]{2,1,0:T(8,128)(2,1)S(1)}, u32[]{:S(2)}, u32[]{:S(2)}) %all-to-all-start.4) | async-done | bytes 262176 | tf_op jit(solution)/shard_map/all_to_all | solution.py:457
  188.6 0.7 sum_part.1
  (44 shorter events, 2.4 us)
Async XLA Ops:
  7.2 82.7 %all-gather.4.cloned.1.call-start = ((), (), s32[]{:S(2)}) async-start(), calls=%async_computation.5 | async-start | bytes 3899392 | tf_op jit(solution)/shard_map/all_gather | solution.py:494
  8.9 16.3 %copy-start.3 = (bf16[256,1024]{1,0:T(8,128)(2,1)S(1)}, bf16[256,1024]{1,0:T(8,128)(2,1)}, u32[]{:S(2)}) copy-start(bf16[256,1024]{1,0:T(8,128)(2,1)} %mesh_ref.3) | copy-start | bytes 1572868
  8.9 16.3 %copy-start.12 = (bf16[1024,64]{0,1:T(8,128)(2,1)S(1)}, bf16[1024,64]{0,1:T(8,128)(2,1)}, u32[]{:S(2)}) copy-start(bf16[1024,64]{0,1:T(8,128)(2,1)} %param.18) | copy-start | bytes 393220
  8.9 33.5 %copy-start.14 = (s32[2,30]{1,0:T(2,128)S(1)}, s32[2,30]{1,0:T(2,128)}, u32[]{:S(2)}) copy-start(s32[2,30]{1,0:T(2,128)} %slot_ref.5) | copy-start | bytes 724
  9.0 33.5 %copy-start.15 = (f32[2,30,1]{1,2,0:T(1,128)S(1)}, f32[2,30,1]{1,2,0:T(1,128)}, u32[]{:S(2)}) copy-start(f32[2,30,1]{1,2,0:T(1,128)} %param.26) | copy-start | bytes 724
  9.0 33.5 %copy-start.17 = (s32[2]{0:T(128)S(1)}, s32[2]{0:T(128)}, u32[]{:S(2)}) copy-start(s32[2]{0:T(128)} %count_ref.5) | copy-start | bytes 28
  14.6 27.9 %copy-start.4 = (bf16[8,128,128]{2,1,0:T(8,128)(2,1)S(1)}, bf16[8,128,128]{2,1,0:T(8,128)(2,1)}, u32[]{:S(2)}) copy-start(bf16[8,128,128]{2,1,0:T(8,128)(2,1)} %get-tuple-element.24.own_ref.kv_ref) | copy-start | bytes 786436
  14.6 27.9 %all-to-all-start = ((bf16[32,128,128]{2,1,0:T(8,128)(2,1)}), bf16[32,128,128]{2,1,0:T(8,128)(2,1)S(1)}, u32[]{:S(2)}, u32[]{:S(2)}) async-start(bf16[32,128,128]{2,1,0:T(8,128)(2,1)} %get-tuple-element.25), calls=%async_computation | async-start | bytes 2097152 | tf_op jit(solution)/shard_map/all_to_all | solution.py:457
  25.8 64.1 %copy-start.10 = (bf16[2,64,128]{2,1,0:T(8,128)(2,1)}, bf16[2,64,128]{2,1,0:T(8,128)(2,1)S(1)}, u32[]{:S(2)}) copy-start(bf16[2,64,128]{2,1,0:T(8,128)(2,1)S(1)} %query_part.1.query_ref) | copy-start | bytes 98308
  42.5 47.4 %copy-start.5 = (bf16[1024,64]{0,1:T(8,128)(2,1)S(1)}, bf16[1024,64]{0,1:T(8,128)(2,1)}, u32[]{:S(2)}) copy-start(bf16[1024,64]{0,1:T(8,128)(2,1)} %param.22) | copy-start | bytes 393220
  42.5 47.4 %copy-start.6 = (bf16[1024,64]{0,1:T(8,128)(2,1)S(1)}, bf16[1024,64]{0,1:T(8,128)(2,1)}, u32[]{:S(2)}) copy-start(bf16[1024,64]{0,1:T(8,128)(2,1)} %param.23) | copy-start | bytes 393220
  42.5 47.4 %copy-start.7 = (bf16[1024,64]{0,1:T(8,128)(2,1)S(1)}, bf16[1024,64]{0,1:T(8,128)(2,1)}, u32[]{:S(2)}) copy-start(bf16[1024,64]{0,1:T(8,128)(2,1)} %param.24) | copy-start | bytes 393220
  42.5 47.4 %copy-start.8 = (bf16[64,1024]{1,0:T(8,128)(2,1)S(1)}, bf16[64,1024]{1,0:T(8,128)(2,1)}, u32[]{:S(2)}) copy-start(bf16[64,1024]{1,0:T(8,128)(2,1)} %wl_ref.3) | copy-start | bytes 393220
  42.5 47.4 %copy-start.18 = (f32[2,3,1]{1,2,0:T(1,128)S(1)}, f32[2,3,1]{1,2,0:T(1,128)}, u32[]{:S(2)}) copy-start(f32[2,3,1]{1,2,0:T(1,128)} %param.27) | copy-start | bytes 76
  50.3 43.9 %copy-start.11 = (bf16[2,64,128]{2,1,0:T(8,128)(2,1)}, bf16[2,64,128]{2,1,0:T(8,128)(2,1)S(1)}, u32[]{:S(2)}) copy-start(bf16[2,64,128]{2,1,0:T(8,128)(2,1)S(1)} %get-tuple-element.27.heads_ref) | copy-start | bytes 98308
  50.3 61.5 %all-to-all-start.1 = ((bf16[32,144,128]{2,1,0:T(8,128)(2,1)}), bf16[32,144,128]{2,1,0:T(8,128)(2,1)}, u32[]{:S(2)}, u32[]{:S(2)}) async-start(bf16[32,144,128]{2,1,0:T(8,128)(2,1)} %get-tuple-element.26), calls=%async_computation.1 | async-start | bytes 2359296 | tf_op jit(solution)/shard_map/all_to_all | solution.py:457
  92.0 14.9 %copy-start.1 = (bf16[1792,1024]{1,0:T(8,128)(2,1)S(1)}, bf16[1792,1024]{1,0:T(8,128)(2,1)}, u32[]{:S(2)}) copy-start(bf16[1792,1024]{1,0:T(8,128)(2,1)} %all-gather.4.cloned.1.call-done) | copy-start | bytes 11010052
  94.2 11.4 %collective-permute-start.1 = (bf16[416,128]{1,0:T(8,128)(2,1)S(1)}, bf16[416,128]{1,0:T(8,128)(2,1)S(1)}, u32[]{:S(2)}, u32[]{:S(2)}) collective-permute-start(bf16[416,128]{1,0:T(8,128)(2,1)S(1)} %get-tuple-element.28.low_ref), channel_id=1, source_target_pairs={{16,0},{32,16},{48,32},{64,48},{80,64},{96,80},{112,96},{128,112},... | collective-permute-start | bytes 319496 | tf_op jit(solution)/shard_map/ppermute | solution.py:534
  102.1 4.8 %collective-permute-start = (bf16[416,128]{1,0:T(8,128)(2,1)S(1)}, bf16[416,128]{1,0:T(8,128)(2,1)S(1)}, u32[]{:S(2)}, u32[]{:S(2)}) collective-permute-start(bf16[416,128]{1,0:T(8,128)(2,1)S(1)} %get-tuple-element.29.high_ref), channel_id=1, source_target_pairs={{0,16},{16,32},{32,48},{48,64},{64,80},{80,96},{96,112},{112,128},... | collective-permute-start | bytes 319496 | tf_op jit(solution)/shard_map/ppermute | solution.py:533
  106.9 11.0 %copy-start.9 = (bf16[64,1024]{1,0:T(8,128)(2,1)S(1)}, bf16[64,1024]{1,0:T(8,128)(2,1)}, u32[]{:S(2)}) copy-start(bf16[64,1024]{1,0:T(8,128)(2,1)} %wo_ref.3) | copy-start | bytes 393220
  111.8 28.5 %all-to-all-start.2 = ((bf16[16,144,128]{2,1,0:T(8,128)(2,1)}), bf16[16,144,128]{2,1,0:T(8,128)(2,1)S(1)}, u32[]{:S(2)}, u32[]{:S(2)}) async-start(bf16[16,144,128]{2,1,0:T(8,128)(2,1)} %layer_part.1), calls=%async_computation.2 | async-start | bytes 1179648 | tf_op jit(solution)/shard_map/all_to_all | solution.py:457
  120.5 59.1 %collective-permute-start.2 = (bf16[16,32,1024]{2,1,0:T(8,128)(2,1)S(1)}, bf16[16,32,1024]{2,1,0:T(8,128)(2,1)}, u32[]{:S(2)}, u32[]{:S(2)}) collective-permute-start(bf16[16,32,1024]{2,1,0:T(8,128)(2,1)S(1)} %get-tuple-element.33.mine_ref), channel_id=1, source_target_pairs={{0,16},{16,0},{32,48},{48,32},{64,80},{80,64},{96,112},{112,96},{1... | collective-permute-start | bytes 3145736 | tf_op jit(solution)/shard_map/ppermute | solution.py:565
  141.3 27.4 %copy-start.13 = (bf16[2,64,128]{2,1,0:T(8,128)(2,1)}, bf16[2,64,128]{2,1,0:T(8,128)(2,1)S(1)}, u32[]{:S(2)}) copy-start(bf16[2,64,128]{2,1,0:T(8,128)(2,1)S(1)} %get-tuple-element.42.grad_ref) | copy-start | bytes 98308
  175.6 13.0 %all-to-all-start.4 = ((bf16[32,32,128]{2,1,0:T(8,128)(2,1)}), bf16[32,32,128]{2,1,0:T(8,128)(2,1)S(1)}, u32[]{:S(2)}, u32[]{:S(2)}) async-start(bf16[32,32,128]{2,1,0:T(8,128)(2,1)} %final_part.1), calls=%async_computation.4 | async-start | bytes 524288 | tf_op jit(solution)/shard_map/all_to_all | solution.py:457
  (3 other events, 4.7 us)
Sparse Core Ops, SparseCore 0:
  10.1 77.1 all-gather.3

commit v10 on v8

--- a/solution.py
+++ b/solution.py
@@ -204,11 +204,11 @@
     height = 2 * B // parts
     tail_ref[height:] = jnp.zeros((8, C), f32)
     messages = (left_ref, right_ref)
+    heads = jnp.concatenate([heads_ref[:, b].reshape(parts * D, B) for b in range(2)], axis=1)
+    enc_ref[...] = mesh_ref[...].astype(f32) + dot(heads, w_out, TN)
     for b in range(2):
         rows = slice(b * B, (b + 1) * B)
-        heads = heads_ref[:, b].reshape(parts * D, B)
-        enc = mesh_ref[rows].astype(f32) + dot(heads, w_out, TN)
-        enc_ref[rows] = enc
+        enc = enc_ref[rows]
         unit, inverse = normalize(enc)
         unit = unit.astype(bf16)
         unit_ref[rows] = unit
@@ -327,10 +327,15 @@
     total = jnp.concatenate(totals, axis=0)
     heads = jnp.concatenate(heads, axis=0)
     share = heads.shape[0] // parts
+    group = 4
+    for start in range(0, parts, group):
+        weight = gathered_ref[start : start + group, 0:D, :].reshape(group * D, C)
+        pieces = dot(weight, total, NT).astype(bf16)
+        for k in range(group):
+            for b in range(2):
+                block = pieces[k * D : (k + 1) * D, b * B : (b + 1) * B]
+                send_ref[start + k, b * D : (b + 1) * D] = block
     for z in range(parts):
-        piece = dot(gathered_ref[z, 0:D, :], total, NT).astype(bf16)
-        for b in range(2):
-            send_ref[z, b * D : (b + 1) * D] = piece[:, b * B : (b + 1) * B]
         rows = heads[z * share : (z + 1) * share]
         send_ref[z, 2 * D :] = jnp.concatenate([rows, stats], axis=1)
 
@@ -409,7 +414,7 @@
     rows = acc_ref[...].reshape(norm_ref.shape[0], 2 * D).astype(bf16)
     copies[2].wait()
     shards, height = out_ref.shape[0], out_ref.shape[1]
-    tile = 256
+    tile = 512
     for c in range(C // tile):
         part = dot(rows, held_ref[:, c * tile : (c + 1) * tile], TN).T
         per = tile // height

time: 197 us -> 195 us (0.990)
  Pallas kernels: 33.6 us -> 31.5 us
  transfers between devices with their start and end apart: 8 -> 8, of which waited for: 5 -> 5; matrix products, arithmetic and copies ran while one was open for 0% -> 0% of each run, Pallas kernels for 16% -> 15%
where the time goes in v10:
time: 195 us; the launch traced here: 194 us
  blocking collectives  61.5 us (32%)
  starting transfers between devices  43.7 us (22%)
  waiting for transfers between devices  38.2 us (20%)
  Pallas kernels  31.5 us (16%)
  between operations  14.3 us (7%)
  local copies, waits for them, and re-layouts  4.75 us (2%)
    all_to_all x4, waiting for transfers between devices, exchange(): return lax.all_to_all(array, axis, split_axis=0, concat_axis=0, tiled=True)  36.5 us
    all_gather x1, blocking collectives, on_device(): all_heads = lax.all_gather(enc_heads, 'head', axis=0, tiled=False)  34.6 us
    all_to_all x1, blocking collectives, exchange(): return lax.all_to_all(array, axis, split_axis=0, concat_axis=0, tiled=True)  26.9 us
    all_to_all x4, starting transfers between devices, exchange(): return lax.all_to_all(array, axis, split_axis=0, concat_axis=0, tiled=True)  25.7 us
    ppermute x1, starting transfers between devices, on_device(): right = lax.ppermute(low, 'grid', backward)  8.27 us
    pallas_call x1, Pallas kernels, on_device(): call(encoder_kernel, (struct((2, D, B), bf16), struct((2, 8, B), f32), st...  7.13 us
    pallas_call x1, Pallas kernels, on_device(): call(final_kernel, struct((shards, C // shards, 2 * D), bf16), [SMEM] * 4...  6.85 us
    ppermute x1, starting transfers between devices, on_device(): lax.ppermute(half_mine, 'grid', [(i, i ^ 1) for i in range(shards)])  6.77 us
  transfers between devices with their start and end apart: 8, of which 5 were waited for; matrix products, arithmetic and copies ran while one was open for 0% of the time, Pallas kernels for 15%

profile of v10, /device:TPU:1, one launch (start us, length us, event | category | flops | bytes accessed | tf_op | source)
XLA Modules:
  0.0 193.9 jit_solution(14526418001112562856)
XLA Ops:
  7.2 1.7 rows_part.1
  9.0 5.6 %grid_part.1 = (bf16[1024,1024]{1,0:T(8,128)(2,1)}, bf16[8,128,128]{2,1,0:T(8,128)(2,1)}, bf16[32,128,128]{2,1,0:T(8,128)(2,1)}) custom-call(s32[32]{0:T(128)} %bitcast.30, bf16[1024,1024]{1,0:T(8,128)(2,1)} %feat_ref.1, bf16[64,1024]{1,0:T(8,128)(2,1)} %bitcast.28, bf16[64,1024]{1,0:T(8,128)(2,1)} %bitcast.29), custom_call_target="tpu_custom_call" | custom-call | flops 268435456 | bytes 6291456 | tf_op jit(solution)/shard_map/grid_part/pallas_call | solution.py:75
  14.6 10.6 %all-to-all-start = ((bf16[32,128,128]{2,1,0:T(8,128)(2,1)}), bf16[32,128,128]{2,1,0:T(8,128)(2,1)S(1)}, u32[]{:S(2)}, u32[]{:S(2)}) async-start(bf16[32,128,128]{2,1,0:T(8,128)(2,1)} %get-tuple-element.25), calls=%async_computation | async-start | bytes 2097152 | tf_op jit(solution)/shard_map/all_to_all | solution.py:445
  25.8 16.6 %all-to-all-done.arrived_ref = bf16[32,128,128]{2,1,0:T(8,128)(2,1)S(1)} async-done(((bf16[32,128,128]{2,1,0:T(8,128)(2,1)}), bf16[32,128,128]{2,1,0:T(8,128)(2,1)S(1)}, u32[]{:S(2)}, u32[]{:S(2)}) %all-to-all-start) | async-done | bytes 1048608 | tf_op jit(solution)/shard_map/all_to_all | solution.py:445
  42.6 7.1 %encoder_part.1 = (bf16[2,64,128]{2,1,0:T(8,128)(2,1)S(1)}, f32[2,8,128]{2,1,0:T(8,128)S(1)}, bf16[32,144,128]{2,1,0:T(8,128)(2,1)}) custom-call(s32[2,30]{1,0:T(2,128)S(1)} %copy-done.14, s32[2]{0:T(128)S(1)} %copy-done.17, f32[2,30]{1,0:T(2,128)S(1)} %bitcast.25, s32[1]{0:T(128)} %bitcast.me_ref, bf16[8,128,128]{2,1,0:T(8,128)(2,1)S(1)} %copy-done.4, ...), custom_call_target="tpu_custom_call" | custom-call | flops 67108864 | bytes 4194304 | tf_op jit(solution)/shard_map/encoder_part/pallas_call | solution.py:494
  50.3 4.7 %all-to-all-start.1 = ((bf16[32,144,128]{2,1,0:T(8,128)(2,1)}), bf16[32,144,128]{2,1,0:T(8,128)(2,1)}, u32[]{:S(2)}, u32[]{:S(2)}) async-start(bf16[32,144,128]{2,1,0:T(8,128)(2,1)} %get-tuple-element.26), calls=%async_computation.1 | async-start | bytes 2359296 | tf_op jit(solution)/shard_map/all_to_all | solution.py:445
  55.0 34.6 %all-gather = bf16[32,64,128]{2,1,0:T(8,128)(2,1)S(1)} all-gather(bf16[2,64,128]{2,1,0:T(8,128)(2,1)S(1)} %get-tuple-element.27.heads_ref), channel_id=2, replica_groups=mesh['grid'=32,'head'=16] {'head'}, dimensions={0}, use_global_device_ids=true | all-gather | bytes 557056 | tf_op jit(solution)/shard_map/all_gather | solution.py:506
  89.6 2.0 %copy-done = bf16[1792,1024]{1,0:T(8,128)(2,1)S(1)} copy-done((bf16[1792,1024]{1,0:T(8,128)(2,1)S(1)}, bf16[1792,1024]{1,0:T(8,128)(2,1)}, u32[]{:S(2)}) %copy-start) | copy-done | bytes 3670040
  91.6 2.0 %middle_part.1 = (bf16[416,128]{1,0:T(8,128)(2,1)S(1)}, bf16[416,128]{1,0:T(8,128)(2,1)S(1)}, f32[24,1024]{1,0:T(8,128)S(1)}, bf16[256,1024]{1,0:T(8,128)(2,1)S(1)}) custom-call(s32[1]{0:T(128)} %bitcast.6.at_ref, f32[2,3]{1,0:T(2,128)S(1)} %bitcast.27, bf16[16,2,64,128]{3,2,1,0:T(8,128)(2,1)S(1)} %bitcast.16, bf16[16,112,1024]{2,1,0:T(8,128)(2,1)S(1)} %bitcast.13, ...), custom_call_target="tpu_custom_call" | custom-call | flops 67108864 | bytes 4194304 | tf_op jit(solution)/shard_map/middle_part/pallas_call | solution.py:507
  93.6 8.3 %collective-permute-start.1 = (bf16[416,128]{1,0:T(8,128)(2,1)S(1)}, bf16[416,128]{1,0:T(8,128)(2,1)S(1)}, u32[]{:S(2)}, u32[]{:S(2)}) collective-permute-start(bf16[416,128]{1,0:T(8,128)(2,1)S(1)} %get-tuple-element.28.low_ref), channel_id=1, source_target_pairs={{16,0},{32,16},{48,32},{64,48},{80,64},{96,80},{112,96},{128,112},... | collective-permute-start | bytes 319496 | tf_op jit(solution)/shard_map/ppermute | solution.py:522
  101.9 3.0 %collective-permute-start = (bf16[416,128]{1,0:T(8,128)(2,1)S(1)}, bf16[416,128]{1,0:T(8,128)(2,1)S(1)}, u32[]{:S(2)}, u32[]{:S(2)}) collective-permute-start(bf16[416,128]{1,0:T(8,128)(2,1)S(1)} %get-tuple-element.29.high_ref), channel_id=1, source_target_pairs={{0,16},{16,32},{32,48},{48,64},{64,80},{80,96},{96,112},{112,128},... | collective-permute-start | bytes 319496 | tf_op jit(solution)/shard_map/ppermute | solution.py:521
  105.4 1.2 collective-permute-done.left_ref
  106.6 3.0 %layer_part.1 = bf16[16,144,128]{2,1,0:T(8,128)(2,1)} custom-call(bf16[416,128]{1,0:T(8,128)(2,1)S(1)} %get-tuple-element.28.low_ref, bf16[416,128]{1,0:T(8,128)(2,1)S(1)} %get-tuple-element.29.high_ref, bf16[416,128]{1,0:T(8,128)(2,1)S(1)} %collective-permute-done.left_ref, bf16[416,128]{1,0:T(8,128)(2,1)S(1)} %collective-permute-done.1.right_ref, ...), custom_call_target="tpu_custom_call" | custom-call | flops 67108864 | bytes 4194304 | tf_op jit(solution)/shard_map/layer_part/pallas_call | solution.py:537
  109.6 6.4 %all-to-all-start.2 = ((bf16[16,144,128]{2,1,0:T(8,128)(2,1)}), bf16[16,144,128]{2,1,0:T(8,128)(2,1)S(1)}, u32[]{:S(2)}, u32[]{:S(2)}) async-start(bf16[16,144,128]{2,1,0:T(8,128)(2,1)} %layer_part.1), calls=%async_computation.2 | async-start | bytes 1179648 | tf_op jit(solution)/shard_map/all_to_all | solution.py:445
  116.0 2.0 %copy-done.2 = bf16[1792,1024]{1,0:T(8,128)(2,1)S(1)} copy-done((bf16[1792,1024]{1,0:T(8,128)(2,1)S(1)}, bf16[1792,1024]{1,0:T(8,128)(2,1)}, u32[]{:S(2)}) %copy-start.2) | copy-done | bytes 3670040
  118.6 6.8 %collective-permute-start.2 = (bf16[16,32,1024]{2,1,0:T(8,128)(2,1)S(1)}, bf16[16,32,1024]{2,1,0:T(8,128)(2,1)}, u32[]{:S(2)}, u32[]{:S(2)}) collective-permute-start(bf16[16,32,1024]{2,1,0:T(8,128)(2,1)S(1)} %get-tuple-element.33.mine_ref), channel_id=1, source_target_pairs={{0,16},{16,0},{32,48},{48,32},{64,80},{80,64},{96,112},{112,96},{1... | collective-permute-start | bytes 3145736 | tf_op jit(solution)/shard_map/ppermute | solution.py:553
  125.4 13.1 %all-to-all-done.2.heads_ref.arrived_ref = bf16[16,144,128]{2,1,0:T(8,128)(2,1)S(1)} async-done(((bf16[16,144,128]{2,1,0:T(8,128)(2,1)}), bf16[16,144,128]{2,1,0:T(8,128)(2,1)S(1)}, u32[]{:S(2)}, u32[]{:S(2)}) %all-to-all-start.2) | async-done | bytes 589856 | tf_op jit(solution)/shard_map/all_to_all | solution.py:445
  138.5 1.0 grad_part.1
  139.6 26.9 %all_to_all.25.grads_ref = bf16[32,64,128]{2,1,0:T(8,128)(2,1)} all-to-all(bf16[32,64,128]{2,1,0:T(8,128)(2,1)S(1)} %get-tuple-element.40), channel_id=1, replica_groups=mesh['grid'=32,'head'=16] {'grid'}, dimensions={0} | all-to-all | bytes 1048576 | tf_op jit(solution)/shard_map/all_to_all | solution.py:445
  166.5 6.9 %final_part.1 = bf16[32,32,128]{2,1,0:T(8,128)(2,1)} custom-call(s32[32]{0:T(128)} %bitcast.31, s32[2,30]{1,0:T(2,128)} %slot_ref.5, s32[2]{0:T(128)} %count_ref.5, f32[2,30]{1,0:T(2,128)} %bitcast.24, bf16[1024,1024]{1,0:T(8,128)(2,1)} %get-tuple-element.34.norm_ref, bf16[8,128,128]{2,1,0:T(8,128)(2,1)} %get-tuple-element.24.own_ref.kv_ref, ...), custom_call_target="tpu_custom_call" | custom-call | flops 67108864 | bytes 4194304 | tf_op jit(solution)/shard_map/final_part/pallas_call | solution.py:554
  173.3 4.0 %all-to-all-start.4 = ((bf16[32,32,128]{2,1,0:T(8,128)(2,1)}), bf16[32,32,128]{2,1,0:T(8,128)(2,1)S(1)}, u32[]{:S(2)}, u32[]{:S(2)}) async-start(bf16[32,32,128]{2,1,0:T(8,128)(2,1)} %final_part.1), calls=%async_computation.4 | async-start | bytes 524288 | tf_op jit(solution)/shard_map/all_to_all | solution.py:445
  177.3 2.3 %output_part.1 = bf16[16,1024]{1,0:T(8,128)(2,1)} custom-call(s32[1]{0:T(128)} %bitcast.me_ref, bf16[16,144,128]{2,1,0:T(8,128)(2,1)S(1)} %all-to-all-done.2.heads_ref.arrived_ref, bf16[16,32,1024]{2,1,0:T(8,128)(2,1)S(1)} %get-tuple-element.33.mine_ref, bf16[16,32,1024]{2,1,0:T(8,128)(2,1)} %collective-permute-done.2.other_ref, ...), custom_call_target="tpu_custom_call" | custom-call | flops 67108864 | bytes 4194304 | tf_op jit(solution)/shard_map/output_part/pallas_call | solution.py:573
  179.7 6.7 %all-to-all-done.4.parts_ref = bf16[32,32,128]{2,1,0:T(8,128)(2,1)S(1)} async-done(((bf16[32,32,128]{2,1,0:T(8,128)(2,1)}), bf16[32,32,128]{2,1,0:T(8,128)(2,1)S(1)}, u32[]{:S(2)}, u32[]{:S(2)}) %all-to-all-start.4) | async-done | bytes 262176 | tf_op jit(solution)/shard_map/all_to_all | solution.py:445
  186.3 0.7 sum_part.1
  (44 shorter events, 2.4 us)
Async XLA Ops:
  7.2 82.4 %all-gather.4.cloned.1.call-start = ((), (), s32[]{:S(2)}) async-start(), calls=%async_computation.5 | async-start | bytes 3899392 | tf_op jit(solution)/shard_map/all_gather | solution.py:482
  8.9 16.3 %copy-start.3 = (bf16[256,1024]{1,0:T(8,128)(2,1)S(1)}, bf16[256,1024]{1,0:T(8,128)(2,1)}, u32[]{:S(2)}) copy-start(bf16[256,1024]{1,0:T(8,128)(2,1)} %mesh_ref.3) | copy-start | bytes 1572868
  8.9 16.3 %copy-start.12 = (bf16[1024,64]{0,1:T(8,128)(2,1)S(1)}, bf16[1024,64]{0,1:T(8,128)(2,1)}, u32[]{:S(2)}) copy-start(bf16[1024,64]{0,1:T(8,128)(2,1)} %param.18) | copy-start | bytes 393220
  8.9 33.5 %copy-start.14 = (s32[2,30]{1,0:T(2,128)S(1)}, s32[2,30]{1,0:T(2,128)}, u32[]{:S(2)}) copy-start(s32[2,30]{1,0:T(2,128)} %slot_ref.5) | copy-start | bytes 724
  9.0 33.5 %copy-start.15 = (f32[2,30,1]{1,2,0:T(1,128)S(1)}, f32[2,30,1]{1,2,0:T(1,128)}, u32[]{:S(2)}) copy-start(f32[2,30,1]{1,2,0:T(1,128)} %param.26) | copy-start | bytes 724
  9.0 33.5 %copy-start.17 = (s32[2]{0:T(128)S(1)}, s32[2]{0:T(128)}, u32[]{:S(2)}) copy-start(s32[2]{0:T(128)} %count_ref.5) | copy-start | bytes 28
  14.6 27.9 %copy-start.4 = (bf16[8,128,128]{2,1,0:T(8,128)(2,1)S(1)}, bf16[8,128,128]{2,1,0:T(8,128)(2,1)}, u32[]{:S(2)}) copy-start(bf16[8,128,128]{2,1,0:T(8,128)(2,1)} %get-tuple-element.24.own_ref.kv_ref) | copy-start | bytes 786436
  14.6 27.9 %all-to-all-start = ((bf16[32,128,128]{2,1,0:T(8,128)(2,1)}), bf16[32,128,128]{2,1,0:T(8,128)(2,1)S(1)}, u32[]{:S(2)}, u32[]{:S(2)}) async-start(bf16[32,128,128]{2,1,0:T(8,128)(2,1)} %get-tuple-element.25), calls=%async_computation | async-start | bytes 2097152 | tf_op jit(solution)/shard_map/all_to_all | solution.py:445
  25.8 63.7 %copy-start.10 = (bf16[2,64,128]{2,1,0:T(8,128)(2,1)}, bf16[2,64,128]{2,1,0:T(8,128)(2,1)S(1)}, u32[]{:S(2)}) copy-start(bf16[2,64,128]{2,1,0:T(8,128)(2,1)S(1)} %query_part.1.query_ref) | copy-start | bytes 98308
  42.5 47.1 %copy-start.5 = (bf16[1024,64]{0,1:T(8,128)(2,1)S(1)}, bf16[1024,64]{0,1:T(8,128)(2,1)}, u32[]{:S(2)}) copy-start(bf16[1024,64]{0,1:T(8,128)(2,1)} %param.22) | copy-start | bytes 393220
  42.5 47.1 %copy-start.6 = (bf16[1024,64]{0,1:T(8,128)(2,1)S(1)}, bf16[1024,64]{0,1:T(8,128)(2,1)}, u32[]{:S(2)}) copy-start(bf16[1024,64]{0,1:T(8,128)(2,1)} %param.23) | copy-start | bytes 393220
  42.5 47.1 %copy-start.7 = (bf16[1024,64]{0,1:T(8,128)(2,1)S(1)}, bf16[1024,64]{0,1:T(8,128)(2,1)}, u32[]{:S(2)}) copy-start(bf16[1024,64]{0,1:T(8,128)(2,1)} %param.24) | copy-start | bytes 393220
  42.5 47.1 %copy-start.8 = (bf16[64,1024]{1,0:T(8,128)(2,1)S(1)}, bf16[64,1024]{1,0:T(8,128)(2,1)}, u32[]{:S(2)}) copy-start(bf16[64,1024]{1,0:T(8,128)(2,1)} %wl_ref.3) | copy-start | bytes 393220
  42.5 47.0 %copy-start.18 = (f32[2,3,1]{1,2,0:T(1,128)S(1)}, f32[2,3,1]{1,2,0:T(1,128)}, u32[]{:S(2)}) copy-start(f32[2,3,1]{1,2,0:T(1,128)} %param.27) | copy-start | bytes 76
  50.3 43.3 %copy-start.11 = (bf16[2,64,128]{2,1,0:T(8,128)(2,1)}, bf16[2,64,128]{2,1,0:T(8,128)(2,1)S(1)}, u32[]{:S(2)}) copy-start(bf16[2,64,128]{2,1,0:T(8,128)(2,1)S(1)} %get-tuple-element.27.heads_ref) | copy-start | bytes 98308
  50.3 59.3 %all-to-all-start.1 = ((bf16[32,144,128]{2,1,0:T(8,128)(2,1)}), bf16[32,144,128]{2,1,0:T(8,128)(2,1)}, u32[]{:S(2)}, u32[]{:S(2)}) async-start(bf16[32,144,128]{2,1,0:T(8,128)(2,1)} %get-tuple-element.26), calls=%async_computation.1 | async-start | bytes 2359296 | tf_op jit(solution)/shard_map/all_to_all | solution.py:445
  91.6 15.0 %copy-start.1 = (bf16[1792,1024]{1,0:T(8,128)(2,1)S(1)}, bf16[1792,1024]{1,0:T(8,128)(2,1)}, u32[]{:S(2)}) copy-start(bf16[1792,1024]{1,0:T(8,128)(2,1)} %all-gather.4.cloned.1.call-done) | copy-start | bytes 11010052
  93.6 11.7 %collective-permute-start.1 = (bf16[416,128]{1,0:T(8,128)(2,1)S(1)}, bf16[416,128]{1,0:T(8,128)(2,1)S(1)}, u32[]{:S(2)}, u32[]{:S(2)}) collective-permute-start(bf16[416,128]{1,0:T(8,128)(2,1)S(1)} %get-tuple-element.28.low_ref), channel_id=1, source_target_pairs={{16,0},{32,16},{48,32},{64,48},{80,64},{96,80},{112,96},{128,112},... | collective-permute-start | bytes 319496 | tf_op jit(solution)/shard_map/ppermute | solution.py:522
  101.9 4.7 %collective-permute-start = (bf16[416,128]{1,0:T(8,128)(2,1)S(1)}, bf16[416,128]{1,0:T(8,128)(2,1)S(1)}, u32[]{:S(2)}, u32[]{:S(2)}) collective-permute-start(bf16[416,128]{1,0:T(8,128)(2,1)S(1)} %get-tuple-element.29.high_ref), channel_id=1, source_target_pairs={{0,16},{16,32},{32,48},{48,64},{64,80},{80,96},{96,112},{112,128},... | collective-permute-start | bytes 319496 | tf_op jit(solution)/shard_map/ppermute | solution.py:521
  106.6 9.4 %copy-start.9 = (bf16[64,1024]{1,0:T(8,128)(2,1)S(1)}, bf16[64,1024]{1,0:T(8,128)(2,1)}, u32[]{:S(2)}) copy-start(bf16[64,1024]{1,0:T(8,128)(2,1)} %wo_ref.3) | copy-start | bytes 393220
  109.6 29.0 %all-to-all-start.2 = ((bf16[16,144,128]{2,1,0:T(8,128)(2,1)}), bf16[16,144,128]{2,1,0:T(8,128)(2,1)S(1)}, u32[]{:S(2)}, u32[]{:S(2)}) async-start(bf16[16,144,128]{2,1,0:T(8,128)(2,1)} %layer_part.1), calls=%async_computation.2 | async-start | bytes 1179648 | tf_op jit(solution)/shard_map/all_to_all | solution.py:445
  118.6 58.7 %collective-permute-start.2 = (bf16[16,32,1024]{2,1,0:T(8,128)(2,1)S(1)}, bf16[16,32,1024]{2,1,0:T(8,128)(2,1)}, u32[]{:S(2)}, u32[]{:S(2)}) collective-permute-start(bf16[16,32,1024]{2,1,0:T(8,128)(2,1)S(1)} %get-tuple-element.33.mine_ref), channel_id=1, source_target_pairs={{0,16},{16,0},{32,48},{48,32},{64,80},{80,64},{96,112},{112,96},{1... | collective-permute-start | bytes 3145736 | tf_op jit(solution)/shard_map/ppermute | solution.py:553
  139.6 26.9 %copy-start.13 = (bf16[2,64,128]{2,1,0:T(8,128)(2,1)}, bf16[2,64,128]{2,1,0:T(8,128)(2,1)S(1)}, u32[]{:S(2)}) copy-start(bf16[2,64,128]{2,1,0:T(8,128)(2,1)S(1)} %get-tuple-element.42.grad_ref) | copy-start | bytes 98308
  173.3 13.0 %all-to-all-start.4 = ((bf16[32,32,128]{2,1,0:T(8,128)(2,1)}), bf16[32,32,128]{2,1,0:T(8,128)(2,1)S(1)}, u32[]{:S(2)}, u32[]{:S(2)}) async-start(bf16[32,32,128]{2,1,0:T(8,128)(2,1)} %final_part.1), calls=%async_computation.4 | async-start | bytes 524288 | tf_op jit(solution)/shard_map/all_to_all | solution.py:445
  (3 other events, 4.7 us)
Sparse Core Ops, SparseCore 0:
  10.1 76.9 all-gather.3

commit v11 on v10

--- a/solution.py
+++ b/solution.py
@@ -200,7 +200,6 @@
     parts = heads_ref.shape[0]
     w_out = gathered_ref[:, 0:D, :].reshape(parts * D, C)
     w_layer = jnp.concatenate([wk_ref[...], wv_ref[...], wq_ref[...]], axis=0)
-    half = parts // 2
     height = 2 * B // parts
     tail_ref[height:] = jnp.zeros((8, C), f32)
     messages = (left_ref, right_ref)
@@ -213,13 +212,14 @@
         unit = unit.astype(bf16)
         unit_ref[rows] = unit
         tail_ref[height:, b * B : (b + 1) * B] = jnp.broadcast_to(inverse, (B, 128)).T[0:8]
-        both = dot(unit, w_layer, NT).astype(bf16)
-        for message in messages:
-            message[rows] = both[:, : 2 * D]
-        queries = (both[:, 2 * D :].astype(f32) * score_scale).astype(bf16)
-        cot = gathered_ref[half * b : half * (b + 1), D + D // 2 :, :].reshape(B, C)
-        grads = dot(cot, wl_ref[...], NT).astype(bf16)
-        messages[b][2 * B : 3 * B] = jnp.concatenate([queries, grads], axis=1)
+    both = dot(unit_ref[...], w_layer, NT).astype(bf16)
+    cot = gathered_ref[:, D + D // 2 :, :].reshape(2 * B, C)
+    grads = dot(cot, wl_ref[...], NT).astype(bf16)
+    queries = (both[:, 2 * D :].astype(f32) * score_scale).astype(bf16)
+    for b in range(2):
+        rows = slice(b * B, (b + 1) * B)
+        messages[b][0 : 2 * B] = both[:, : 2 * D]
+        messages[b][2 * B : 3 * B] = jnp.concatenate([queries[rows], grads[rows]], axis=1)
     tail_ref[:height] = enc_ref[pl.ds(pl.multiple_of(at_ref[0] * height, height), height), :]
     row = lax.broadcasted_iota(jnp.int32, (8, 128), 0)
     table = jnp.zeros((8, 128), f32)
@@ -327,7 +327,7 @@
     total = jnp.concatenate(totals, axis=0)
     heads = jnp.concatenate(heads, axis=0)
     share = heads.shape[0] // parts
-    group = 4
+    group = 8
     for start in range(0, parts, group):
         weight = gathered_ref[start : start + group, 0:D, :].reshape(group * D, C)
         pieces = dot(weight, total, NT).astype(bf16)

time: 195 us -> 195 us (level)
  no operation moved by 1% of the time
where the time goes in v11:
time: 195 us; the launch traced here: 194 us
  blocking collectives  62.3 us (32%)
  starting transfers between devices  43.6 us (22%)
  waiting for transfers between devices  37.5 us (19%)
  Pallas kernels  31.4 us (16%)
  between operations  14.3 us (7%)
  local copies, waits for them, and re-layouts  4.75 us (2%)
    all_to_all x4, waiting for transfers between devices, exchange(): return lax.all_to_all(array, axis, split_axis=0, concat_axis=0, tiled=True)  35.7 us
    all_gather x1, blocking collectives, on_device(): all_heads = lax.all_gather(enc_heads, 'head', axis=0, tiled=False)  34.7 us
    all_to_all x1, blocking collectives, exchange(): return lax.all_to_all(array, axis, split_axis=0, concat_axis=0, tiled=True)  27.7 us
    all_to_all x4, starting transfers between devices, exchange(): return lax.all_to_all(array, axis, split_axis=0, concat_axis=0, tiled=True)  25.4 us
    ppermute x1, starting transfers between devices, on_device(): right = lax.ppermute(low, 'grid', backward)  8.2 us
    pallas_call x1, Pallas kernels, on_device(): call(encoder_kernel, (struct((2, D, B), bf16), struct((2, 8, B), f32), st...  7.13 us
    ppermute x1, starting transfers between devices, on_device(): lax.ppermute(half_mine, 'grid', [(i, i ^ 1) for i in range(shards)])  7.05 us
    pallas_call x1, Pallas kernels, on_device(): call(final_kernel, struct((shards, C // shards, 2 * D), bf16), [SMEM] * 4...  6.85 us
  transfers between devices with their start and end apart: 8, of which 5 were waited for; matrix products, arithmetic and copies ran while one was open for 0% of the time, Pallas kernels for 15%

profile of v11, /device:TPU:1, one launch (start us, length us, event | category | flops | bytes accessed | tf_op | source)
XLA Modules:
  0.0 193.9 jit_solution(7710253899766418320)
XLA Ops:
  7.2 1.7 rows_part.1
  9.0 5.6 %grid_part.1 = (bf16[1024,1024]{1,0:T(8,128)(2,1)}, bf16[8,128,128]{2,1,0:T(8,128)(2,1)}, bf16[32,128,128]{2,1,0:T(8,128)(2,1)}) custom-call(s32[32]{0:T(128)} %bitcast.30, bf16[1024,1024]{1,0:T(8,128)(2,1)} %feat_ref.1, bf16[64,1024]{1,0:T(8,128)(2,1)} %bitcast.28, bf16[64,1024]{1,0:T(8,128)(2,1)} %bitcast.29), custom_call_target="tpu_custom_call" | custom-call | flops 268435456 | bytes 6291456 | tf_op jit(solution)/shard_map/grid_part/pallas_call | solution.py:75
  14.6 10.6 %all-to-all-start = ((bf16[32,128,128]{2,1,0:T(8,128)(2,1)}), bf16[32,128,128]{2,1,0:T(8,128)(2,1)S(1)}, u32[]{:S(2)}, u32[]{:S(2)}) async-start(bf16[32,128,128]{2,1,0:T(8,128)(2,1)} %get-tuple-element.25), calls=%async_computation | async-start | bytes 2097152 | tf_op jit(solution)/shard_map/all_to_all | solution.py:445
  25.8 16.6 %all-to-all-done.arrived_ref = bf16[32,128,128]{2,1,0:T(8,128)(2,1)S(1)} async-done(((bf16[32,128,128]{2,1,0:T(8,128)(2,1)}), bf16[32,128,128]{2,1,0:T(8,128)(2,1)S(1)}, u32[]{:S(2)}, u32[]{:S(2)}) %all-to-all-start) | async-done | bytes 1048608 | tf_op jit(solution)/shard_map/all_to_all | solution.py:445
  42.6 7.1 %encoder_part.1 = (bf16[2,64,128]{2,1,0:T(8,128)(2,1)S(1)}, f32[2,8,128]{2,1,0:T(8,128)S(1)}, bf16[32,144,128]{2,1,0:T(8,128)(2,1)}) custom-call(s32[2,30]{1,0:T(2,128)S(1)} %copy-done.14, s32[2]{0:T(128)S(1)} %copy-done.17, f32[2,30]{1,0:T(2,128)S(1)} %bitcast.25, s32[1]{0:T(128)} %bitcast.me_ref, bf16[8,128,128]{2,1,0:T(8,128)(2,1)S(1)} %copy-done.4, ...), custom_call_target="tpu_custom_call" | custom-call | flops 67108864 | bytes 4194304 | tf_op jit(solution)/shard_map/encoder_part/pallas_call | solution.py:494
  50.3 4.7 %all-to-all-start.1 = ((bf16[32,144,128]{2,1,0:T(8,128)(2,1)}), bf16[32,144,128]{2,1,0:T(8,128)(2,1)}, u32[]{:S(2)}, u32[]{:S(2)}) async-start(bf16[32,144,128]{2,1,0:T(8,128)(2,1)} %get-tuple-element.26), calls=%async_computation.1 | async-start | bytes 2359296 | tf_op jit(solution)/shard_map/all_to_all | solution.py:445
  55.0 34.7 %all-gather = bf16[32,64,128]{2,1,0:T(8,128)(2,1)S(1)} all-gather(bf16[2,64,128]{2,1,0:T(8,128)(2,1)S(1)} %get-tuple-element.27.heads_ref), channel_id=2, replica_groups=mesh['grid'=32,'head'=16] {'head'}, dimensions={0}, use_global_device_ids=true | all-gather | bytes 557056 | tf_op jit(solution)/shard_map/all_gather | solution.py:506
  89.7 2.0 %copy-done = bf16[1792,1024]{1,0:T(8,128)(2,1)S(1)} copy-done((bf16[1792,1024]{1,0:T(8,128)(2,1)S(1)}, bf16[1792,1024]{1,0:T(8,128)(2,1)}, u32[]{:S(2)}) %copy-start) | copy-done | bytes 3670040
  91.7 1.9 middle_part.1
  93.6 8.2 %collective-permute-start.1 = (bf16[416,128]{1,0:T(8,128)(2,1)S(1)}, bf16[416,128]{1,0:T(8,128)(2,1)S(1)}, u32[]{:S(2)}, u32[]{:S(2)}) collective-permute-start(bf16[416,128]{1,0:T(8,128)(2,1)S(1)} %get-tuple-element.28.low_ref), channel_id=1, source_target_pairs={{16,0},{32,16},{48,32},{64,48},{80,64},{96,80},{112,96},{128,112},... | collective-permute-start | bytes 319496 | tf_op jit(solution)/shard_map/ppermute | solution.py:522
  101.8 3.0 %collective-permute-start = (bf16[416,128]{1,0:T(8,128)(2,1)S(1)}, bf16[416,128]{1,0:T(8,128)(2,1)S(1)}, u32[]{:S(2)}, u32[]{:S(2)}) collective-permute-start(bf16[416,128]{1,0:T(8,128)(2,1)S(1)} %get-tuple-element.29.high_ref), channel_id=1, source_target_pairs={{0,16},{16,32},{32,48},{48,64},{64,80},{80,96},{96,112},{112,128},... | collective-permute-start | bytes 319496 | tf_op jit(solution)/shard_map/ppermute | solution.py:521
  105.3 1.2 collective-permute-done.left_ref
  106.5 3.0 %layer_part.1 = bf16[16,144,128]{2,1,0:T(8,128)(2,1)} custom-call(bf16[416,128]{1,0:T(8,128)(2,1)S(1)} %get-tuple-element.28.low_ref, bf16[416,128]{1,0:T(8,128)(2,1)S(1)} %get-tuple-element.29.high_ref, bf16[416,128]{1,0:T(8,128)(2,1)S(1)} %collective-permute-done.left_ref, bf16[416,128]{1,0:T(8,128)(2,1)S(1)} %collective-permute-done.1.right_ref, ...), custom_call_target="tpu_custom_call" | custom-call | flops 67108864 | bytes 4194304 | tf_op jit(solution)/shard_map/layer_part/pallas_call | solution.py:537
  109.5 6.1 %all-to-all-start.2 = ((bf16[16,144,128]{2,1,0:T(8,128)(2,1)}), bf16[16,144,128]{2,1,0:T(8,128)(2,1)S(1)}, u32[]{:S(2)}, u32[]{:S(2)}) async-start(bf16[16,144,128]{2,1,0:T(8,128)(2,1)} %layer_part.1), calls=%async_computation.2 | async-start | bytes 1179648 | tf_op jit(solution)/shard_map/all_to_all | solution.py:445
  115.7 2.0 %copy-done.2 = bf16[1792,1024]{1,0:T(8,128)(2,1)S(1)} copy-done((bf16[1792,1024]{1,0:T(8,128)(2,1)S(1)}, bf16[1792,1024]{1,0:T(8,128)(2,1)}, u32[]{:S(2)}) %copy-start.2) | copy-done | bytes 3670040
  118.3 7.1 %collective-permute-start.2 = (bf16[16,32,1024]{2,1,0:T(8,128)(2,1)S(1)}, bf16[16,32,1024]{2,1,0:T(8,128)(2,1)}, u32[]{:S(2)}, u32[]{:S(2)}) collective-permute-start(bf16[16,32,1024]{2,1,0:T(8,128)(2,1)S(1)} %get-tuple-element.33.mine_ref), channel_id=1, source_target_pairs={{0,16},{16,0},{32,48},{48,32},{64,80},{80,64},{96,112},{112,96},{1... | collective-permute-start | bytes 3145736 | tf_op jit(solution)/shard_map/ppermute | solution.py:553
  125.3 12.4 %all-to-all-done.2.heads_ref.arrived_ref = bf16[16,144,128]{2,1,0:T(8,128)(2,1)S(1)} async-done(((bf16[16,144,128]{2,1,0:T(8,128)(2,1)}), bf16[16,144,128]{2,1,0:T(8,128)(2,1)S(1)}, u32[]{:S(2)}, u32[]{:S(2)}) %all-to-all-start.2) | async-done | bytes 589856 | tf_op jit(solution)/shard_map/all_to_all | solution.py:445
  137.8 1.0 grad_part.1
  138.8 27.7 %all_to_all.25.grads_ref = bf16[32,64,128]{2,1,0:T(8,128)(2,1)} all-to-all(bf16[32,64,128]{2,1,0:T(8,128)(2,1)S(1)} %get-tuple-element.40), channel_id=1, replica_groups=mesh['grid'=32,'head'=16] {'grid'}, dimensions={0} | all-to-all | bytes 1048576 | tf_op jit(solution)/shard_map/all_to_all | solution.py:445
  166.4 6.8 %final_part.1 = bf16[32,32,128]{2,1,0:T(8,128)(2,1)} custom-call(s32[32]{0:T(128)} %bitcast.31, s32[2,30]{1,0:T(2,128)} %slot_ref.5, s32[2]{0:T(128)} %count_ref.5, f32[2,30]{1,0:T(2,128)} %bitcast.24, bf16[1024,1024]{1,0:T(8,128)(2,1)} %get-tuple-element.34.norm_ref, bf16[8,128,128]{2,1,0:T(8,128)(2,1)} %get-tuple-element.24.own_ref.kv_ref, ...), custom_call_target="tpu_custom_call" | custom-call | flops 67108864 | bytes 4194304 | tf_op jit(solution)/shard_map/final_part/pallas_call | solution.py:554
  173.3 4.0 %all-to-all-start.4 = ((bf16[32,32,128]{2,1,0:T(8,128)(2,1)}), bf16[32,32,128]{2,1,0:T(8,128)(2,1)S(1)}, u32[]{:S(2)}, u32[]{:S(2)}) async-start(bf16[32,32,128]{2,1,0:T(8,128)(2,1)} %final_part.1), calls=%async_computation.4 | async-start | bytes 524288 | tf_op jit(solution)/shard_map/all_to_all | solution.py:445
  177.3 2.3 %output_part.1 = bf16[16,1024]{1,0:T(8,128)(2,1)} custom-call(s32[1]{0:T(128)} %bitcast.me_ref, bf16[16,144,128]{2,1,0:T(8,128)(2,1)S(1)} %all-to-all-done.2.heads_ref.arrived_ref, bf16[16,32,1024]{2,1,0:T(8,128)(2,1)S(1)} %get-tuple-element.33.mine_ref, bf16[16,32,1024]{2,1,0:T(8,128)(2,1)} %collective-permute-done.2.other_ref, ...), custom_call_target="tpu_custom_call" | custom-call | flops 67108864 | bytes 4194304 | tf_op jit(solution)/shard_map/output_part/pallas_call | solution.py:573
  179.6 6.7 %all-to-all-done.4.parts_ref = bf16[32,32,128]{2,1,0:T(8,128)(2,1)S(1)} async-done(((bf16[32,32,128]{2,1,0:T(8,128)(2,1)}), bf16[32,32,128]{2,1,0:T(8,128)(2,1)S(1)}, u32[]{:S(2)}, u32[]{:S(2)}) %all-to-all-start.4) | async-done | bytes 262176 | tf_op jit(solution)/shard_map/all_to_all | solution.py:445
  186.3 0.7 sum_part.1
  (44 shorter events, 2.4 us)
Async XLA Ops:
  7.2 82.5 %all-gather.4.cloned.1.call-start = ((), (), s32[]{:S(2)}) async-start(), calls=%async_computation.5 | async-start | bytes 3899392 | tf_op jit(solution)/shard_map/all_gather | solution.py:482
  8.9 16.3 %copy-start.3 = (bf16[256,1024]{1,0:T(8,128)(2,1)S(1)}, bf16[256,1024]{1,0:T(8,128)(2,1)}, u32[]{:S(2)}) copy-start(bf16[256,1024]{1,0:T(8,128)(2,1)} %mesh_ref.3) | copy-start | bytes 1572868
  8.9 16.3 %copy-start.12 = (bf16[1024,64]{0,1:T(8,128)(2,1)S(1)}, bf16[1024,64]{0,1:T(8,128)(2,1)}, u32[]{:S(2)}) copy-start(bf16[1024,64]{0,1:T(8,128)(2,1)} %param.18) | copy-start | bytes 393220
  8.9 33.5 %copy-start.14 = (s32[2,30]{1,0:T(2,128)S(1)}, s32[2,30]{1,0:T(2,128)}, u32[]{:S(2)}) copy-start(s32[2,30]{1,0:T(2,128)} %slot_ref.5) | copy-start | bytes 724
  9.0 33.5 %copy-start.15 = (f32[2,30,1]{1,2,0:T(1,128)S(1)}, f32[2,30,1]{1,2,0:T(1,128)}, u32[]{:S(2)}) copy-start(f32[2,30,1]{1,2,0:T(1,128)} %param.26) | copy-start | bytes 724
  9.0 33.5 %copy-start.17 = (s32[2]{0:T(128)S(1)}, s32[2]{0:T(128)}, u32[]{:S(2)}) copy-start(s32[2]{0:T(128)} %count_ref.5) | copy-start | bytes 28
  14.6 27.9 %copy-start.4 = (bf16[8,128,128]{2,1,0:T(8,128)(2,1)S(1)}, bf16[8,128,128]{2,1,0:T(8,128)(2,1)}, u32[]{:S(2)}) copy-start(bf16[8,128,128]{2,1,0:T(8,128)(2,1)} %get-tuple-element.24.own_ref.kv_ref) | copy-start | bytes 786436
  14.6 27.9 %all-to-all-start = ((bf16[32,128,128]{2,1,0:T(8,128)(2,1)}), bf16[32,128,128]{2,1,0:T(8,128)(2,1)S(1)}, u32[]{:S(2)}, u32[]{:S(2)}) async-start(bf16[32,128,128]{2,1,0:T(8,128)(2,1)} %get-tuple-element.25), calls=%async_computation | async-start | bytes 2097152 | tf_op jit(solution)/shard_map/all_to_all | solution.py:445
  25.8 63.8 %copy-start.10 = (bf16[2,64,128]{2,1,0:T(8,128)(2,1)}, bf16[2,64,128]{2,1,0:T(8,128)(2,1)S(1)}, u32[]{:S(2)}) copy-start(bf16[2,64,128]{2,1,0:T(8,128)(2,1)S(1)} %query_part.1.query_ref) | copy-start | bytes 98308
  42.5 47.1 %copy-start.5 = (bf16[1024,64]{0,1:T(8,128)(2,1)S(1)}, bf16[1024,64]{0,1:T(8,128)(2,1)}, u32[]{:S(2)}) copy-start(bf16[1024,64]{0,1:T(8,128)(2,1)} %param.22) | copy-start | bytes 393220
  42.5 47.1 %copy-start.6 = (bf16[1024,64]{0,1:T(8,128)(2,1)S(1)}, bf16[1024,64]{0,1:T(8,128)(2,1)}, u32[]{:S(2)}) copy-start(bf16[1024,64]{0,1:T(8,128)(2,1)} %param.23) | copy-start | bytes 393220
  42.5 47.1 %copy-start.7 = (bf16[1024,64]{0,1:T(8,128)(2,1)S(1)}, bf16[1024,64]{0,1:T(8,128)(2,1)}, u32[]{:S(2)}) copy-start(bf16[1024,64]{0,1:T(8,128)(2,1)} %param.24) | copy-start | bytes 393220
  42.5 47.1 %copy-start.8 = (bf16[64,1024]{1,0:T(8,128)(2,1)S(1)}, bf16[64,1024]{1,0:T(8,128)(2,1)}, u32[]{:S(2)}) copy-start(bf16[64,1024]{1,0:T(8,128)(2,1)} %wl_ref.3) | copy-start | bytes 393220
  42.5 47.1 %copy-start.18 = (f32[2,3,1]{1,2,0:T(1,128)S(1)}, f32[2,3,1]{1,2,0:T(1,128)}, u32[]{:S(2)}) copy-start(f32[2,3,1]{1,2,0:T(1,128)} %param.27) | copy-start | bytes 76
  50.3 43.3 %copy-start.11 = (bf16[2,64,128]{2,1,0:T(8,128)(2,1)}, bf16[2,64,128]{2,1,0:T(8,128)(2,1)S(1)}, u32[]{:S(2)}) copy-start(bf16[2,64,128]{2,1,0:T(8,128)(2,1)S(1)} %get-tuple-element.27.heads_ref) | copy-start | bytes 98308
  50.3 59.2 %all-to-all-start.1 = ((bf16[32,144,128]{2,1,0:T(8,128)(2,1)}), bf16[32,144,128]{2,1,0:T(8,128)(2,1)}, u32[]{:S(2)}, u32[]{:S(2)}) async-start(bf16[32,144,128]{2,1,0:T(8,128)(2,1)} %get-tuple-element.26), calls=%async_computation.1 | async-start | bytes 2359296 | tf_op jit(solution)/shard_map/all_to_all | solution.py:445
  91.7 14.8 %copy-start.1 = (bf16[1792,1024]{1,0:T(8,128)(2,1)S(1)}, bf16[1792,1024]{1,0:T(8,128)(2,1)}, u32[]{:S(2)}) copy-start(bf16[1792,1024]{1,0:T(8,128)(2,1)} %all-gather.4.cloned.1.call-done) | copy-start | bytes 11010052
  93.6 11.6 %collective-permute-start.1 = (bf16[416,128]{1,0:T(8,128)(2,1)S(1)}, bf16[416,128]{1,0:T(8,128)(2,1)S(1)}, u32[]{:S(2)}, u32[]{:S(2)}) collective-permute-start(bf16[416,128]{1,0:T(8,128)(2,1)S(1)} %get-tuple-element.28.low_ref), channel_id=1, source_target_pairs={{16,0},{32,16},{48,32},{64,48},{80,64},{96,80},{112,96},{128,112},... | collective-permute-start | bytes 319496 | tf_op jit(solution)/shard_map/ppermute | solution.py:522
  101.8 4.7 %collective-permute-start = (bf16[416,128]{1,0:T(8,128)(2,1)S(1)}, bf16[416,128]{1,0:T(8,128)(2,1)S(1)}, u32[]{:S(2)}, u32[]{:S(2)}) collective-permute-start(bf16[416,128]{1,0:T(8,128)(2,1)S(1)} %get-tuple-element.29.high_ref), channel_id=1, source_target_pairs={{0,16},{16,32},{32,48},{48,64},{64,80},{80,96},{96,112},{112,128},... | collective-permute-start | bytes 319496 | tf_op jit(solution)/shard_map/ppermute | solution.py:521
  106.5 9.1 %copy-start.9 = (bf16[64,1024]{1,0:T(8,128)(2,1)S(1)}, bf16[64,1024]{1,0:T(8,128)(2,1)}, u32[]{:S(2)}) copy-start(bf16[64,1024]{1,0:T(8,128)(2,1)} %wo_ref.3) | copy-start | bytes 393220
  109.5 28.3 %all-to-all-start.2 = ((bf16[16,144,128]{2,1,0:T(8,128)(2,1)}), bf16[16,144,128]{2,1,0:T(8,128)(2,1)S(1)}, u32[]{:S(2)}, u32[]{:S(2)}) async-start(bf16[16,144,128]{2,1,0:T(8,128)(2,1)} %layer_part.1), calls=%async_computation.2 | async-start | bytes 1179648 | tf_op jit(solution)/shard_map/all_to_all | solution.py:445
  118.3 59.0 %collective-permute-start.2 = (bf16[16,32,1024]{2,1,0:T(8,128)(2,1)S(1)}, bf16[16,32,1024]{2,1,0:T(8,128)(2,1)}, u32[]{:S(2)}, u32[]{:S(2)}) collective-permute-start(bf16[16,32,1024]{2,1,0:T(8,128)(2,1)S(1)} %get-tuple-element.33.mine_ref), channel_id=1, source_target_pairs={{0,16},{16,0},{32,48},{48,32},{64,80},{80,64},{96,112},{112,96},{1... | collective-permute-start | bytes 3145736 | tf_op jit(solution)/shard_map/ppermute | solution.py:553
  138.8 27.7 %copy-start.13 = (bf16[2,64,128]{2,1,0:T(8,128)(2,1)}, bf16[2,64,128]{2,1,0:T(8,128)(2,1)S(1)}, u32[]{:S(2)}) copy-start(bf16[2,64,128]{2,1,0:T(8,128)(2,1)S(1)} %get-tuple-element.42.grad_ref) | copy-start | bytes 98308
  173.3 13.0 %all-to-all-start.4 = ((bf16[32,32,128]{2,1,0:T(8,128)(2,1)}), bf16[32,32,128]{2,1,0:T(8,128)(2,1)S(1)}, u32[]{:S(2)}, u32[]{:S(2)}) async-start(bf16[32,32,128]{2,1,0:T(8,128)(2,1)} %final_part.1), calls=%async_computation.4 | async-start | bytes 524288 | tf_op jit(solution)/shard_map/all_to_all | solution.py:445
  (3 other events, 4.7 us)
Sparse Core Ops, SparseCore 0:
  10.1 76.9 all-gather.3
